TPU v7x, 256 devices: a whole 4x4x8 slice. The times are simulated.
256 devices in a mesh: gx: 4 (over y), gy: 8 (over x, core), gz: 8 (over z).
Axes of the slice: x: 4, y: 4, z: 8, core: 2. Of those that a mesh axis runs over, the one named last changes fastest.
Arguments:
- x_field: float32 [64, 16, 64, 1024], P(None, 'gx', 'gy', 'gz'), may hold values from -1.2 to 1.2
- right_side: float32 [64, 16, 64, 1024], P(None, 'gx', 'gy', 'gz'), may hold values from -8 to 8, as said below
- diag_shift: float32 [16, 64, 1024], P('gx', 'gy', 'gz'), may hold values from 0.2 to 3
- velocity: float32 [3, 16, 64, 1024], P(None, 'gx', 'gy', 'gz'), may hold values from -0.6 to 0.6
- earlier_blocks: float32 [8, 64, 16, 64, 1024], P(None, None, 'gx', 'gy', 'gz'), may hold values from -1 to 1, as said below
- sep_cells: int32 [8, 1024], P('gz', ('gx', 'gy')), may hold values from 0 to 4095
- low_inv: bfloat16 [8, 1024, 1024], P('gz', ('gx', 'gy')), may hold values from -0.1875 to 0.1875
- low_off: bfloat16 [8, 1024, 1024], P('gz', ('gx', 'gy')), may hold values from -0.15625 to 0.15625
- up_off: bfloat16 [8, 1024, 1024], P('gz', ('gx', 'gy')), may hold values from -0.15625 to 0.15625
Outputs:
- residual: float32 [64, 16, 64, 1024], P(None, 'gx', 'gy', 'gz')
- new_block: float32 [64, 16, 64, 1024], P(None, 'gx', 'gy', 'gz')
- projection: float32 [512, 64], replicated
- chol_scaled: float32 [64, 64], replicated
Inputs may be any that keep to these rules, and one draw needn't show every extreme that they name: `sep_cells`: every entry indexes a cell of its device's brick; cells may repeat. `right_side`: entries of order one. `earlier_blocks`: entries of order one over the square root of 1048576.
All inputs are finite; a program needn't handle non-finite values.
Results may differ from a plain program's by a relative error of at most 0.015.
Values may be sent and summed in bfloat16 or wider, within the bound.
A program may use at most 128 MiB of HBM per device.

v0:
```python
import jax
import jax.numpy as jnp
from jax import lax
from jax.sharding import PartitionSpec as P


def extended(block, sides, width):
    for axis, dim in sides:
        count = lax.axis_size(axis)
        forward = [(i, i + 1) for i in range(count - 1)]
        backward = [(target, source) for source, target in forward]
        low = lax.ppermute(
            lax.slice_in_dim(block, block.shape[dim] - width, None, axis=dim), axis, forward
        )
        high = lax.ppermute(lax.slice_in_dim(block, 0, width, axis=dim), axis, backward)
        block = jnp.concatenate([low, block, high], axis=dim)
    return block


def passed_along(block, axis, distance):
    devices = range(lax.axis_size(axis))
    route = [(i - distance, i) for i in devices if i - distance in devices]
    return lax.ppermute(block, axis, route)


def operate(field, diag_shift, velocity):
    padded = extended(field.astype(jnp.bfloat16), (("gx", 1), ("gy", 2), ("gz", 3)), 1).astype(
        field.dtype
    )
    result = (6.0 + diag_shift) * field
    result = (
        result
        - (1.0 + velocity[0]) * padded[:, :-2, 1:-1, 1:-1]
        - (1.0 - velocity[0]) * padded[:, 2:, 1:-1, 1:-1]
    )
    result = (
        result
        - (1.0 + velocity[1]) * padded[:, 1:-1, :-2, 1:-1]
        - (1.0 - velocity[1]) * padded[:, 1:-1, 2:, 1:-1]
    )
    result = (
        result
        - (1.0 + velocity[2]) * padded[:, 1:-1, 1:-1, :-2]
        - (1.0 - velocity[2]) * padded[:, 1:-1, 1:-1, 2:]
    )
    return result


def apply_rows(matrix, piece):
    return jnp.dot(matrix, piece, preferred_element_type=jnp.float32)


def sweep(start_rows, matrix, direction):
    state = start_rows
    position = lax.axis_index("gz")
    count = lax.axis_size("gz")
    for turn_index in range(1, count):
        outgoing = state.astype(jnp.bfloat16)
        incoming = passed_along(outgoing, "gz", direction)
        product = apply_rows(matrix, lax.all_gather(incoming, ("gx", "gy"), axis=0, tiled=True))
        candidate = start_rows - product
        target = turn_index if direction == 1 else count - 1 - turn_index
        state = jnp.where(position == target, candidate, state)
    return state


def body(
    x_field, right_side, diag_shift, velocity, earlier_blocks, sep_cells, low_inv, low_off, up_off
):
    residual = right_side - operate(x_field, diag_shift, velocity)
    rhs_column_count = residual.shape[0]
    mesh_cell_count = residual.shape[1] * residual.shape[2] * residual.shape[3]
    res_flat = residual.reshape(rhs_column_count, mesh_cell_count)
    positions = sep_cells[0]
    seps = res_flat[:, positions].T.astype(jnp.bfloat16)
    start_rows = apply_rows(low_inv[0], lax.all_gather(seps, ("gx", "gy"), axis=0, tiled=True))
    forward = sweep(start_rows, low_off[0], 1)
    solved = sweep(forward, up_off[0], -1)
    separator_update = res_flat / (6.0 + diag_shift).reshape(1, mesh_cell_count)
    separator_update = separator_update.at[:, positions].add(solved.T)
    basis_matrix = earlier_blocks.reshape(
        earlier_blocks.shape[0] * rhs_column_count, mesh_cell_count
    )
    contract_basis = (((1,), (1,)), ((), ()))
    partial_projection = lax.dot_general(
        basis_matrix, separator_update, contract_basis, precision=lax.Precision.HIGHEST
    )
    projection = lax.psum(partial_projection, ("gx", "gy", "gz"))
    orthogonalize = separator_update - jnp.dot(
        projection.T, basis_matrix, precision=lax.Precision.HIGHEST
    )
    part_gram = lax.dot_general(
        orthogonalize, orthogonalize, contract_basis, precision=lax.Precision.HIGHEST
    )
    gram = lax.psum(part_gram, ("gx", "gy", "gz"))
    factor = jnp.linalg.cholesky(gram)
    total_cells = mesh_cell_count * lax.axis_size("gx") * lax.axis_size("gy") * lax.axis_size("gz")
    norm_scale = jnp.sqrt(jnp.float32(total_cells))
    solved_block = lax.linalg.triangular_solve(factor, orthogonalize, left_side=True, lower=True)
    new_block = (solved_block * norm_scale).reshape(residual.shape)
    return (residual, new_block, projection, factor / norm_scale)


def solution(mesh):
    return jax.shard_map(
        body,
        mesh=mesh,
        in_specs=(
            P(None, "gx", "gy", "gz"),
            P(None, "gx", "gy", "gz"),
            P("gx", "gy", "gz"),
            P(None, "gx", "gy", "gz"),
            P(None, None, "gx", "gy", "gz"),
            P("gz", ("gx", "gy")),
            P("gz", ("gx", "gy"), None),
            P("gz", ("gx", "gy"), None),
            P("gz", ("gx", "gy"), None),
        ),
        out_specs=(P(None, "gx", "gy", "gz"), P(None, "gx", "gy", "gz"), P(), P()),
        check_vma=False,
    )
```

profile of v0, /device:TPU:1, one launch (start us, length us, event | category | flops | bytes accessed | tf_op | source)
XLA Modules:
  0.0 862.4 jit_solution(11785849363314304821)
XLA Ops:
  18.9 5.1 collective-permute-start.2
  46.2 24.3 %all_gather.45 = bf16[1024,64]{1,0:T(8,128)(2,1)S(1)} all-gather(bf16[32,64]{1,0:T(8,128)(2,1)S(1)} %gather_fusion), channel_id=1, replica_groups=mesh['gx'=4,'gy'=8,'gz'=8] {'gx','gy'}, dimensions={0}, use_global_device_ids=true | all-gather | bytes 135168 | tf_op jit(solution)/shard_map/all_gather | solution.py:76
  75.4 23.9 %all_gather.46 = bf16[1024,64]{1,0:T(8,128)(2,1)S(1)} all-gather(bf16[32,64]{1,0:T(8,128)(2,1)S(1)} %collective-permute-done.6), channel_id=1, replica_groups=mesh['gx'=4,'gy'=8,'gz'=8] {'gx','gy'}, dimensions={0}, use_global_device_ids=true | all-gather | bytes 135168 | tf_op jit(solution)/shard_map/all_gather | solution.py:60
  104.1 24.5 %all_gather.47 = bf16[1024,64]{1,0:T(8,128)(2,1)S(1)} all-gather(bf16[32,64]{1,0:T(8,128)(2,1)S(1)} %collective-permute-done.7), channel_id=1, replica_groups=mesh['gx'=4,'gy'=8,'gz'=8] {'gx','gy'}, dimensions={0}, use_global_device_ids=true | all-gather | bytes 135168 | tf_op jit(solution)/shard_map/all_gather | solution.py:60
  133.6 24.0 %all_gather.48 = bf16[1024,64]{1,0:T(8,128)(2,1)S(1)} all-gather(bf16[32,64]{1,0:T(8,128)(2,1)S(1)} %collective-permute-done.8), channel_id=1, replica_groups=mesh['gx'=4,'gy'=8,'gz'=8] {'gx','gy'}, dimensions={0}, use_global_device_ids=true | all-gather | bytes 135168 | tf_op jit(solution)/shard_map/all_gather | solution.py:60
  157.8 5.1 collective-permute-start.9
  163.7 24.5 %all_gather.49 = bf16[1024,64]{1,0:T(8,128)(2,1)S(1)} all-gather(bf16[32,64]{1,0:T(8,128)(2,1)S(1)} %collective-permute-done.9), channel_id=1, replica_groups=mesh['gx'=4,'gy'=8,'gz'=8] {'gx','gy'}, dimensions={0}, use_global_device_ids=true | all-gather | bytes 135168 | tf_op jit(solution)/shard_map/all_gather | solution.py:60
  188.4 5.1 collective-permute-start.10
  194.3 23.9 %all_gather.50 = bf16[1024,64]{1,0:T(8,128)(2,1)S(1)} all-gather(bf16[32,64]{1,0:T(8,128)(2,1)S(1)} %collective-permute-done.10), channel_id=1, replica_groups=mesh['gx'=4,'gy'=8,'gz'=8] {'gx','gy'}, dimensions={0}, use_global_device_ids=true | all-gather | bytes 135168 | tf_op jit(solution)/shard_map/all_gather | solution.py:60
  218.3 5.1 collective-permute-start.11
  224.2 24.5 %all_gather.51 = bf16[1024,64]{1,0:T(8,128)(2,1)S(1)} all-gather(bf16[32,64]{1,0:T(8,128)(2,1)S(1)} %collective-permute-done.11), channel_id=1, replica_groups=mesh['gx'=4,'gy'=8,'gz'=8] {'gx','gy'}, dimensions={0}, use_global_device_ids=true | all-gather | bytes 135168 | tf_op jit(solution)/shard_map/all_gather | solution.py:60
  248.9 5.1 collective-permute-start.12
  254.8 23.9 %all_gather.52 = bf16[1024,64]{1,0:T(8,128)(2,1)S(1)} all-gather(bf16[32,64]{1,0:T(8,128)(2,1)S(1)} %collective-permute-done.12), channel_id=1, replica_groups=mesh['gx'=4,'gy'=8,'gz'=8] {'gx','gy'}, dimensions={0}, use_global_device_ids=true | all-gather | bytes 135168 | tf_op jit(solution)/shard_map/all_gather | solution.py:60
  280.1 4.9 collective-permute-done.13
  285.0 24.5 %all_gather.53 = bf16[1024,64]{1,0:T(8,128)(2,1)S(1)} all-gather(bf16[32,64]{1,0:T(8,128)(2,1)S(1)} %collective-permute-done.13), channel_id=1, replica_groups=mesh['gx'=4,'gy'=8,'gz'=8] {'gx','gy'}, dimensions={0}, use_global_device_ids=true | all-gather | bytes 135168 | tf_op jit(solution)/shard_map/all_gather | solution.py:60
  311.0 4.9 collective-permute-done.14
  315.8 23.9 %all_gather.54 = bf16[1024,64]{1,0:T(8,128)(2,1)S(1)} all-gather(bf16[32,64]{1,0:T(8,128)(2,1)S(1)} %collective-permute-done.14), channel_id=1, replica_groups=mesh['gx'=4,'gy'=8,'gz'=8] {'gx','gy'}, dimensions={0}, use_global_device_ids=true | all-gather | bytes 135168 | tf_op jit(solution)/shard_map/all_gather | solution.py:60
  341.2 4.9 collective-permute-done.15
  346.1 24.7 %all_gather.55 = bf16[1024,64]{1,0:T(8,128)(2,1)S(1)} all-gather(bf16[32,64]{1,0:T(8,128)(2,1)S(1)} %collective-permute-done.15), channel_id=1, replica_groups=mesh['gx'=4,'gy'=8,'gz'=8] {'gx','gy'}, dimensions={0}, use_global_device_ids=true | all-gather | bytes 135168 | tf_op jit(solution)/shard_map/all_gather | solution.py:60
  372.2 4.9 collective-permute-done.16
  377.1 23.9 %all_gather.56 = bf16[1024,64]{1,0:T(8,128)(2,1)S(1)} all-gather(bf16[32,64]{1,0:T(8,128)(2,1)S(1)} %collective-permute-done.16), channel_id=1, replica_groups=mesh['gx'=4,'gy'=8,'gz'=8] {'gx','gy'}, dimensions={0}, use_global_device_ids=true | all-gather | bytes 135168 | tf_op jit(solution)/shard_map/all_gather | solution.py:60
  402.5 4.6 collective-permute-done.17
  407.1 24.5 %all_gather.57 = bf16[1024,64]{1,0:T(8,128)(2,1)S(1)} all-gather(bf16[32,64]{1,0:T(8,128)(2,1)S(1)} %collective-permute-done.17), channel_id=1, replica_groups=mesh['gx'=4,'gy'=8,'gz'=8] {'gx','gy'}, dimensions={0}, use_global_device_ids=true | all-gather | bytes 135168 | tf_op jit(solution)/shard_map/all_gather | solution.py:60
  433.0 9.5 %reshape.58 = f32[512,4096]{1,0:T(8,128)} reshape(f32[8,64,4,8,128]{4,3,2,1,0:T(8,128)} %param.13) | data formatting | bytes 16777216 | tf_op jit(solution)/shard_map/reshape | solution.py:81
  442.5 23.0 %all_gather.58 = bf16[1024,64]{1,0:T(8,128)(2,1)S(1)} all-gather(bf16[32,64]{1,0:T(8,128)(2,1)S(1)} %collective-permute-done.18), channel_id=1, replica_groups=mesh['gx'=4,'gy'=8,'gz'=8] {'gx','gy'}, dimensions={0}, use_global_device_ids=true | all-gather | bytes 135168 | tf_op jit(solution)/shard_map/all_gather | solution.py:60
  472.2 24.5 %all_gather.59 = bf16[1024,64]{1,0:T(8,128)(2,1)S(1)} all-gather(bf16[32,64]{1,0:T(8,128)(2,1)S(1)} %collective-permute-done.19), channel_id=1, replica_groups=mesh['gx'=4,'gy'=8,'gz'=8] {'gx','gy'}, dimensions={0}, use_global_device_ids=true | all-gather | bytes 135168 | tf_op jit(solution)/shard_map/all_gather | solution.py:60
  498.6 11.3 %convolution_bitcast_fusion = f32[512,64]{0,1:T(8,128)} fusion(f32[64,4096]{0,1:T(8,128)S(1)} %scatter_fusion, f32[512,4096]{1,0:T(8,128)} %reshape.58), kind=kOutput, calls=%fused_computation.6 | convolution fusion | flops 1610612736 | bytes 9568256 | tf_op jit(solution)/shard_map/dot_general | solution.py:85
  513.1 240.2 %all-reduce.2.cloned.1.call-done = f32[512,64]{0,1:T(8,128)} async-done(((f32[512,64]{0,1:T(8,128)}), f32[512,64]{0,1:T(8,128)}) %all-reduce.2.cloned.1.call-update) | async-done | bytes 131088 | tf_op jit(solution)/shard_map/psum | solution.py:88
  753.3 8.8 %convolution_subtract_fusion = f32[64,4096]{1,0:T(8,128)S(1)} fusion(f32[64,4096]{1,0:T(8,128)} %copy.25, f32[512,64]{0,1:T(8,128)} %all-reduce.2.cloned.1.call-done, f32[512,4096]{1,0:T(8,128)} %reshape.58), kind=kOutput, calls=%fused_computation.3 | convolution fusion | flops 1610874880 | bytes 10616832 | tf_op jit(solution)/shard_map/dot_general | solution.py:89
  763.1 76.3 %psum.15 = f32[64,64]{0,1:T(8,128)S(1)} all-reduce(f32[64,64]{0,1:T(8,128)S(1)} %fusion.83), channel_id=1, replica_groups=mesh['gx'=4,'gy'=8,'gz'=8] {'gx','gy','gz'}, use_global_device_ids=true, to_apply=%region_2.3 | all-reduce | flops 4096 | bytes 32768 | tf_op jit(solution)/shard_map/psum | solution.py:95
  839.5 5.8 cholesky.16
  847.3 4.9 custom-call.6
  (92 shorter events, 78.6 us)
Async XLA Ops:
  7.2 92.1 %copy-start = (bf16[1,32,1024]{2,1,0:T(8,128)(2,1)S(1)}, bf16[1,32,1024]{2,1,0:T(8,128)(2,1)}, u32[]{:S(2)}) copy-start(bf16[1,32,1024]{2,1,0:T(8,128)(2,1)} %param.16) | copy-start | bytes 196612
  7.2 746.1 %all-reduce.2.cloned.1.call-start = ((), (), s32[]{:S(2)}) async-start(), calls=%async_computation | async-start | bytes 262144 | tf_op jit(solution)/shard_map/psum | solution.py:88
  9.1 6.8 collective-permute-start
  13.1 5.7 collective-permute-start.1
  18.9 7.7 collective-permute-start.2
  24.0 5.9 collective-permute-start.3
  31.7 6.9 collective-permute-start.5
  33.0 5.1 collective-permute-start.4
  38.6 4.7 copy-start.2
  40.0 3.3 copy-start.4
  43.3 27.2 %copy-start.6 = (bf16[1,32,1024]{2,1,0:T(8,128)(2,1)S(1)}, bf16[1,32,1024]{2,1,0:T(8,128)(2,1)}, u32[]{:S(2)}) copy-start(bf16[1,32,1024]{2,1,0:T(8,128)(2,1)} %param.15) | copy-start | bytes 196612
  45.0 264.5 %copy-start.3 = (bf16[1,32,1024]{2,1,0:T(8,128)(2,1)S(1)}, bf16[1,32,1024]{2,1,0:T(8,128)(2,1)}, u32[]{:S(2)}) copy-start(bf16[1,32,1024]{2,1,0:T(8,128)(2,1)} %param.17) | copy-start | bytes 196612
  45.6 355.6 %copy-start.1 = (f32[64,4,8,128]{0,3,2,1:T(8,128)}, f32[64,4,8,128]{0,3,2,1:T(8,128)S(1)}, u32[]{:S(2)}) copy-start(f32[64,4,8,128]{0,3,2,1:T(8,128)S(1)} %copy.24) | copy-start | bytes 3145732
  70.7 4.7 collective-permute-start.6
  99.4 4.7 collective-permute-start.7
  128.8 4.8 collective-permute-start.8
  157.8 5.9 collective-permute-start.9
  188.4 5.9 collective-permute-start.10
  218.3 5.9 collective-permute-start.11
  248.9 5.9 collective-permute-start.12
  278.8 6.2 collective-permute-start.13
  309.7 6.2 collective-permute-start.14
  339.9 6.2 collective-permute-start.15
  370.9 6.2 collective-permute-start.16
  401.2 5.9 collective-permute-start.17
  431.7 10.8 %collective-permute-start.18 = (bf16[32,64]{1,0:T(8,128)(2,1)S(1)}, bf16[32,64]{1,0:T(8,128)(2,1)S(1)}, u32[]{:S(2)}, u32[]{:S(2)}) collective-permute-start(bf16[32,64]{1,0:T(8,128)(2,1)S(1)} %get-tuple-element.51), channel_id=1, source_target_pairs={{1,0},{2,1},{3,2},{4,3},{5,4},{6,5},{7,6},{9,8},{10,9},{11,10},{12... | collective-permute-start | bytes 12296 | tf_op jit(solution)/shard_map/ppermute | solution.py:23
  465.7 6.5 collective-permute-start.19
  762.1 92.3 %copy-start.5 = (f32[512,64]{0,1:T(8,128)S(1)}, f32[512,64]{0,1:T(8,128)}, u32[]{:S(2)}) copy-start(f32[512,64]{0,1:T(8,128)} %all-reduce.2.cloned.1.call-done) | copy-start | bytes 393220
Sparse Core Ops, SparseCore 0:
  510.1 243.1 all-reduce.1
where the time goes:
time: 872 us; the launch traced here: 862 us
  blocking collectives  439 us (50%)
  waiting for transfers between devices  280 us (32%)
  starting transfers between devices  59.2 us (7%)
  matrix products  24.6 us (3%)
  other arithmetic  23.7 us (3%)
  local copies, waits for them, and re-layouts  21 us (2%)
  between operations  15.1 us (2%)
    all_gather x14, blocking collectives, sweep(): lax.all_gather(incoming, ('gx', 'gy'), axis=0, tiled=True)  338 us
    psum x1, waiting for transfers between devices, body(): projection = lax.psum(partial_projection, ('gx', 'gy', 'gz'))  240 us
    psum x1, blocking collectives, body(): gram = lax.psum(part_gram, ('gx', 'gy', 'gz'))  76.3 us
    ppermute x14, starting transfers between devices, passed_along(): return lax.ppermute(block, axis, route)  41.4 us
    ppermute x14, waiting for transfers between devices, passed_along(): return lax.ppermute(block, axis, route)  32.7 us
    all_gather x1, blocking collectives, body(): lax.all_gather(seps, ('gx', 'gy'), axis=0, tiled=True)  24.3 us
  transfers between devices with their start and end apart: 21, of which 17 were waited for; matrix products, arithmetic and copies ran while one was open for 2% of the time, Pallas kernels for 0%

commit v1 on v0

v1 whole, which is shorter than its diff:
```python
import functools
import math

import jax
import jax.numpy as jnp
from jax import lax
from jax.experimental import pallas as pl
from jax.experimental.pallas import tpu as pltpu
from jax.sharding import PartitionSpec as P

bf16, f32 = jnp.bfloat16, jnp.float32
RHS, CX, CY, CZ, SEP = 64, 4, 8, 128, 32
SLABS = CX * CY
PAIRS = SLABS // 2
ROWS = RHS * SLABS
LANES = 128


def nt(a, b):
    return lax.dot_general(a, b, (((1,), (1,)), ((), ())), preferred_element_type=f32)


def nn(a, b):
    return jnp.dot(a, b, preferred_element_type=f32)


def split(v):
    hi = v.astype(bf16)
    return hi, (v - hi.astype(f32)).astype(bf16)


def iota(shape, dim):
    return lax.broadcasted_iota(jnp.int32, shape, dim)


def flag(cond):
    return jnp.where(cond, jnp.float32(1.0), jnp.float32(0.0))


def cholesky_and_inverse(gram):
    n = RHS
    lane8 = iota((8, LANES), 1)
    row8 = iota((8, LANES), 0)
    blocks, low, inverse = [], [], []
    for k in range(n // 8):
        eye = (lane8 - n == row8 + 8 * k).astype(f32)
        blocks.append(jnp.where(lane8 < n, gram[8 * k : 8 * k + 8, :], eye))
        low.append(jnp.zeros((8, LANES), f32))
        inverse.append(jnp.zeros((8, LANES), f32))
    for j in range(n):
        kj, r = divmod(j, 8)
        row = jnp.broadcast_to(blocks[kj][r : r + 1, :], (8, LANES))
        pivot = jnp.broadcast_to(row[:, j : j + 1], (8, LANES))
        root = lax.rsqrt(pivot)
        scaled = row * root
        inverse[kj] = jnp.where(row8 == r, scaled, inverse[kj])
        for k in range(kj, n // 8):
            col = jnp.broadcast_to(blocks[k][:, j : j + 1], (8, LANES)) * root
            if k == kj:
                col = jnp.where(row8 >= r, col, 0.0)
                below = jnp.where(row8 > r, col, 0.0)
            else:
                below = col
            low[k] = jnp.where(lane8 == j, col, low[k])
            blocks[k] = blocks[k] - below * scaled
    return jnp.concatenate(low, axis=0), jnp.concatenate(inverse, axis=0)


def kernel(
    na, nb, nz, early,
    x_h, r_h, d_h, v_h, e_h, c_h, li_h, lo_h, up_h,
    res_o, new_o, proj_o, chol_o,
    x_v, r_v, d_v, v_v, e_v, c_v, m_v,
    xsb, hx, hy, hz, zsend, oh, gath,
    w0, wh, wl, vh, vl, pacc, vsh, vsl,
    sep_loc, sep_hop, sep_all, base, state, stateb, fw_in, bw_in, ret,
    psend, pin1, psum1, pin2, pin3, pin4, pin5, pt_hl,
    orth, g_loc, gin1, gin2, gin3, gin4, chol_v,
    loc_sem, send_sem, recv_sem,
):
    a, b, z = lax.axis_index("gx"), lax.axis_index("gy"), lax.axis_index("gz")
    size = {"gx": na, "gy": nb, "gz": nz}
    pos = {"gx": a, "gy": b, "gz": z}
    group = RHS // na
    wide = SEP * na
    depth = nb * wide
    count = [0]
    sent = []

    def place(axis, index):
        at = dict(pos)
        at[axis] = index
        return (at["gx"], at["gy"], at["gz"])

    def send(src, dst, where, keep=True):
        n = count[0]
        count[0] += 1
        copy = pltpu.make_async_remote_copy(
            src_ref=src, dst_ref=dst, send_sem=send_sem.at[n], recv_sem=recv_sem.at[n],
            device_id=where, device_id_type=pl.DeviceIdType.MESH,
        )
        copy.start()
        if keep:
            sent.append(copy)
        return copy

    def share(axis, src_of, dst):
        n = size[axis]
        copies = []
        for d in range(1, n):
            to = lax.rem(pos[axis] + d, n)
            copies.append(send(src_of(to), dst, place(axis, to)))
        return copies

    def arrive(copies):
        for copy in copies:
            copy.wait_recv()

    barrier = pltpu.get_barrier_semaphore()
    partners = 0
    for axis in ("gx", "gy", "gz"):
        for d in range(1, size[axis]):
            pl.semaphore_signal(
                barrier, inc=1, device_id=place(axis, lax.rem(pos[axis] + d, size[axis])),
                device_id_type=pl.DeviceIdType.MESH,
            )
            partners += 1

    def fetch(n, src, dst):
        copy = pltpu.make_async_copy(src, dst, loc_sem.at[n])
        copy.start()
        return copy

    get_x = fetch(0, x_h, x_v)
    get_m = [fetch(1 + i, h, m_v.at[i]) for i, h in enumerate((li_h, lo_h, up_h))]
    get_c = fetch(4, c_h, c_v)
    get_d = fetch(5, d_h, d_v)
    get_v = fetch(6, v_h, v_v)
    get_r = fetch(7, r_h, r_v)
    get_e = fetch(8, e_h, e_v)

    def slab(ref, s, n=RHS):
        return ref[pl.ds(s, n, stride=SLABS), :]

    get_x.wait()
    for s in range(SLABS):
        xsb[s // CY, (s % CY) * RHS : (s % CY + 1) * RHS, :] = slab(x_v, s).astype(bf16)
    q32, l32 = iota((32, LANES), 0), iota((32, LANES), 1)
    edge = jnp.zeros((32, LANES), f32)
    for p in range(PAIRS):
        pick = ((q32 == p) & (l32 == CZ - 1)) | ((q32 == 16 + p) & (l32 == 0))
        rows = xsb[p // 4, (p % 4) * 128 : (p % 4 + 1) * 128, :]
        edge = edge + nt(pick.astype(bf16), rows)
    zsend[...] = edge.astype(bf16)

    pl.semaphore_wait(barrier, partners)

    def ring(axis, step):
        n = size[axis]
        return place(axis, lax.rem(pos[axis] + step + n, n))

    halo = [
        send(zsend.at[pl.ds(0, 16)], hz.at[0], ring("gz", 1)),
        send(zsend.at[pl.ds(16, 16)], hz.at[1], ring("gz", -1)),
        send(xsb.at[CX - 1], hx.at[0], ring("gx", 1)),
        send(xsb.at[0], hx.at[1], ring("gx", -1)),
        send(xsb.at[:, pl.ds((CY - 1) * RHS, RHS)], hy.at[0], ring("gy", 1)),
        send(xsb.at[:, pl.ds(0, RHS)], hy.at[1], ring("gy", -1)),
    ]

    mine = pl.ds(pl.multiple_of(a * SEP, SEP), SEP)
    lane_group = iota((SEP, LANES), 1) // SEP
    per_tile = LANES // SEP
    gather = []
    for i in range(3):
        get_m[i].wait()
        tiles = [
            m_v[i, :, t * LANES : (t + 1) * LANES].astype(f32) for t in range(depth // LANES)
        ]
        for t in range(depth // LANES):
            out = jnp.zeros((SEP, LANES), f32)
            for g in range(per_tile):
                chunk = t * per_tile + g
                old = (chunk % na) * nb + chunk // na
                piece = tiles[old // per_tile]
                shift = ((g - old % per_tile) * SEP) % LANES
                if shift:
                    piece = pltpu.roll(piece, shift, 1)
                out = jnp.where(lane_group == g, piece, out)
            gath[i, mine, t * LANES : (t + 1) * LANES] = out.astype(bf16)
        gather.append(
            share("gx", lambda to, i=i: gath.at[i, mine], gath.at[i, mine])
        )

    get_c.wait()
    cells = jnp.broadcast_to(c_v[...], (SEP, SEP)).astype(f32)
    square = iota((SEP, SEP), 0) == iota((SEP, SEP), 1)
    column = jnp.sum(jnp.where(square, cells, 0.0), axis=1, keepdims=True)
    column = jnp.broadcast_to(column, (SEP, 2 * CZ))
    z256 = iota((SEP, 2 * CZ), 1).astype(f32)
    for p in range(PAIRS):
        oh[p] = jnp.zeros((wide, 2 * CZ), bf16)
        oh[p, mine, :] = jnp.where(column == z256 + float(p * 2 * CZ), 1.0, 0.0).astype(bf16)
    vsh[...] = jnp.zeros(vsh.shape, bf16)
    vsl[...] = jnp.zeros(vsl.shape, bf16)

    get_d.wait()
    get_v.wait()
    get_r.wait()
    arrive(halo)

    before_z = hz[0].astype(f32) * flag(z > 0)
    after_z = hz[1].astype(f32) * flag(z < nz - 1)
    ends = jnp.concatenate(
        [before_z, after_z, jnp.zeros((LANES - 32, LANES), f32)], axis=0
    ).T.astype(bf16)
    keep = {
        (0, -1): flag(a > 0), (0, 1): flag(a < na - 1),
        (1, -1): flag(b > 0), (1, 1): flag(b < nb - 1),
    }
    q128, l128 = iota((LANES, LANES), 0), iota((LANES, LANES), 1)
    lane64 = iota((RHS, LANES), 1)
    seps = jnp.zeros((RHS, wide), f32)
    for p in range(PAIRS):
        spread = ((q128 == p) & (l128 == 0)) | ((q128 == 16 + p) & (l128 == CZ - 1))
        z_ends = nn(ends, spread.astype(bf16))
        halves = []
        for h in range(2):
            s = 2 * p + h
            cx, cy = divmod(s, CY)
            x = slab(x_v, s)
            diag = 6.0 + d_v[s : s + 1, :]

            def beside(k, step):
                if k == 0 and not 0 <= cx + step < CX:
                    rows = hx[(step + 1) // 2, cy * RHS : (cy + 1) * RHS, :]
                    return rows.astype(f32), keep[0, step]
                if k == 1 and not 0 <= cy + step < CY:
                    return hy[(step + 1) // 2, cx].astype(f32), keep[1, step]
                return slab(x_v, s + step * (CY if k == 0 else 1)), None

            total = diag * x
            for k in range(2):
                for step in (-1, 1):
                    coef = 1.0 - step * v_v[k * SLABS + s : k * SLABS + s + 1, :]
                    value, mask = beside(k, step)
                    if mask is not None:
                        coef = coef * mask
                    total = total - coef * value
            end = z_ends[h * RHS : (h + 1) * RHS, :]
            v2 = v_v[2 * SLABS + s : 2 * SLABS + s + 1, :]
            before = jnp.where(lane64 == 0, end, pltpu.roll(x, 1, 1))
            after = jnp.where(lane64 == CZ - 1, end, pltpu.roll(x, CZ - 1, 1))
            total = total - (1.0 + v2) * before - (1.0 - v2) * after
            res = slab(r_v, s) - total
            r_v[pl.ds(s, RHS, stride=SLABS), :] = res
            halves.append(res.astype(bf16))
            w = res / diag
            hi, lo = split(w)
            at = slice(h * CZ, (h + 1) * CZ)
            w0[p, :, at] = w
            wh[p, :, at] = hi
            wl[p, :, at] = lo
        seps = seps + nt(jnp.concatenate(halves, axis=1), oh[p])
    put_res = pltpu.make_async_copy(r_v, res_o, loc_sem.at[9])
    put_res.start()

    sep_loc[...] = seps.astype(bf16).reshape(na, group, wide)
    hop = share("gx", lambda to: sep_loc.at[to], sep_hop.at[a])
    sep_hop[a] = sep_loc[a]
    arrive(hop)
    mixed = sep_hop[0].astype(f32)
    for i in range(1, na):
        mixed = mixed + sep_hop[i].astype(f32)
    sep_all[b] = mixed.astype(bf16)
    hop = share("gy", lambda to: sep_all.at[b], sep_all.at[b])
    arrive(hop)

    def row_of(ref):
        return jnp.concatenate([ref[i] for i in range(nb)], axis=1)

    arrive(gather[0])
    base[...] = nt(row_of(sep_all), gath[0])

    def earlier_work():
        get_e.wait()
        pacc[...] = jnp.zeros(pacc.shape, f32)

        def step(p, carry):
            s_h, s_l = carry
            rows = e_v.shape[0] // SLABS
            both = jnp.concatenate(
                [slab(e_v, 2 * p, rows), slab(e_v, 2 * p + 1, rows)], axis=1
            )
            hi, lo = split(both)
            vh[p] = hi
            vl[p] = lo
            own = oh[p, mine, :]
            first = nt(jnp.concatenate([wh[p], wl[p], own], axis=0), hi)
            second = nt(jnp.concatenate([wh[p], own], axis=0), lo)
            pacc[...] += first[:RHS] + first[RHS : 2 * RHS] + second[:RHS]
            return s_h + first[2 * RHS :], s_l + second[RHS:]

        zero = jnp.zeros((SEP, e_v.shape[0] // SLABS), f32)
        s_h, s_l = lax.fori_loop(0, PAIRS, step, (zero, zero))
        vsh[mine, :] = s_h.astype(bf16)
        vsl[mine, :] = s_l.astype(bf16)

    def sweep_push(dst, step):
        out = []
        for d in range(nb):
            to = lax.rem(b + d, nb)
            out.append(send(stateb.at[0 if step > 0 else 1], dst.at[b], (a, to, z + step), False))
        return out

    def sweep_copies(first, dst, step):
        return [
            pltpu.make_async_remote_copy(
                src_ref=stateb.at[0 if step > 0 else 1], dst_ref=dst.at[b],
                send_sem=send_sem.at[first + d], recv_sem=recv_sem.at[first + d],
                device_id=(a, lax.rem(b + d, nb), z + step),
                device_id_type=pl.DeviceIdType.MESH,
            )
            for d in range(nb)
        ]

    pl.when(z >= early)(earlier_work)

    fw_first = count[0]
    arrive(gather[1])

    @pl.when(z == 0)
    def _():
        state[...] = base[...]

    @pl.when(z > 0)
    def _():
        arrive(sweep_copies(fw_first, fw_in, 1))
        state[...] = base[...] - nt(row_of(fw_in), gath[1])

    @pl.when(z < nz - 1)
    def _():
        stateb[0] = state[...].astype(bf16)
        sweep_push(fw_in, 1)

    count[0] = fw_first + nb
    pl.when(z < early)(earlier_work)

    bw_first = count[0]
    arrive(gather[2])

    @pl.when(z < nz - 1)
    def _():
        arrive(sweep_copies(bw_first, bw_in, -1))
        state[...] = state[...] - nt(row_of(bw_in), gath[2])

    @pl.when(z > 0)
    def _():
        stateb[1] = state[...].astype(bf16)
        sweep_push(bw_in, -1)

    count[0] = bw_first + nb

    hop = share("gx", lambda to: state, ret.at[a])
    ret[a] = state[...]
    arrive(hop)
    sol_h, sol_l = split(ret[...].reshape(RHS, wide))
    corr = nn(jnp.concatenate([sol_h, sol_l], axis=0), vsh[...])
    corr = pacc[...] + corr[:RHS] + corr[RHS:] + nn(sol_h, vsl[...])
    cols = corr.shape[1]

    psend[...] = corr.reshape(na, group, cols)
    hop = share("gx", lambda to: psend.at[to], pin1.at[a])
    pin1[a] = psend[a]

    sol_hl = jnp.concatenate([sol_h, sol_l], axis=1)

    def add_sol(p, carry):
        w0[p] = w0[p] + nn(sol_hl, jnp.concatenate([oh[p], oh[p]], axis=0))
        return carry

    lax.fori_loop(0, PAIRS, add_sol, 0, unroll=2)

    def total_of(ref, n):
        out = ref[0]
        for i in range(1, n):
            out = out + ref[i]
        return out

    arrive(hop)
    part = total_of(pin1, na)
    ph = group // 8
    pw = nb // ph
    width = cols // pw
    for i in range(nb):
        r, c = divmod(i, pw)
        psum1[i] = part[r * 8 : r * 8 + 8, c * width : (c + 1) * width]
    hop = share("gy", lambda to: psum1.at[to], pin2.at[b])
    pin2[b] = psum1[b]
    arrive(hop)
    pin3[z] = total_of(pin2, nb)
    hop = share("gz", lambda to: pin3.at[z], pin3.at[z])
    arrive(hop)
    pin4[b] = total_of(pin3, nz)
    hop = share("gy", lambda to: pin4.at[b], pin4.at[b])
    arrive(hop)
    pin5[a] = jnp.concatenate(
        [jnp.concatenate([pin4[r * pw + c] for c in range(pw)], axis=1) for r in range(ph)], axis=0
    )
    hop = share("gx", lambda to: pin5.at[a], pin5.at[a])
    arrive(hop)
    full = pin5[...].reshape(RHS, cols)
    hi, lo = split(full)
    pt_hl[:RHS] = hi
    pt_hl[RHS:] = lo

    def project(p, gram):
        main = nn(pt_hl[...], vh[p])
        o = w0[p] - (main[:RHS] + main[RHS:] + nn(pt_hl[:RHS], vl[p]))
        hi, lo = split(o)
        both = jnp.concatenate([hi, lo], axis=0)
        orth[p] = both
        return gram + nt(both, both)

    gram = lax.fori_loop(0, PAIRS, project, jnp.zeros((2 * RHS, 2 * RHS), f32), unroll=2)
    gram = gram[:RHS] + gram[RHS:]
    gram = gram + pltpu.roll(gram, RHS, 1)
    piece = RHS // nz
    g_loc[...] = gram.reshape(nz, piece, LANES)
    hop = share("gz", lambda to: g_loc.at[to], gin1.at[z])
    gin1[z] = g_loc[z]

    proj_o[...] = jnp.concatenate([full, jnp.zeros((LANES - RHS, cols), f32)], axis=0).T[:, :RHS]

    arrive(hop)
    gin2[b] = total_of(gin1, nz)
    arrive(share("gy", lambda to: gin2.at[b], gin2.at[b]))
    gin3[a] = total_of(gin2, nb)
    arrive(share("gx", lambda to: gin3.at[a], gin3.at[a]))
    gin4[z] = total_of(gin3, na)
    arrive(share("gz", lambda to: gin4.at[z], gin4.at[z]))

    low, inverse = cholesky_and_inverse(gin4[...].reshape(RHS, LANES))
    scale = math.sqrt(na * nb * nz * CX * CY * CZ)
    chol_o[...] = low[:, :RHS] * (1.0 / scale)
    inverse = inverse * scale
    hi, lo = split(inverse)
    lhs = jnp.where(lane64 < RHS, pltpu.roll(hi.astype(f32), RHS, 1), lo.astype(f32)).astype(bf16)
    lhs = jnp.concatenate([lhs, lhs], axis=1)
    put_res.wait()
    for p in range(PAIRS):
        hi, lo = orth[p, :RHS], orth[p, RHS:]
        out = nn(lhs, jnp.concatenate([hi, hi, lo, lo], axis=0))
        for h in range(2):
            x_v[pl.ds(2 * p + h, RHS, stride=SLABS), :] = out[:, h * CZ : (h + 1) * CZ]
    put_new = pltpu.make_async_copy(x_v, new_o, loc_sem.at[10])
    put_new.start()

    for copy in sent:
        copy.wait_send()

    @pl.when(z < nz - 1)
    def _():
        for copy in sweep_copies(fw_first, fw_in, 1):
            copy.wait_send()

    @pl.when(z > 0)
    def _():
        for copy in sweep_copies(bw_first, bw_in, -1):
            copy.wait_send()

    put_new.wait()


def body(
    x_field, right_side, diag_shift, velocity, earlier_blocks, sep_cells, low_inv, low_off, up_off
):
    na, nb, nz = (lax.axis_size(n) for n in ("gx", "gy", "gz"))
    group, wide = RHS // na, SEP * na
    depth = nb * wide
    vecs = earlier_blocks.shape[0] * earlier_blocks.shape[1]
    pw = nb // (group // 8)
    width = vecs // pw
    piece = RHS // nz
    vmem = pltpu.VMEM
    scratch = [
        vmem((ROWS, CZ), f32),
        vmem((ROWS, CZ), f32),
        vmem((SLABS, CZ), f32),
        vmem((3 * SLABS, CZ), f32),
        vmem((vecs * SLABS, CZ), f32),
        vmem((1, SEP), jnp.int32),
        vmem((3, SEP, depth), bf16),
        vmem((CX, CY * RHS, CZ), bf16),
        vmem((2, CY * RHS, CZ), bf16),
        vmem((2, CX, RHS, CZ), bf16),
        vmem((2, 16, LANES), bf16),
        vmem((32, LANES), bf16),
        vmem((PAIRS, wide, 2 * CZ), bf16),
        vmem((3, wide, depth), bf16),
        vmem((PAIRS, RHS, 2 * CZ), f32),
        vmem((PAIRS, RHS, 2 * CZ), bf16),
        vmem((PAIRS, RHS, 2 * CZ), bf16),
        vmem((PAIRS, vecs, 2 * CZ), bf16),
        vmem((PAIRS, vecs, 2 * CZ), bf16),
        vmem((RHS, vecs), f32),
        vmem((wide, vecs), bf16),
        vmem((wide, vecs), bf16),
        vmem((na, group, wide), bf16),
        vmem((na, group, wide), bf16),
        vmem((nb, group, wide), bf16),
        vmem((group, wide), f32),
        vmem((group, wide), f32),
        vmem((2, group, wide), bf16),
        vmem((nb, group, wide), bf16),
        vmem((nb, group, wide), bf16),
        vmem((na, group, wide), f32),
        vmem((na, group, vecs), f32),
        vmem((na, group, vecs), f32),
        vmem((nb, 8, width), f32),
        vmem((nb, 8, width), f32),
        vmem((nz, 8, width), f32),
        vmem((nb, 8, width), f32),
        vmem((na, group, vecs), f32),
        vmem((2 * RHS, vecs), bf16),
        vmem((PAIRS, 2 * RHS, 2 * CZ), bf16),
        vmem((nz, piece, LANES), f32),
        vmem((nz, piece, LANES), f32),
        vmem((nb, piece, LANES), f32),
        vmem((na, piece, LANES), f32),
        vmem((nz, piece, LANES), f32),
        vmem((8, LANES), f32),
        pltpu.SemaphoreType.DMA((11,)),
        pltpu.SemaphoreType.DMA((128,)),
        pltpu.SemaphoreType.DMA((128,)),
    ]
    flat = lambda v: v.reshape(-1, CZ)
    anywhere = pl.BlockSpec(memory_space=pl.ANY)
    in_vmem = pl.BlockSpec(memory_space=pltpu.VMEM)
    res, new, projection, factor = pl.pallas_call(
        functools.partial(kernel, na, nb, nz, (nz * 5) // 8),
        out_shape=(
            jax.ShapeDtypeStruct((ROWS, CZ), f32),
            jax.ShapeDtypeStruct((ROWS, CZ), f32),
            jax.ShapeDtypeStruct((vecs, RHS), f32),
            jax.ShapeDtypeStruct((RHS, RHS), f32),
        ),
        in_specs=[anywhere] * 9,
        out_specs=(anywhere, anywhere, in_vmem, in_vmem),
        scratch_shapes=scratch,
        compiler_params=pltpu.CompilerParams(
            collective_id=0, has_side_effects=True, vmem_limit_bytes=50 * 2**20
        ),
        cost_estimate=pl.CostEstimate(
            flops=2 * 10**9, bytes_accessed=13 * 2**20, transcendentals=0
        ),
        name="step",
    )(
        flat(x_field), flat(right_side), flat(diag_shift), flat(velocity), flat(earlier_blocks),
        sep_cells, low_inv[0], low_off[0], up_off[0],
    )
    shape = right_side.shape
    return (res.reshape(shape), new.reshape(shape), projection, factor)


def solution(mesh):
    return jax.shard_map(
        body,
        mesh=mesh,
        in_specs=(
            P(None, "gx", "gy", "gz"),
            P(None, "gx", "gy", "gz"),
            P("gx", "gy", "gz"),
            P(None, "gx", "gy", "gz"),
            P(None, None, "gx", "gy", "gz"),
            P("gz", ("gx", "gy")),
            P("gz", ("gx", "gy"), None),
            P("gz", ("gx", "gy"), None),
            P("gz", ("gx", "gy"), None),
        ),
        out_specs=(P(None, "gx", "gy", "gz"), P(None, "gx", "gy", "gz"), P(), P()),
        check_vma=False,
    )
```

time: 872 us -> 150 us (0.17); the launches traced: 862 us -> 149 us
  blocking collectives: 439 us -> 0 us
  waiting for transfers between devices: 280 us -> 0 us
  Pallas kernels: 0 us -> 140 us
  starting transfers between devices: 59.2 us -> 0 us
  matrix products: 24.6 us -> 0 us
  other arithmetic: 23.7 us -> 0 us
  between operations: 15.1 us -> 0.66 us
  local copies, waits for them, and re-layouts: 21 us -> 9.23 us
    all_gather x15 -> x0, blocking collectives: 362 us -> none  [the longest x14 338 us: sweep(): lax.all_gather(incoming, ('gx', 'gy'), axis=0, tiled=True)]
    psum x1 -> x0, waiting for transfers between devices: 240 us -> none  [body(): projection = lax.psum(partial_projection, ('gx', 'gy', 'gz'))]
    pallas_call x0 -> x1, Pallas kernels: none -> 140 us  [body(): pl.pallas_call(functools.partial(kernel, na, nb, nz, nz * 5 // 8), out_sh...]
    psum x1 -> x0, blocking collectives: 76.3 us -> none  [body(): gram = lax.psum(part_gram, ('gx', 'gy', 'gz'))]
    ppermute x20 -> x0, starting transfers between devices: 59.2 us -> none  [the longest x14 41.4 us: passed_along(): return lax.ppermute(block, axis, route)]
    ppermute x20 -> x0, waiting for transfers between devices: 39.8 us -> none  [the longest x14 32.7 us: passed_along(): return lax.ppermute(block, axis, route)]
    dot_general x18 -> x0, matrix products: 23.6 us -> none  [the longest x1 11.3 us: body(): lax.dot_general(basis_matrix, separator_update, contract_basis, precision...]
    another operation x4 -> x0, other arithmetic: 11.4 us -> none  [the longest x3 6.52 us: body(): factor = jnp.linalg.cholesky(gram)]
  transfers between devices with their start and end apart: 21 -> 0, of which waited for: 17 -> 0; matrix products, arithmetic and copies ran while one was open for 2% -> 0% of each run, Pallas kernels for 0% -> 0%
where the time goes in v1:
time: 150 us; the launch traced here: 149 us
  Pallas kernels  140 us (93%)
  local copies, waits for them, and re-layouts  9.23 us (6%)
    pallas_call x1, Pallas kernels, body(): pl.pallas_call(functools.partial(kernel, na, nb, nz, nz * 5 // 8), out_sh...  140 us
    unnamed x18, local copies, waits for them, and re-layouts  9.23 us

profile of v1, /device:TPU:1, one launch (start us, length us, event | category | flops | bytes accessed | tf_op | source)
XLA Modules:
  0.0 149.4 jit_solution(7137764348719711290)
XLA Ops:
  0.6 0.0 copy-start
  0.6 1.2 copy-done
  1.9 0.0 copy-start.1
  1.9 0.8 copy-done.1
  2.7 0.0 copy-start.2
  2.7 0.8 copy-done.2
  3.5 0.0 copy-start.3
  3.5 0.8 copy-done.3
  4.4 0.0 copy-start.4
  4.4 0.8 copy-done.4
  5.2 0.0 copy-start.5
  5.2 0.7 copy-done.5
  5.9 0.0 copy-start.6
  5.9 0.7 copy-done.6
  6.6 139.6 %step.1 = (f32[2048,128]{1,0:T(8,128)S(1)}, f32[2048,128]{1,0:T(8,128)S(1)}, f32[512,64]{1,0:T(8,128)S(1)}, f32[64,64]{1,0:T(8,128)S(1)}) custom-call(f32[2048,128]{1,0:T(8,128)S(1)} %bitcast.12, f32[2048,128]{1,0:T(8,128)} %bitcast.19, f32[32,128]{1,0:T(8,128)S(1)} %bitcast.17, f32[96,128]{1,0:T(8,128)S(1)} %bitcast.16, f32[16384,128]{1,0:T(8,128)} %bitcast.18, ...), custom_call_target="tpu_custom_call" | custom-call | flops 2000000000 | bytes 13631488 | tf_op jit(solution)/shard_map/step/pallas_call | solution.py:540
  146.1 0.8 copy.13
  146.9 1.0 copy.17
  147.9 1.0 copy.18
  148.8 0.6 copy.19
Async XLA Ops:
  0.6 1.2 copy-start
  1.9 0.8 copy-start.1
  2.7 0.8 copy-start.2
  3.5 0.8 copy-start.3
  4.4 0.8 copy-start.4
  5.2 0.7 copy-start.5
  5.9 0.7 copy-start.6

commit v2 on v1

v2 whole, which is shorter than its diff:
```python
import functools
import math

import jax
import jax.numpy as jnp
from jax import lax
from jax.experimental import pallas as pl
from jax.experimental.pallas import tpu as pltpu
from jax.sharding import PartitionSpec as P

bf16, f32 = jnp.bfloat16, jnp.float32
RHS, CX, CY, CZ, SEP = 64, 4, 8, 128, 32
SLABS = CX * CY
PAIRS = SLABS // 2
ROWS = RHS * SLABS
LANES = 128


def nt(a, b):
    return lax.dot_general(a, b, (((1,), (1,)), ((), ())), preferred_element_type=f32)


def nn(a, b):
    return jnp.dot(a, b, preferred_element_type=f32)


def split(v):
    hi = v.astype(bf16)
    return hi, (v - hi.astype(f32)).astype(bf16)


def iota(shape, dim):
    return lax.broadcasted_iota(jnp.int32, shape, dim)


def flag(cond):
    return jnp.where(cond, jnp.float32(1.0), jnp.float32(0.0))


def cholesky_rows(gram, out):
    n = RHS
    lane8, row8 = iota((8, LANES), 1), iota((8, LANES), 0)
    blocks = []
    for k in range(n // 8):
        eye = (lane8 - n == row8 + 8 * k).astype(f32)
        blocks.append(jnp.where(lane8 < n, gram[8 * k : 8 * k + 8, :], eye))

    def sublane(v, r):
        return jnp.broadcast_to(v[r : r + 1, :], (8, LANES))

    def panel(turn, blocks):
        first = blocks[0]
        columns = [jnp.broadcast_to(first[:, j : j + 1], (8, LANES)) for j in range(8)]
        entry = {(i, j): sublane(columns[j], i) for j in range(8) for i in range(j, 8)}
        rows = [sublane(first, i) for i in range(8)]
        for j in range(8):
            root = lax.rsqrt(entry[j, j])
            rows[j] = rows[j] * root
            for i in range(j + 1, 8):
                entry[i, j] = entry[i, j] * root
            for i in range(j + 1, 8):
                rows[i] = rows[i] - entry[i, j] * rows[j]
                for k in range(j + 1, i + 1):
                    entry[i, k] = entry[i, k] - entry[i, j] * entry[k, j]
        done = rows[0]
        for i in range(1, 8):
            done = jnp.where(row8 == i, rows[i], done)
        hi = done.astype(bf16).astype(f32)
        mid = (done - hi).astype(bf16).astype(f32)
        low = done - hi - mid
        left = jnp.concatenate([hi, hi, mid, hi, low, mid], axis=0).astype(bf16)
        right = jnp.concatenate([hi, mid, hi, low, hi, mid], axis=0).astype(bf16)
        change = lax.dot_general(
            left, right, (((0,), (0,)), ((), ())), preferred_element_type=f32
        )
        out[pl.ds(pl.multiple_of(turn * 8, 8), 8), :] = pltpu.roll(done, turn * 8, 1)
        rest = [
            pltpu.roll(blocks[k] - change[8 * k : 8 * k + 8], LANES - 8, 1)
            for k in range(1, n // 8)
        ]
        return tuple(rest + [jnp.zeros((8, LANES), f32)])

    lax.fori_loop(0, n // 8, panel, tuple(blocks))


def kernel(
    na, nb, nz, early,
    x_h, r_h, d_h, v_h, e_h, c_h, li_h, lo_h, up_h,
    res_o, orth_o, proj_o, gram_o,
    x_v, r_v, d_v, v_v, e_v, c_v, m_v,
    xp, xsb, hx, hy, hz, zsend, oh, gath, gath_t,
    w0, wh, wl, vh, vl, eacc, pacc, vsh, vsl,
    sep_loc, sep_hop, sep_all, base, state, stateb, fw_in, bw_in, ret,
    psend, pin1, psum1, pin2, pin3, pin4, pin5, pt_hl,
    orth, g_loc, gin1, gin2, gin3, gin4,
    loc_sem, send_sem, recv_sem,
):
    a, b, z = lax.axis_index("gx"), lax.axis_index("gy"), lax.axis_index("gz")
    size = {"gx": na, "gy": nb, "gz": nz}
    pos = {"gx": a, "gy": b, "gz": z}
    members, slots = nb // 2, na * 2
    member, core = b // 2, lax.rem(b, 2)
    slot = a * 2 + core
    group = RHS // members
    wide = SEP * members
    depth = slots * wide
    count = [0]
    sent = []

    def place(axis, index):
        if axis == "member":
            return (a, index * 2 + core, z)
        if axis == "slot":
            return (index // 2, member * 2 + lax.rem(index, 2), z)
        at = dict(pos)
        at[axis] = index
        return (at["gx"], at["gy"], at["gz"])

    size["member"], size["slot"] = members, slots
    pos_of = dict(pos, member=member, slot=slot)

    def send(src, dst, where, keep=True):
        n = count[0]
        count[0] += 1
        copy = pltpu.make_async_remote_copy(
            src_ref=src, dst_ref=dst, send_sem=send_sem.at[n], recv_sem=recv_sem.at[n],
            device_id=where, device_id_type=pl.DeviceIdType.MESH,
        )
        copy.start()
        if keep:
            sent.append(copy)
        return copy

    def share(axis, src_of, dst):
        n = size[axis]
        copies = []
        for d in range(1, n):
            to = lax.rem(pos_of[axis] + d, n)
            copies.append(send(src_of(to), dst, place(axis, to)))
        return copies

    def arrive(copies):
        for copy in copies:
            copy.wait_recv()

    barrier = pltpu.get_barrier_semaphore()
    partners = 0

    def greet(where):
        pl.semaphore_signal(
            barrier, inc=1, device_id=where, device_id_type=pl.DeviceIdType.MESH
        )

    for axis in ("gx", "gy", "gz"):
        for d in range(1, size[axis]):
            greet(place(axis, lax.rem(pos[axis] + d, size[axis])))
            partners += 1
    for d in range(1, na):
        greet((lax.rem(a + d, na), member * 2 + 1 - core, z))
        partners += 1

    def fetch(n, src, dst):
        copy = pltpu.make_async_copy(src, dst, loc_sem.at[n])
        copy.start()
        return copy

    get_x = fetch(0, x_h, x_v)
    get_m = [fetch(1 + i, h, m_v.at[i]) for i, h in enumerate((li_h, lo_h, up_h))]
    get_c = fetch(4, c_h, c_v)
    get_d = fetch(5, d_h, d_v)
    get_v = fetch(6, v_h, v_v)
    get_r = fetch(7, r_h, r_v)
    get_e = fetch(8, e_h, e_v)

    def slab(ref, s, n=RHS):
        return ref[pl.ds(s, n, stride=SLABS), :]

    def rows_at(start, n):
        return pl.ds(pl.multiple_of(start, n), n)

    get_x.wait()
    pad = CY + 2

    def spread_x(cx, carry):
        for cy in range(CY):
            v = slab(x_v, cx * CY + cy)
            xp[(cx + 1) * pad + cy + 1] = v
            xsb[cx, cy * RHS : (cy + 1) * RHS, :] = v.astype(bf16)
        return carry

    lax.fori_loop(0, CX, spread_x, 0)
    q32, l32 = iota((32, LANES), 0), iota((32, LANES), 1)

    def pick_edge(p, edge):
        pick = ((q32 == p) & (l32 == CZ - 1)) | ((q32 == 16 + p) & (l32 == 0))
        rows = xsb[p // 4, rows_at(lax.rem(p, 4) * 128, 128), :]
        return edge + nt(pick.astype(bf16), rows)

    zsend[...] = lax.fori_loop(
        0, PAIRS, pick_edge, jnp.zeros((32, LANES), f32), unroll=4
    ).astype(bf16)

    pl.semaphore_wait(barrier, partners)

    def ring(axis, step):
        n = size[axis]
        return place(axis, lax.rem(pos[axis] + step + n, n))

    halo = [
        send(xsb.at[CX - 1], hx.at[0], ring("gx", 1)),
        send(xsb.at[0], hx.at[1], ring("gx", -1)),
        send(xsb.at[:, pl.ds((CY - 1) * RHS, RHS)], hy.at[0], ring("gy", 1)),
        send(xsb.at[:, pl.ds(0, RHS)], hy.at[1], ring("gy", -1)),
        send(zsend.at[pl.ds(0, 16)], hz.at[0], ring("gz", 1)),
        send(zsend.at[pl.ds(16, 16)], hz.at[1], ring("gz", -1)),
    ]

    mine = rows_at(member * SEP, SEP)
    lane_group = iota((SEP, LANES), 1) // SEP
    per_tile = LANES // SEP
    for i in range(3):
        get_m[i].wait()

    def reorder(i, carry):
        tiles = [
            m_v[i, :, t * LANES : (t + 1) * LANES].astype(f32) for t in range(depth // LANES)
        ]
        for t in range(depth // LANES):
            out = jnp.zeros((SEP, LANES), f32)
            for g in range(per_tile):
                new = t * per_tile + g
                from_slot, from_member = new // members, new % members
                old = (from_slot // 2) * nb + from_member * 2 + from_slot % 2
                piece = tiles[old // per_tile]
                shift = ((g - old % per_tile) * SEP) % LANES
                if shift:
                    piece = pltpu.roll(piece, shift, 1)
                out = jnp.where(lane_group == g, piece, out)
            gath[i, mine, t * LANES : (t + 1) * LANES] = out.astype(bf16)
        return carry

    lax.fori_loop(0, 3, reorder, 0)

    def share_matrix(i):
        return share("member", lambda to: gath.at[i, mine], gath.at[i, mine])

    gather_base = share_matrix(0)

    get_c.wait()
    cells = jnp.broadcast_to(c_v[...], (SEP, SEP)).astype(f32)
    square = iota((SEP, SEP), 0) == iota((SEP, SEP), 1)
    column = jnp.sum(jnp.where(square, cells, 0.0), axis=1, keepdims=True)
    column = jnp.broadcast_to(column, (SEP, 2 * CZ))
    z256 = iota((SEP, 2 * CZ), 1)

    def mark(p, carry):
        oh[p] = jnp.zeros((wide, 2 * CZ), bf16)
        at = (z256 + p * 2 * CZ).astype(f32)
        oh[p, mine, :] = jnp.where(column == at, 1.0, 0.0).astype(bf16)
        return carry

    lax.fori_loop(0, PAIRS, mark, 0)

    get_d.wait()
    get_v.wait()
    get_r.wait()
    arrive(halo)

    before_z = hz[0].astype(f32) * flag(z > 0)
    after_z = hz[1].astype(f32) * flag(z < nz - 1)
    ends = jnp.concatenate(
        [before_z, after_z, jnp.zeros((LANES - 32, LANES), f32)], axis=0
    ).T.astype(bf16)
    for k, mask in enumerate((flag(a > 0), flag(a < na - 1))):
        for cy in range(CY):
            xp[k * (CX + 1) * pad + cy + 1] = (
                hx[k, cy * RHS : (cy + 1) * RHS, :].astype(f32) * mask
            )
    for k, mask in enumerate((flag(b > 0), flag(b < nb - 1))):
        for cx in range(CX):
            xp[(cx + 1) * pad + k * (CY + 1)] = hy[k, cx].astype(f32) * mask
    q128, l128 = iota((LANES, LANES), 0), iota((LANES, LANES), 1)
    lane64 = iota((RHS, LANES), 1)

    def residual_of(p, seps):
        spread = ((q128 == p) & (l128 == 0)) | ((q128 == 16 + p) & (l128 == CZ - 1))
        z_ends = nn(ends, spread.astype(bf16))
        halves = []
        for h in range(2):
            s = 2 * p + h
            i = (p // 4 + 1) * pad + lax.rem(p, 4) * 2 + h + 1
            x = xp[i]
            diag = 6.0 + d_v[pl.ds(s, 1), :]
            v0, v1, v2 = (v_v[pl.ds(k * SLABS + s, 1), :] for k in range(3))
            end = z_ends[h * RHS : (h + 1) * RHS, :]
            before = jnp.where(lane64 == 0, end, pltpu.roll(x, 1, 1))
            after = jnp.where(lane64 == CZ - 1, end, pltpu.roll(x, CZ - 1, 1))
            res = slab(r_v, s) - diag * x
            res = res + (1.0 + v0) * xp[i - pad] + (1.0 - v0) * xp[i + pad]
            res = res + (1.0 + v1) * xp[i - 1] + (1.0 - v1) * xp[i + 1]
            res = res + (1.0 + v2) * before + (1.0 - v2) * after
            r_v[pl.ds(s, RHS, stride=SLABS), :] = res
            halves.append(res.astype(bf16))
            w = res / diag
            hi, lo = split(w)
            at = slice(h * CZ, (h + 1) * CZ)
            w0[p, :, at] = w
            wh[p, :, at] = hi
            wl[p, :, at] = lo
        return seps + nt(jnp.concatenate(halves, axis=1), oh[p])

    seps = lax.fori_loop(0, PAIRS, residual_of, jnp.zeros((RHS, wide), f32))
    put_res = pltpu.make_async_copy(r_v, res_o, loc_sem.at[9])
    put_res.start()

    sep_loc[...] = seps.astype(bf16).reshape(members, group, wide)
    hop = share("member", lambda to: sep_loc.at[to], sep_hop.at[member])
    sep_hop[member] = sep_loc[member]
    gather_fw = share_matrix(1)
    arrive(hop)
    mixed = sep_hop[0].astype(f32)
    for i in range(1, members):
        mixed = mixed + sep_hop[i].astype(f32)
    sep_all[slot] = mixed.astype(bf16)
    hop = share("slot", lambda to: sep_all.at[slot], sep_all.at[slot])
    gather_bw = share_matrix(2)
    arrive(gather_base)
    arrive(hop)

    def row_of(ref):
        return jnp.concatenate([ref[i] for i in range(slots)], axis=1)

    base[...] = nt(row_of(sep_all), gath[0])

    vecs = e_v.shape[0] // SLABS

    def earlier_work():
        get_e.wait()
        eacc[...] = jnp.zeros(eacc.shape, f32)

        def step(p, carry):
            both = jnp.concatenate(
                [slab(e_v, 2 * p, vecs), slab(e_v, 2 * p + 1, vecs)], axis=1
            )
            hi, lo = split(both)
            vh[p] = hi
            vl[p] = lo
            right = jnp.concatenate([wh[p], wl[p], oh[p]], axis=0)
            eacc[:vecs] += nt(hi, right)
            eacc[vecs:] += nt(lo, right)
            return carry

        lax.fori_loop(0, PAIRS, step, 0)
        main = eacc[:vecs, :LANES] + eacc[vecs:, :LANES]
        main = main.T
        pacc[...] = main[:RHS] + main[RHS:]
        vsh[...] = eacc[:vecs, LANES:].T.astype(bf16)
        vsl[...] = eacc[vecs:, LANES:].T.astype(bf16)

    def sweep_copies(first, dst, step):
        copies = []
        for d in range(slots):
            to = lax.rem(slot + d, slots)
            copies.append(
                pltpu.make_async_remote_copy(
                    src_ref=stateb.at[0 if step > 0 else 1], dst_ref=dst.at[slot],
                    send_sem=send_sem.at[first + d], recv_sem=recv_sem.at[first + d],
                    device_id=(to // 2, member * 2 + lax.rem(to, 2), z + step),
                    device_id_type=pl.DeviceIdType.MESH,
                )
            )
        return copies

    def sweep_push(first, dst, step):
        for copy in sweep_copies(first, dst, step):
            copy.start()

    pl.when(z >= early)(earlier_work)

    fw_first = count[0]
    bw_first = fw_first + slots
    count[0] = bw_first + slots
    arrive(gather_fw)

    @pl.when(z == 0)
    def _():
        state[...] = base[...]

    @pl.when(z > 0)
    def _():
        gath_t[...] = gath[1].astype(f32).T.astype(bf16)
        arrive(sweep_copies(fw_first, fw_in, 1))
        state[...] = base[...] - nn(row_of(fw_in), gath_t[...])

    @pl.when(z < nz - 1)
    def _():
        stateb[0] = state[...].astype(bf16)
        sweep_push(fw_first, fw_in, 1)

    pl.when(z < early)(earlier_work)
    arrive(gather_bw)

    @pl.when(z < nz - 1)
    def _():
        gath_t[...] = gath[2].astype(f32).T.astype(bf16)
        arrive(sweep_copies(bw_first, bw_in, -1))
        state[...] = state[...] - nn(row_of(bw_in), gath_t[...])

    @pl.when(z > 0)
    def _():
        stateb[1] = state[...].astype(bf16)
        sweep_push(bw_first, bw_in, -1)

    hop = share("member", lambda to: state, ret.at[member])
    ret[member] = state[...]
    arrive(hop)
    sol_h, sol_l = split(ret[...].reshape(RHS, wide))
    corr = nn(jnp.concatenate([sol_h, sol_l], axis=0), vsh[...])
    corr = pacc[...] + corr[:RHS] + corr[RHS:] + nn(sol_h, vsl[...])
    cols = vecs

    part_rows = RHS // na
    psend[...] = corr.reshape(na, part_rows, cols)
    hop = share("gx", lambda to: psend.at[to], pin1.at[a])
    pin1[a] = psend[a]

    sol_hl = jnp.concatenate([sol_h, sol_l], axis=1)

    def add_sol(p, carry):
        w0[p] = w0[p] + nn(sol_hl, jnp.concatenate([oh[p], oh[p]], axis=0))
        return carry

    lax.fori_loop(0, PAIRS, add_sol, 0, unroll=2)

    def total_of(ref, n):
        out = ref[0]
        for i in range(1, n):
            out = out + ref[i]
        return out

    arrive(hop)
    part = total_of(pin1, na)
    ph = part_rows // 8
    pw = nb // ph
    width = cols // pw
    for i in range(nb):
        r, c = divmod(i, pw)
        psum1[i] = part[r * 8 : r * 8 + 8, c * width : (c + 1) * width]
    hop = share("gy", lambda to: psum1.at[to], pin2.at[b])
    pin2[b] = psum1[b]
    arrive(hop)
    pin3[z] = total_of(pin2, nb)
    arrive(share("gz", lambda to: pin3.at[z], pin3.at[z]))
    pin4[b] = total_of(pin3, nz)
    arrive(share("gy", lambda to: pin4.at[b], pin4.at[b]))
    pin5[a] = jnp.concatenate(
        [jnp.concatenate([pin4[r * pw + c] for c in range(pw)], axis=1) for r in range(ph)], axis=0
    )
    arrive(share("gx", lambda to: pin5.at[a], pin5.at[a]))
    full = pin5[...].reshape(RHS, cols)
    pin5_put = pltpu.make_async_copy(pin5, proj_o, loc_sem.at[10])
    pin5_put.start()
    hi, lo = split(full)
    pt_hl[:RHS] = hi
    pt_hl[RHS:] = lo

    def project(p, gram):
        main = nn(pt_hl[...], vh[p])
        o = w0[p] - (main[:RHS] + main[RHS:] + nn(pt_hl[:RHS], vl[p]))
        hi, lo = split(o)
        both = jnp.concatenate([hi, lo], axis=0)
        orth[p] = both
        return gram + nt(both, both)

    gram = lax.fori_loop(0, PAIRS, project, jnp.zeros((2 * RHS, 2 * RHS), f32), unroll=2)
    gram = gram[:RHS] + gram[RHS:]
    gram = gram + pltpu.roll(gram, RHS, 1)
    put_orth = pltpu.make_async_copy(orth, orth_o, loc_sem.at[11])
    put_orth.start()
    piece = RHS // nz
    g_loc[...] = gram.reshape(nz, piece, LANES)
    hop = share("gz", lambda to: g_loc.at[to], gin1.at[z])
    gin1[z] = g_loc[z]
    arrive(hop)
    gin2[b] = total_of(gin1, nz)
    arrive(share("gy", lambda to: gin2.at[b], gin2.at[b]))
    gin3[a] = total_of(gin2, nb)
    arrive(share("gx", lambda to: gin3.at[a], gin3.at[a]))
    gin4[z] = total_of(gin3, na)
    arrive(share("gz", lambda to: gin4.at[z], gin4.at[z]))

    put_gram = pltpu.make_async_copy(gin4, gram_o, loc_sem.at[12])
    put_gram.start()
    for copy in sent:
        copy.wait_send()

    @pl.when(z < nz - 1)
    def _():
        for copy in sweep_copies(fw_first, fw_in, 1):
            copy.wait_send()

    @pl.when(z > 0)
    def _():
        for copy in sweep_copies(bw_first, bw_in, -1):
            copy.wait_send()

    for put in (put_res, pin5_put, put_orth, put_gram):
        put.wait()


def finish_kernel(
    scale, gram_v, orth_h, res_h, proj_h, res_o, new_o, proj_o, chol_o,
    orth, rows_v, new_v, res_v, proj_v, sem,
):
    get = pltpu.make_async_copy(orth_h, orth, sem.at[0])
    hand_on = [
        (pltpu.make_async_copy(res_h, res_v, sem.at[1]), pltpu.make_async_copy(res_v, res_o, sem.at[2])),
        (pltpu.make_async_copy(proj_h, proj_v, sem.at[3]), pltpu.make_async_copy(proj_v, proj_o, sem.at[4])),
    ]
    get.start()
    for copy, _ in hand_on:
        copy.start()
    cholesky_rows(gram_v[...], rows_v)
    rows = rows_v[...]
    lane64, row64 = iota((RHS, LANES), 1), iota((RHS, LANES), 0)
    upper = jnp.where((lane64 >= row64) & (lane64 < RHS), rows * (1.0 / scale), 0.0)
    inverse = jnp.where(lane64 - RHS <= row64, rows * scale, 0.0)
    hi, lo = split(inverse)
    lhs = jnp.where(lane64 < RHS, pltpu.roll(hi.astype(f32), RHS, 1), lo.astype(f32)).astype(bf16)
    lhs = jnp.concatenate([lhs, lhs], axis=1)
    for copy, onward in hand_on:
        copy.wait()
        onward.start()
    get.wait()

    def finish(p, carry):
        hi, lo = orth[p, :RHS], orth[p, RHS:]
        out = nn(lhs, jnp.concatenate([hi, hi, lo, lo], axis=0))
        for h in range(2):
            new_v[pl.ds(2 * p + h, RHS, stride=SLABS), :] = out[:, h * CZ : (h + 1) * CZ]
        return carry

    lax.fori_loop(0, PAIRS, finish, 0, unroll=2)
    put_new = pltpu.make_async_copy(new_v, new_o, sem.at[5])
    put_new.start()
    upper = jnp.concatenate([upper, jnp.zeros((LANES - RHS, LANES), f32)], axis=0)
    chol_o[...] = upper.T[:RHS, :RHS]
    for _, onward in hand_on:
        onward.wait()
    put_new.wait()


def body(
    x_field, right_side, diag_shift, velocity, earlier_blocks, sep_cells, low_inv, low_off, up_off
):
    na, nb, nz = (lax.axis_size(n) for n in ("gx", "gy", "gz"))
    members, slots = nb // 2, na * 2
    group, wide = RHS // members, SEP * members
    depth = slots * wide
    part_rows = RHS // na
    vecs = earlier_blocks.shape[0] * earlier_blocks.shape[1]
    pw = nb // (part_rows // 8)
    width = vecs // pw
    piece = RHS // nz
    vmem = pltpu.VMEM
    scratch = [
        vmem((ROWS, CZ), f32),
        vmem((ROWS, CZ), f32),
        vmem((SLABS, CZ), f32),
        vmem((3 * SLABS, CZ), f32),
        vmem((vecs * SLABS, CZ), f32),
        vmem((1, SEP), jnp.int32),
        vmem((3, SEP, depth), bf16),
        vmem(((CX + 2) * (CY + 2), RHS, CZ), f32),
        vmem((CX, CY * RHS, CZ), bf16),
        vmem((2, CY * RHS, CZ), bf16),
        vmem((2, CX, RHS, CZ), bf16),
        vmem((2, 16, LANES), bf16),
        vmem((32, LANES), bf16),
        vmem((PAIRS, wide, 2 * CZ), bf16),
        vmem((3, wide, depth), bf16),
        vmem((depth, wide), bf16),
        vmem((PAIRS, RHS, 2 * CZ), f32),
        vmem((PAIRS, RHS, 2 * CZ), bf16),
        vmem((PAIRS, RHS, 2 * CZ), bf16),
        vmem((PAIRS, vecs, 2 * CZ), bf16),
        vmem((PAIRS, vecs, 2 * CZ), bf16),
        vmem((2 * vecs, 2 * LANES), f32),
        vmem((RHS, vecs), f32),
        vmem((wide, vecs), bf16),
        vmem((wide, vecs), bf16),
        vmem((members, group, wide), bf16),
        vmem((members, group, wide), bf16),
        vmem((slots, group, wide), bf16),
        vmem((group, wide), f32),
        vmem((group, wide), f32),
        vmem((2, group, wide), bf16),
        vmem((slots, group, wide), bf16),
        vmem((slots, group, wide), bf16),
        vmem((members, group, wide), f32),
        vmem((na, part_rows, vecs), f32),
        vmem((na, part_rows, vecs), f32),
        vmem((nb, 8, width), f32),
        vmem((nb, 8, width), f32),
        vmem((nz, 8, width), f32),
        vmem((nb, 8, width), f32),
        vmem((na, part_rows, vecs), f32),
        vmem((2 * RHS, vecs), bf16),
        vmem((PAIRS, 2 * RHS, 2 * CZ), bf16),
        vmem((nz, piece, LANES), f32),
        vmem((nz, piece, LANES), f32),
        vmem((nb, piece, LANES), f32),
        vmem((na, piece, LANES), f32),
        vmem((nz, piece, LANES), f32),
        pltpu.SemaphoreType.DMA((13,)),
        pltpu.SemaphoreType.DMA((128,)),
        pltpu.SemaphoreType.DMA((128,)),
    ]
    flat = lambda v: v.reshape(-1, CZ)
    anywhere = pl.BlockSpec(memory_space=pl.ANY)
    in_vmem = pl.BlockSpec(memory_space=pltpu.VMEM)
    res, orth, projection, gram = pl.pallas_call(
        functools.partial(kernel, na, nb, nz, (nz * 5) // 8),
        out_shape=(
            jax.ShapeDtypeStruct((ROWS, CZ), f32),
            jax.ShapeDtypeStruct((PAIRS, 2 * RHS, 2 * CZ), bf16),
            jax.ShapeDtypeStruct((na, part_rows, vecs), f32),
            jax.ShapeDtypeStruct((nz, piece, LANES), f32),
        ),
        in_specs=[anywhere] * 9,
        out_specs=(anywhere,) * 4,
        scratch_shapes=scratch,
        compiler_params=pltpu.CompilerParams(
            collective_id=0, has_side_effects=True, vmem_limit_bytes=60 * 2**20
        ),
        cost_estimate=pl.CostEstimate(
            flops=2 * 10**9, bytes_accessed=13 * 2**20, transcendentals=0
        ),
        name="step",
    )(
        flat(x_field), flat(right_side), flat(diag_shift), flat(velocity), flat(earlier_blocks),
        sep_cells, low_inv[0], low_off[0], up_off[0],
    )
    res, new, projection, factor = pl.pallas_call(
        functools.partial(finish_kernel, math.sqrt(na * nb * nz * CX * CY * CZ)),
        out_shape=(
            jax.ShapeDtypeStruct((ROWS, CZ), f32),
            jax.ShapeDtypeStruct((ROWS, CZ), f32),
            jax.ShapeDtypeStruct((RHS, vecs), f32),
            jax.ShapeDtypeStruct((RHS, RHS), f32),
        ),
        in_specs=[in_vmem, anywhere, anywhere, anywhere],
        out_specs=(anywhere, anywhere, anywhere, in_vmem),
        scratch_shapes=[
            vmem((PAIRS, 2 * RHS, 2 * CZ), bf16),
            vmem((RHS, LANES), f32),
            vmem((ROWS, CZ), f32),
            vmem((ROWS, CZ), f32),
            vmem((RHS, vecs), f32),
            pltpu.SemaphoreType.DMA((6,)),
        ],
        compiler_params=pltpu.CompilerParams(vmem_limit_bytes=60 * 2**20),
        cost_estimate=pl.CostEstimate(flops=2 * 10**8, bytes_accessed=5 * 2**20, transcendentals=0),
        name="finish",
    )(gram.reshape(RHS, LANES), orth, res, projection.reshape(RHS, vecs))
    shape = right_side.shape
    return (res.reshape(shape), new.reshape(shape), projection.T, factor)


def solution(mesh):
    return jax.shard_map(
        body,
        mesh=mesh,
        in_specs=(
            P(None, "gx", "gy", "gz"),
            P(None, "gx", "gy", "gz"),
            P("gx", "gy", "gz"),
            P(None, "gx", "gy", "gz"),
            P(None, None, "gx", "gy", "gz"),
            P("gz", ("gx", "gy")),
            P("gz", ("gx", "gy"), None),
            P("gz", ("gx", "gy"), None),
            P("gz", ("gx", "gy"), None),
        ),
        out_specs=(P(None, "gx", "gy", "gz"), P(None, "gx", "gy", "gz"), P(), P()),
        check_vma=False,
    )
```

time: 150 us -> 139 us (0.927)
  local copies, waits for them, and re-layouts: 9.23 us -> 0 us
  Pallas kernels: 140 us -> 138 us
    unnamed x18 -> x0, local copies, waits for them, and re-layouts: 9.23 us -> none
    pallas_call x1, Pallas kernels: 140 us -> 130 us  [body(): pl.pallas_call(functools.partial(kernel, na, nb, nz, nz * 5 // 8), out_sh...]
    pallas_call x0 -> x1, Pallas kernels: none -> 7.66 us  [body(): pl.pallas_call(functools.partial(finish_kernel, math.sqrt(na * nb * nz *...]
where the time goes in v2:
time: 139 us
  Pallas kernels  138 us (99%)
    pallas_call x1, Pallas kernels, body(): pl.pallas_call(functools.partial(kernel, na, nb, nz, nz * 5 // 8), out_sh...  130 us
    pallas_call x1, Pallas kernels, body(): pl.pallas_call(functools.partial(finish_kernel, math.sqrt(na * nb * nz *...  7.66 us

profile of v2, /device:TPU:1, one launch (start us, length us, event | category | flops | bytes accessed | tf_op | source)
XLA Modules:
  0.0 138.8 jit_solution(15971545180770452523)
XLA Ops:
  0.6 130.5 %step.1 = (f32[2048,128]{1,0:T(8,128)}, bf16[16,128,256]{2,1,0:T(8,128)(2,1)}, f32[4,16,512]{2,1,0:T(8,128)}, f32[8,8,128]{2,1,0:T(8,128)}) custom-call(f32[2048,128]{1,0:T(8,128)} %bitcast.14, f32[2048,128]{1,0:T(8,128)} %bitcast.15, f32[32,128]{1,0:T(8,128)} %bitcast.22, f32[96,128]{1,0:T(8,128)} %bitcast.20, f32[16384,128]{1,0:T(8,128)} %bitcast.13, ...), custom_call_target="tpu_custom_call" | custom-call | flops 2000000000 | bytes 13631488 | tf_op jit(solution)/shard_map/step/pallas_call | solution.py:622
  131.1 7.7 %finish.1 = (f32[2048,128]{1,0:T(8,128)}, f32[2048,128]{1,0:T(8,128)}, f32[64,512]{1,0:T(8,128)}, f32[64,64]{1,0:T(8,128)}) custom-call(f32[64,128]{1,0:T(8,128)} %bitcast.21, bf16[16,128,256]{2,1,0:T(8,128)(2,1)} %get-tuple-element.13.orth_h, f32[2048,128]{1,0:T(8,128)} %get-tuple-element.14.res_h, f32[64,512]{1,0:T(8,128)} %bitcast.16), custom_call_target="tpu_custom_call" | custom-call | flops 200000000 | bytes 5242880 | tf_op jit(solution)/shard_map/finish/pallas_call | solution.py:644

commit v3 on v2

--- a/solution.py
+++ b/solution.py
@@ -12,6 +12,7 @@
 RHS, CX, CY, CZ, SEP = 64, 4, 8, 128, 32
 SLABS = CX * CY
 PAIRS = SLABS // 2
+QUADS = SLABS // 4
 ROWS = RHS * SLABS
 LANES = 128
 
@@ -84,13 +85,13 @@
 
 
 def kernel(
-    na, nb, nz, early,
+    na, nb, nz,
     x_h, r_h, d_h, v_h, e_h, c_h, li_h, lo_h, up_h,
     res_o, orth_o, proj_o, gram_o,
     x_v, r_v, d_v, v_v, e_v, c_v, m_v,
-    xp, xsb, hx, hy, hz, zsend, oh, gath, gath_t,
+    xp, xsb, hx, hy, hz, zsend, oh, gath, gath_in, gath_t,
     w0, wh, wl, vh, vl, eacc, pacc, vsh, vsl,
-    sep_loc, sep_hop, sep_all, base, state, stateb, fw_in, bw_in, ret,
+    sep_loc, sep_hop, sep_all, base_loc, base_in, base, state, stateb, tiles, fw_in, bw_in, ret,
     psend, pin1, psum1, pin2, pin3, pin4, pin5, pt_hl,
     orth, g_loc, gin1, gin2, gin3, gin4,
     loc_sem, send_sem, recv_sem,
@@ -100,10 +101,11 @@
     pos = {"gx": a, "gy": b, "gz": z}
     members, slots = nb // 2, na * 2
     member, core = b // 2, lax.rem(b, 2)
-    slot = a * 2 + core
+    slot = core * na + a
     group = RHS // members
     wide = SEP * members
     depth = slots * wide
+    half = na * wide
     count = [0]
     sent = []
 
@@ -111,7 +113,7 @@
         if axis == "member":
             return (a, index * 2 + core, z)
         if axis == "slot":
-            return (index // 2, member * 2 + lax.rem(index, 2), z)
+            return (lax.rem(index, na), member * 2 + index // na, z)
         at = dict(pos)
         at[axis] = index
         return (at["gx"], at["gy"], at["gz"])
@@ -119,25 +121,34 @@
     size["member"], size["slot"] = members, slots
     pos_of = dict(pos, member=member, slot=slot)
 
-    def send(src, dst, where, keep=True):
-        n = count[0]
-        count[0] += 1
-        copy = pltpu.make_async_remote_copy(
+    def remote(n, src, dst, where):
+        return pltpu.make_async_remote_copy(
             src_ref=src, dst_ref=dst, send_sem=send_sem.at[n], recv_sem=recv_sem.at[n],
             device_id=where, device_id_type=pl.DeviceIdType.MESH,
         )
+
+    def send(src, dst, where):
+        copy = remote(count[0], src, dst, where)
+        count[0] += 1
         copy.start()
-        if keep:
-            sent.append(copy)
+        sent.append(copy.wait_send)
         return copy
+
+    def exchange(pairs, dst):
+        n = count[0]
+        count[0] += 1
+        for src, there, where in pairs:
+            remote(n, src, there, where).start()
+        whole = dst.at[pl.ds(0, len(pairs))]
+        out = pltpu.make_async_copy(whole, whole, send_sem.at[n])
+        sent.append(out.wait)
+        return pltpu.make_async_copy(whole, whole, recv_sem.at[n])
 
     def share(axis, src_of, dst):
         n = size[axis]
-        copies = []
-        for d in range(1, n):
-            to = lax.rem(pos_of[axis] + d, n)
-            copies.append(send(src_of(to), dst, place(axis, to)))
-        return copies
+        others = [lax.rem(pos_of[axis] + d, n) for d in range(1, n)]
+        there = dst.at[pos_of[axis]]
+        return exchange([(src_of(to), there, place(axis, to)) for to in others], dst)
 
     def arrive(copies):
         for copy in copies:
@@ -151,11 +162,14 @@
             barrier, inc=1, device_id=where, device_id_type=pl.DeviceIdType.MESH
         )
 
-    for axis in ("gx", "gy", "gz"):
+    for axis in ("gy", "gz"):
         for d in range(1, size[axis]):
             greet(place(axis, lax.rem(pos[axis] + d, size[axis])))
             partners += 1
     for d in range(1, na):
+        for e in range(members):
+            greet((lax.rem(a + d, na), lax.rem(member + e, members) * 2 + core, z))
+            partners += 1
         greet((lax.rem(a + d, na), member * 2 + 1 - core, z))
         partners += 1
 
@@ -170,7 +184,11 @@
     get_d = fetch(5, d_h, d_v)
     get_v = fetch(6, v_h, v_v)
     get_r = fetch(7, r_h, r_v)
-    get_e = fetch(8, e_h, e_v)
+    chunk = e_v.shape[0] // 4
+    get_e = [
+        fetch((8, 13, 14, 15)[i], e_h.at[pl.ds(i * chunk, chunk)], e_v.at[pl.ds(i * chunk, chunk)])
+        for i in range(4)
+    ]
 
     def slab(ref, s, n=RHS):
         return ref[pl.ds(s, n, stride=SLABS), :]
@@ -189,28 +207,30 @@
         return carry
 
     lax.fori_loop(0, CX, spread_x, 0)
-    q32, l32 = iota((32, LANES), 0), iota((32, LANES), 1)
-
-    def pick_edge(p, edge):
-        pick = ((q32 == p) & (l32 == CZ - 1)) | ((q32 == 16 + p) & (l32 == 0))
-        rows = xsb[p // 4, rows_at(lax.rem(p, 4) * 128, 128), :]
-        return edge + nt(pick.astype(bf16), rows)
-
-    zsend[...] = lax.fori_loop(
-        0, PAIRS, pick_edge, jnp.zeros((32, LANES), f32), unroll=4
-    ).astype(bf16)
-
     pl.semaphore_wait(barrier, partners)
 
     def ring(axis, step):
         n = size[axis]
-        return place(axis, lax.rem(pos[axis] + step + n, n))
+        return place(axis, lax.rem(pos_of[axis] + step + n, n))
 
     halo = [
         send(xsb.at[CX - 1], hx.at[0], ring("gx", 1)),
         send(xsb.at[0], hx.at[1], ring("gx", -1)),
         send(xsb.at[:, pl.ds((CY - 1) * RHS, RHS)], hy.at[0], ring("gy", 1)),
         send(xsb.at[:, pl.ds(0, RHS)], hy.at[1], ring("gy", -1)),
+    ]
+    q32, l32 = iota((32, LANES), 0), iota((32, LANES), 1)
+
+    def pick_edge(p, edge):
+        pick = ((q32 == p) & (l32 == CZ - 1)) | ((q32 == 16 + p) & (l32 == 0))
+        rows = xsb[p // 4, rows_at(lax.rem(p, 4) * 128, 128), :]
+        return edge + nt(pick.astype(bf16), rows)
+
+    zsend[...] = lax.fori_loop(
+        0, PAIRS, pick_edge, jnp.zeros((32, LANES), f32), unroll=4
+    ).astype(bf16)
+
+    halo += [
         send(zsend.at[pl.ds(0, 16)], hz.at[0], ring("gz", 1)),
         send(zsend.at[pl.ds(16, 16)], hz.at[1], ring("gz", -1)),
     ]
@@ -221,50 +241,138 @@
     for i in range(3):
         get_m[i].wait()
 
-    def reorder(i, carry):
-        tiles = [
+    def reorder(i):
+        pieces = [
             m_v[i, :, t * LANES : (t + 1) * LANES].astype(f32) for t in range(depth // LANES)
         ]
         for t in range(depth // LANES):
             out = jnp.zeros((SEP, LANES), f32)
             for g in range(per_tile):
-                new = t * per_tile + g
-                from_slot, from_member = new // members, new % members
-                old = (from_slot // 2) * nb + from_member * 2 + from_slot % 2
-                piece = tiles[old // per_tile]
+                old = (t % na) * nb + g * 2 + t // na
+                piece = pieces[old // per_tile]
                 shift = ((g - old % per_tile) * SEP) % LANES
                 if shift:
                     piece = pltpu.roll(piece, shift, 1)
                 out = jnp.where(lane_group == g, piece, out)
-            gath[i, mine, t * LANES : (t + 1) * LANES] = out.astype(bf16)
-        return carry
-
-    lax.fori_loop(0, 3, reorder, 0)
-
-    def share_matrix(i):
-        return share("member", lambda to: gath.at[i, mine], gath.at[i, mine])
-
-    gather_base = share_matrix(0)
+            at = slice(t * LANES, (t + 1) * LANES)
+            if i == 0:
+                gath_in[mine, at] = out.astype(bf16)
+            else:
+                gath[i - 1, a, member, :, at] = out.astype(bf16)
+
+    for i in range(3):
+        reorder(i)
+
+    axes = ("member", "gx")
+
+    def own(m, c):
+        return gath.at[m, a, member, :, pl.ds(c * half, half)]
+
+    def near(m, c, axis, step, part):
+        at = ring_index(axis, step)
+        rows = pl.ds(part * (SEP // 2), SEP // 2)
+        if axis == "member":
+            return gath.at[m, a, at, rows, pl.ds(c * half, half)]
+        return gath.at[m, at, member, rows, pl.ds(c * half, half)]
+
+    def line(m, c, axis, step):
+        at = ring_index(axis, step)
+        if axis == "member":
+            return gath.at[m, :, at, :, pl.ds(c * half, half)]
+        return gath.at[m, at, :, :, pl.ds(c * half, half)]
+
+    def near_line(m, c, axis, step, part):
+        at = ring_index(axis, step)
+        cut = pl.ds(part * 2, 2)
+        if axis == "member":
+            return gath.at[m, cut, at, :, pl.ds(c * half, half)]
+        return gath.at[m, at, cut, :, pl.ds(c * half, half)]
+
+    def ring_index(axis, step):
+        return lax.rem(pos_of[axis] + step + size[axis], size[axis])
+
+    def later(src, where):
+        copy = remote(count[0], src, src, where)
+        count[0] += 1
+        return copy
+
+    def ring_pair(block, axis):
+        return [later(block, ring(axis, step)) for step in (1, -1)]
+
+    def gather_stages(m):
+        one, two, three, four = [], [], [], []
+        for c in range(2):
+            first, second = axes[c], axes[1 - c]
+            one += ring_pair(own(m, c), first)
+            three += ring_pair(line(m, c, second, 0), second)
+            for part, step in enumerate((1, -1)):
+                two.append(later(near(m, c, first, -step, part), ring(first, step)))
+                four.append(later(near_line(m, c, second, -step, part), ring(second, step)))
+        return one, two, three, four
+
+    def launch(copies):
+        for copy in copies:
+            copy.start()
+
+    def relay(came, onward):
+        for got, copy in zip(came, onward):
+            got.wait_recv()
+            copy.start()
+
+    low_stages, up_stages = gather_stages(0), gather_stages(1)
+    use_low, use_up = z > 0, z < nz - 1
+    up_after = z < (nz * 5) // 8
+    up_before = jnp.logical_and(use_up, jnp.logical_not(up_after))
+    pl.when(use_low)(lambda: launch(low_stages[0]))
+    gather_base = [
+        send(gath_in.at[mine], gath_in.at[mine], place("member", lax.rem(member + d, members)))
+        for d in range(1, members)
+    ]
 
     get_c.wait()
     cells = jnp.broadcast_to(c_v[...], (SEP, SEP)).astype(f32)
     square = iota((SEP, SEP), 0) == iota((SEP, SEP), 1)
     column = jnp.sum(jnp.where(square, cells, 0.0), axis=1, keepdims=True)
-    column = jnp.broadcast_to(column, (SEP, 2 * CZ))
-    z256 = iota((SEP, 2 * CZ), 1)
-
-    def mark(p, carry):
-        oh[p] = jnp.zeros((wide, 2 * CZ), bf16)
-        at = (z256 + p * 2 * CZ).astype(f32)
-        oh[p, mine, :] = jnp.where(column == at, 1.0, 0.0).astype(bf16)
+    column = jnp.broadcast_to(column, (SEP, 4 * CZ))
+    z512 = iota((SEP, 4 * CZ), 1)
+
+    def mark(q, carry):
+        oh[q] = jnp.zeros((wide, 4 * CZ), bf16)
+        at = (z512 + q * 4 * CZ).astype(f32)
+        oh[q, mine, :] = jnp.where(column == at, 1.0, 0.0).astype(bf16)
         return carry
 
-    lax.fori_loop(0, PAIRS, mark, 0)
-
+    lax.fori_loop(0, QUADS, mark, 0)
+
+    vecs = e_v.shape[0] // SLABS
+    part_vecs = vecs // 4
+
+    def relayout(c):
+        get_e[c].wait()
+        at = slice(c * part_vecs, (c + 1) * part_vecs)
+
+        def step(q, carry):
+            for h in range(4):
+                rows = pl.ds(c * chunk + 4 * q + h, part_vecs, stride=SLABS)
+                hi, lo = split(e_v[rows, :])
+                vh[q, at, h * CZ : (h + 1) * CZ] = hi
+                vl[q, at, h * CZ : (h + 1) * CZ] = lo
+            return carry
+
+        lax.fori_loop(0, QUADS, step, 0)
+
+    split_early = z >= 2
+    pl.when(split_early)(lambda: relayout(0))
     get_d.wait()
     get_v.wait()
     get_r.wait()
+    pl.when(use_low)(lambda: relay(low_stages[0], low_stages[1]))
     arrive(halo)
+
+    @pl.when(use_low)
+    def _():
+        arrive(low_stages[1])
+        launch(low_stages[2])
 
     before_z = hz[0].astype(f32) * flag(z > 0)
     after_z = hz[1].astype(f32) * flag(z < nz - 1)
@@ -282,17 +390,19 @@
     q128, l128 = iota((LANES, LANES), 0), iota((LANES, LANES), 1)
     lane64 = iota((RHS, LANES), 1)
 
-    def residual_of(p, seps):
-        spread = ((q128 == p) & (l128 == 0)) | ((q128 == 16 + p) & (l128 == CZ - 1))
-        z_ends = nn(ends, spread.astype(bf16))
-        halves = []
-        for h in range(2):
-            s = 2 * p + h
-            i = (p // 4 + 1) * pad + lax.rem(p, 4) * 2 + h + 1
+    def residual_of(q, seps):
+        slabs = []
+        for h in range(4):
+            s = 4 * q + h
+            if h % 2 == 0:
+                p = 2 * q + h // 2
+                spread = ((q128 == p) & (l128 == 0)) | ((q128 == 16 + p) & (l128 == CZ - 1))
+                z_ends = nn(ends, spread.astype(bf16))
+            i = (q // 2 + 1) * pad + lax.rem(q, 2) * 4 + h + 1
             x = xp[i]
             diag = 6.0 + d_v[pl.ds(s, 1), :]
             v0, v1, v2 = (v_v[pl.ds(k * SLABS + s, 1), :] for k in range(3))
-            end = z_ends[h * RHS : (h + 1) * RHS, :]
+            end = z_ends[(h % 2) * RHS : (h % 2 + 1) * RHS, :]
             before = jnp.where(lane64 == 0, end, pltpu.roll(x, 1, 1))
             after = jnp.where(lane64 == CZ - 1, end, pltpu.roll(x, CZ - 1, 1))
             res = slab(r_v, s) - diag * x
@@ -300,87 +410,123 @@
             res = res + (1.0 + v1) * xp[i - 1] + (1.0 - v1) * xp[i + 1]
             res = res + (1.0 + v2) * before + (1.0 - v2) * after
             r_v[pl.ds(s, RHS, stride=SLABS), :] = res
-            halves.append(res.astype(bf16))
+            slabs.append(res.astype(bf16))
             w = res / diag
             hi, lo = split(w)
             at = slice(h * CZ, (h + 1) * CZ)
-            w0[p, :, at] = w
-            wh[p, :, at] = hi
-            wl[p, :, at] = lo
-        return seps + nt(jnp.concatenate(halves, axis=1), oh[p])
-
-    seps = lax.fori_loop(0, PAIRS, residual_of, jnp.zeros((RHS, wide), f32))
+            w0[q, :, at] = w
+            wh[q, :, at] = hi
+            wl[q, :, at] = lo
+        return seps + nt(jnp.concatenate(slabs, axis=1), oh[q])
+
+    seps = lax.fori_loop(0, QUADS, residual_of, jnp.zeros((RHS, wide), f32))
     put_res = pltpu.make_async_copy(r_v, res_o, loc_sem.at[9])
     put_res.start()
 
     sep_loc[...] = seps.astype(bf16).reshape(members, group, wide)
-    hop = share("member", lambda to: sep_loc.at[to], sep_hop.at[member])
+    hop = share("member", lambda to: sep_loc.at[to], sep_hop)
     sep_hop[member] = sep_loc[member]
-    gather_fw = share_matrix(1)
-    arrive(hop)
+    pl.when(split_early)(lambda: relayout(1))
+    hop.wait()
     mixed = sep_hop[0].astype(f32)
     for i in range(1, members):
         mixed = mixed + sep_hop[i].astype(f32)
     sep_all[slot] = mixed.astype(bf16)
-    hop = share("slot", lambda to: sep_all.at[slot], sep_all.at[slot])
-    gather_bw = share_matrix(2)
+    hop = share("slot", lambda to: sep_all.at[slot], sep_all)
+    pl.when(split_early)(lambda: relayout(2))
+    pl.when(use_low)(lambda: relay(low_stages[2], low_stages[3]))
     arrive(gather_base)
-    arrive(hop)
-
-    def row_of(ref):
-        return jnp.concatenate([ref[i] for i in range(slots)], axis=1)
-
-    base[...] = nt(row_of(sep_all), gath[0])
-
-    vecs = e_v.shape[0] // SLABS
-
-    def earlier_work():
-        get_e.wait()
-        eacc[...] = jnp.zeros(eacc.shape, f32)
-
-        def step(p, carry):
-            both = jnp.concatenate(
-                [slab(e_v, 2 * p, vecs), slab(e_v, 2 * p + 1, vecs)], axis=1
-            )
-            hi, lo = split(both)
-            vh[p] = hi
-            vl[p] = lo
-            right = jnp.concatenate([wh[p], wl[p], oh[p]], axis=0)
-            eacc[:vecs] += nt(hi, right)
-            eacc[vecs:] += nt(lo, right)
-            return carry
-
-        lax.fori_loop(0, PAIRS, step, 0)
+    hop.wait()
+
+    row8 = iota((8, LANES), 0)
+    base_loc[...] = nt(jnp.concatenate([sep_all[i] for i in range(slots)], axis=1), gath_in[...])
+    hop = share("gx", lambda to: base_loc, base_in)
+    base_in[a] = base_loc[...]
+    pl.when(split_early)(lambda: relayout(3))
+    hop.wait()
+    gx_here = jnp.zeros((8, LANES), jnp.int32) + a
+    for j in range(na):
+        both = base_in[j]
+        v = jnp.where(gx_here >= 2, both[8:], both[:8])
+        v = jnp.where(lax.rem(gx_here, 2) == 1, pltpu.roll(v, 4, 0), v)
+        base[:, j * wide : (j + 1) * wide] = jnp.where(row8 < 4, v, pltpu.roll(v, 4, 0))
+
+    eacc[...] = jnp.zeros(eacc.shape, f32)
+
+    def earlier_product(q, carry):
+        right = jnp.concatenate([wh[q], wl[q], oh[q]], axis=0)
+        eacc[:vecs] += nt(vh[q], right)
+        eacc[vecs:] += nt(vl[q], right)
+        return carry
+
+    def earlier_results():
         main = eacc[:vecs, :LANES] + eacc[vecs:, :LANES]
         main = main.T
         pacc[...] = main[:RHS] + main[RHS:]
         vsh[...] = eacc[:vecs, LANES:].T.astype(bf16)
         vsl[...] = eacc[vecs:, LANES:].T.astype(bf16)
 
+    turns = (QUADS * z) // (2 * (nz - 1) - z)
+
     def sweep_copies(first, dst, step):
-        copies = []
-        for d in range(slots):
-            to = lax.rem(slot + d, slots)
-            copies.append(
-                pltpu.make_async_remote_copy(
-                    src_ref=stateb.at[0 if step > 0 else 1], dst_ref=dst.at[slot],
-                    send_sem=send_sem.at[first + d], recv_sem=recv_sem.at[first + d],
-                    device_id=(to // 2, member * 2 + lax.rem(to, 2), z + step),
-                    device_id_type=pl.DeviceIdType.MESH,
-                )
+        return [
+            remote(
+                first + d, stateb.at[0 if step > 0 else 1], dst.at[core],
+                (a, member * 2 + lax.rem(core + d, 2), z + step),
             )
-        return copies
+            for d in range(2)
+        ]
 
     def sweep_push(first, dst, step):
+        v = state[...]
+        t = [v[:, j * wide : (j + 1) * wide] for j in range(na)]
+        packed = jnp.concatenate(
+            [jnp.where(row8 < 4, t[0], t[1]), jnp.where(row8 < 4, t[2], t[3])], axis=0
+        )
+        stateb[0 if step > 0 else 1] = packed.astype(bf16)
         for copy in sweep_copies(first, dst, step):
             copy.start()
 
-    pl.when(z >= early)(earlier_work)
+    row_group = iota((16, LANES), 0) // 4
+
+    def product_of(first, dst, step):
+        arrive(sweep_copies(first, dst, step))
+        left = []
+        for i in range(2):
+            v = dst[i].astype(f32)
+            left += [jnp.where(row_group == j, v, 0.0).astype(bf16) for j in range(na)]
+        out = nn(jnp.concatenate(left, axis=1), gath_t[...])
+        out = out[:8] + out[8:]
+        return out + pltpu.roll(out, 4, 0)
+
+    def transpose_matrix(m):
+        def step(t, carry):
+            at = rows_at(t * LANES, LANES)
+            block = gath[m, :, :, :, at].reshape(half, LANES)
+            gath_t[at, :] = block.astype(f32).T.astype(bf16)
+            return carry
+
+        lax.fori_loop(0, depth // LANES, step, 0)
 
     fw_first = count[0]
-    bw_first = fw_first + slots
-    count[0] = bw_first + slots
-    arrive(gather_fw)
+    bw_first = fw_first + 2
+    count[0] = bw_first + 2
+
+    @pl.when(up_before)
+    def _():
+        launch(up_stages[0])
+        relay(up_stages[0], up_stages[1])
+        arrive(up_stages[1])
+        launch(up_stages[2])
+
+    @pl.when(use_low)
+    def _():
+        arrive(low_stages[3])
+        transpose_matrix(0)
+
+    lax.fori_loop(0, turns, earlier_product, 0)
+    pl.when(z == nz - 1)(earlier_results)
+    pl.when(up_before)(lambda: relay(up_stages[2], up_stages[3]))
 
     @pl.when(z == 0)
     def _():
@@ -388,49 +534,74 @@
 
     @pl.when(z > 0)
     def _():
-        gath_t[...] = gath[1].astype(f32).T.astype(bf16)
-        arrive(sweep_copies(fw_first, fw_in, 1))
-        state[...] = base[...] - nn(row_of(fw_in), gath_t[...])
+        state[...] = base[...] - product_of(fw_first, fw_in, 1)
 
     @pl.when(z < nz - 1)
     def _():
-        stateb[0] = state[...].astype(bf16)
         sweep_push(fw_first, fw_in, 1)
 
-    pl.when(z < early)(earlier_work)
-    arrive(gather_bw)
+    pl.when(up_after)(lambda: launch(up_stages[0]))
+
+    @pl.when(jnp.logical_not(split_early))
+    def _():
+        for c in range(4):
+            relayout(c)
+
+    half_way = (turns + QUADS) // 2
+    lax.fori_loop(turns, half_way, earlier_product, 0)
+
+    @pl.when(up_after)
+    def _():
+        relay(up_stages[0], up_stages[1])
+        arrive(up_stages[1])
+        launch(up_stages[2])
+
+    lax.fori_loop(half_way, QUADS, earlier_product, 0)
+    pl.when(z < nz - 1)(earlier_results)
+    pl.when(up_after)(lambda: relay(up_stages[2], up_stages[3]))
 
     @pl.when(z < nz - 1)
     def _():
-        gath_t[...] = gath[2].astype(f32).T.astype(bf16)
-        arrive(sweep_copies(bw_first, bw_in, -1))
-        state[...] = state[...] - nn(row_of(bw_in), gath_t[...])
+        arrive(up_stages[3])
+        transpose_matrix(1)
+        state[...] = state[...] - product_of(bw_first, bw_in, -1)
 
     @pl.when(z > 0)
     def _():
-        stateb[1] = state[...].astype(bf16)
         sweep_push(bw_first, bw_in, -1)
 
-    hop = share("member", lambda to: state, ret.at[member])
-    ret[member] = state[...]
-    arrive(hop)
-    sol_h, sol_l = split(ret[...].reshape(RHS, wide))
+    for j in range(na):
+        tiles[j] = state[:, j * wide : (j + 1) * wide]
+    here = member * na + a
+    pairs = []
+    for d in range(na):
+        for e in range(members):
+            if d or e:
+                to, far = lax.rem(a + d, na), lax.rem(member + e, members)
+                pairs.append((tiles.at[to], ret.at[here], (to, far * 2 + core, z)))
+    hop = exchange(pairs, ret)
+    ret[here] = tiles[a]
+    hop.wait()
+    sol = jnp.concatenate(
+        [jnp.where(row8 < 4, ret[2 * i], ret[2 * i + 1]) for i in range(na * members // 2)], axis=0
+    )
+    sol_h, sol_l = split(sol)
     corr = nn(jnp.concatenate([sol_h, sol_l], axis=0), vsh[...])
     corr = pacc[...] + corr[:RHS] + corr[RHS:] + nn(sol_h, vsl[...])
     cols = vecs
 
     part_rows = RHS // na
     psend[...] = corr.reshape(na, part_rows, cols)
-    hop = share("gx", lambda to: psend.at[to], pin1.at[a])
+    hop = share("gx", lambda to: psend.at[to], pin1)
     pin1[a] = psend[a]
 
     sol_hl = jnp.concatenate([sol_h, sol_l], axis=1)
 
-    def add_sol(p, carry):
-        w0[p] = w0[p] + nn(sol_hl, jnp.concatenate([oh[p], oh[p]], axis=0))
+    def add_sol(q, carry):
+        w0[q] = w0[q] + nn(sol_hl, jnp.concatenate([oh[q], oh[q]], axis=0))
         return carry
 
-    lax.fori_loop(0, PAIRS, add_sol, 0, unroll=2)
+    lax.fori_loop(0, QUADS, add_sol, 0)
 
     def total_of(ref, n):
         out = ref[0]
@@ -438,7 +609,7 @@
             out = out + ref[i]
         return out
 
-    arrive(hop)
+    hop.wait()
     part = total_of(pin1, na)
     ph = part_rows // 8
     pw = nb // ph
@@ -446,17 +617,17 @@
     for i in range(nb):
         r, c = divmod(i, pw)
         psum1[i] = part[r * 8 : r * 8 + 8, c * width : (c + 1) * width]
-    hop = share("gy", lambda to: psum1.at[to], pin2.at[b])
+    hop = share("gy", lambda to: psum1.at[to], pin2)
     pin2[b] = psum1[b]
-    arrive(hop)
+    hop.wait()
     pin3[z] = total_of(pin2, nb)
-    arrive(share("gz", lambda to: pin3.at[z], pin3.at[z]))
+    share("gz", lambda to: pin3.at[z], pin3).wait()
     pin4[b] = total_of(pin3, nz)
-    arrive(share("gy", lambda to: pin4.at[b], pin4.at[b]))
+    share("gy", lambda to: pin4.at[b], pin4).wait()
     pin5[a] = jnp.concatenate(
         [jnp.concatenate([pin4[r * pw + c] for c in range(pw)], axis=1) for r in range(ph)], axis=0
     )
-    arrive(share("gx", lambda to: pin5.at[a], pin5.at[a]))
+    share("gx", lambda to: pin5.at[a], pin5).wait()
     full = pin5[...].reshape(RHS, cols)
     pin5_put = pltpu.make_async_copy(pin5, proj_o, loc_sem.at[10])
     pin5_put.start()
@@ -464,35 +635,47 @@
     pt_hl[:RHS] = hi
     pt_hl[RHS:] = lo
 
-    def project(p, gram):
-        main = nn(pt_hl[...], vh[p])
-        o = w0[p] - (main[:RHS] + main[RHS:] + nn(pt_hl[:RHS], vl[p]))
+    def project(q, gram):
+        main = nn(pt_hl[...], vh[q])
+        o = w0[q] - (main[:RHS] + main[RHS:] + nn(pt_hl[:RHS], vl[q]))
         hi, lo = split(o)
         both = jnp.concatenate([hi, lo], axis=0)
-        orth[p] = both
+        orth[q] = both
         return gram + nt(both, both)
 
-    gram = lax.fori_loop(0, PAIRS, project, jnp.zeros((2 * RHS, 2 * RHS), f32), unroll=2)
+    gram = lax.fori_loop(0, QUADS, project, jnp.zeros((2 * RHS, 2 * RHS), f32))
     gram = gram[:RHS] + gram[RHS:]
     gram = gram + pltpu.roll(gram, RHS, 1)
     put_orth = pltpu.make_async_copy(orth, orth_o, loc_sem.at[11])
     put_orth.start()
     piece = RHS // nz
     g_loc[...] = gram.reshape(nz, piece, LANES)
-    hop = share("gz", lambda to: g_loc.at[to], gin1.at[z])
+    hop = share("gz", lambda to: g_loc.at[to], gin1)
     gin1[z] = g_loc[z]
-    arrive(hop)
+    hop.wait()
     gin2[b] = total_of(gin1, nz)
-    arrive(share("gy", lambda to: gin2.at[b], gin2.at[b]))
+    share("gy", lambda to: gin2.at[b], gin2).wait()
     gin3[a] = total_of(gin2, nb)
-    arrive(share("gx", lambda to: gin3.at[a], gin3.at[a]))
+    share("gx", lambda to: gin3.at[a], gin3).wait()
     gin4[z] = total_of(gin3, na)
-    arrive(share("gz", lambda to: gin4.at[z], gin4.at[z]))
+    share("gz", lambda to: gin4.at[z], gin4).wait()
 
     put_gram = pltpu.make_async_copy(gin4, gram_o, loc_sem.at[12])
     put_gram.start()
-    for copy in sent:
-        copy.wait_send()
+    for wait in sent:
+        wait()
+
+    @pl.when(use_low)
+    def _():
+        for stage in low_stages:
+            for copy in stage:
+                copy.wait_send()
+
+    @pl.when(use_up)
+    def _():
+        for stage in up_stages:
+            for copy in stage:
+                copy.wait_send()
 
     @pl.when(z < nz - 1)
     def _():
@@ -533,14 +716,14 @@
         onward.start()
     get.wait()
 
-    def finish(p, carry):
-        hi, lo = orth[p, :RHS], orth[p, RHS:]
+    def finish(q, carry):
+        hi, lo = orth[q, :RHS], orth[q, RHS:]
         out = nn(lhs, jnp.concatenate([hi, hi, lo, lo], axis=0))
-        for h in range(2):
-            new_v[pl.ds(2 * p + h, RHS, stride=SLABS), :] = out[:, h * CZ : (h + 1) * CZ]
+        for h in range(4):
+            new_v[pl.ds(4 * q + h, RHS, stride=SLABS), :] = out[:, h * CZ : (h + 1) * CZ]
         return carry
 
-    lax.fori_loop(0, PAIRS, finish, 0, unroll=2)
+    lax.fori_loop(0, QUADS, finish, 0)
     put_new = pltpu.make_async_copy(new_v, new_o, sem.at[5])
     put_new.start()
     upper = jnp.concatenate([upper, jnp.zeros((LANES - RHS, LANES), f32)], axis=0)
@@ -556,7 +739,7 @@
     na, nb, nz = (lax.axis_size(n) for n in ("gx", "gy", "gz"))
     members, slots = nb // 2, na * 2
     group, wide = RHS // members, SEP * members
-    depth = slots * wide
+    depth, half = slots * wide, na * wide
     part_rows = RHS // na
     vecs = earlier_blocks.shape[0] * earlier_blocks.shape[1]
     pw = nb // (part_rows // 8)
@@ -577,14 +760,15 @@
         vmem((2, CX, RHS, CZ), bf16),
         vmem((2, 16, LANES), bf16),
         vmem((32, LANES), bf16),
-        vmem((PAIRS, wide, 2 * CZ), bf16),
-        vmem((3, wide, depth), bf16),
-        vmem((depth, wide), bf16),
-        vmem((PAIRS, RHS, 2 * CZ), f32),
-        vmem((PAIRS, RHS, 2 * CZ), bf16),
-        vmem((PAIRS, RHS, 2 * CZ), bf16),
-        vmem((PAIRS, vecs, 2 * CZ), bf16),
-        vmem((PAIRS, vecs, 2 * CZ), bf16),
+        vmem((QUADS, wide, 4 * CZ), bf16),
+        vmem((2, na, members, SEP, depth), bf16),
+        vmem((wide, depth), bf16),
+        vmem((depth, half), bf16),
+        vmem((QUADS, RHS, 4 * CZ), f32),
+        vmem((QUADS, RHS, 4 * CZ), bf16),
+        vmem((QUADS, RHS, 4 * CZ), bf16),
+        vmem((QUADS, vecs, 4 * CZ), bf16),
+        vmem((QUADS, vecs, 4 * CZ), bf16),
         vmem((2 * vecs, 2 * LANES), f32),
         vmem((RHS, vecs), f32),
         vmem((wide, vecs), bf16),
@@ -593,11 +777,14 @@
         vmem((members, group, wide), bf16),
         vmem((slots, group, wide), bf16),
         vmem((group, wide), f32),
-        vmem((group, wide), f32),
-        vmem((2, group, wide), bf16),
-        vmem((slots, group, wide), bf16),
-        vmem((slots, group, wide), bf16),
-        vmem((members, group, wide), f32),
+        vmem((na, group, wide), f32),
+        vmem((8, half), f32),
+        vmem((8, half), f32),
+        vmem((2, 16, wide), bf16),
+        vmem((na, 8, wide), f32),
+        vmem((2, 16, wide), bf16),
+        vmem((2, 16, wide), bf16),
+        vmem((na * members, 8, wide), f32),
         vmem((na, part_rows, vecs), f32),
         vmem((na, part_rows, vecs), f32),
         vmem((nb, 8, width), f32),
@@ -606,24 +793,24 @@
         vmem((nb, 8, width), f32),
         vmem((na, part_rows, vecs), f32),
         vmem((2 * RHS, vecs), bf16),
-        vmem((PAIRS, 2 * RHS, 2 * CZ), bf16),
+        vmem((QUADS, 2 * RHS, 4 * CZ), bf16),
         vmem((nz, piece, LANES), f32),
         vmem((nz, piece, LANES), f32),
         vmem((nb, piece, LANES), f32),
         vmem((na, piece, LANES), f32),
         vmem((nz, piece, LANES), f32),
-        pltpu.SemaphoreType.DMA((13,)),
-        pltpu.SemaphoreType.DMA((128,)),
-        pltpu.SemaphoreType.DMA((128,)),
+        pltpu.SemaphoreType.DMA((16,)),
+        pltpu.SemaphoreType.DMA((144,)),
+        pltpu.SemaphoreType.DMA((144,)),
     ]
     flat = lambda v: v.reshape(-1, CZ)
     anywhere = pl.BlockSpec(memory_space=pl.ANY)
     in_vmem = pl.BlockSpec(memory_space=pltpu.VMEM)
     res, orth, projection, gram = pl.pallas_call(
-        functools.partial(kernel, na, nb, nz, (nz * 5) // 8),
+        functools.partial(kernel, na, nb, nz),
         out_shape=(
             jax.ShapeDtypeStruct((ROWS, CZ), f32),
-            jax.ShapeDtypeStruct((PAIRS, 2 * RHS, 2 * CZ), bf16),
+            jax.ShapeDtypeStruct((QUADS, 2 * RHS, 4 * CZ), bf16),
             jax.ShapeDtypeStruct((na, part_rows, vecs), f32),
             jax.ShapeDtypeStruct((nz, piece, LANES), f32),
         ),
@@ -652,7 +839,7 @@
         in_specs=[in_vmem, anywhere, anywhere, anywhere],
         out_specs=(anywhere, anywhere, anywhere, in_vmem),
         scratch_shapes=[
-            vmem((PAIRS, 2 * RHS, 2 * CZ), bf16),
+            vmem((QUADS, 2 * RHS, 4 * CZ), bf16),
             vmem((RHS, LANES), f32),
             vmem((ROWS, CZ), f32),
             vmem((ROWS, CZ), f32),

time: 139 us -> 127 us (0.914)
  Pallas kernels: 138 us -> 126 us
    pallas_call x1, Pallas kernels: 130 us -> 119 us  [body(): pl.pallas_call(functools.partial(kernel, na, nb, nz), out_shape=(jax.Shap...]
where the time goes in v3:
time: 127 us
  Pallas kernels  126 us (99%)
    pallas_call x1, Pallas kernels, body(): pl.pallas_call(functools.partial(kernel, na, nb, nz), out_shape=(jax.Shap...  119 us
    pallas_call x1, Pallas kernels, body(): pl.pallas_call(functools.partial(finish_kernel, math.sqrt(na * nb * nz *...  7.66 us

profile of v3, /device:TPU:1, one launch (start us, length us, event | category | flops | bytes accessed | tf_op | source)
XLA Modules:
  0.0 127.1 jit_solution(9050525136659752931)
XLA Ops:
  0.6 118.8 %step.1 = (f32[2048,128]{1,0:T(8,128)}, bf16[8,128,512]{2,1,0:T(8,128)(2,1)}, f32[4,16,512]{2,1,0:T(8,128)}, f32[8,8,128]{2,1,0:T(8,128)}) custom-call(f32[2048,128]{1,0:T(8,128)} %bitcast.14, f32[2048,128]{1,0:T(8,128)} %bitcast.15, f32[32,128]{1,0:T(8,128)} %bitcast.22, f32[96,128]{1,0:T(8,128)} %bitcast.20, f32[16384,128]{1,0:T(8,128)} %bitcast.13, ...), custom_call_target="tpu_custom_call" | custom-call | flops 2000000000 | bytes 13631488 | tf_op jit(solution)/shard_map/step/pallas_call | solution.py:809
  119.4 7.7 %finish.1 = (f32[2048,128]{1,0:T(8,128)}, f32[2048,128]{1,0:T(8,128)}, f32[64,512]{1,0:T(8,128)}, f32[64,64]{1,0:T(8,128)}) custom-call(f32[64,128]{1,0:T(8,128)} %bitcast.21, bf16[8,128,512]{2,1,0:T(8,128)(2,1)} %get-tuple-element.13.orth_h, f32[2048,128]{1,0:T(8,128)} %get-tuple-element.14.res_h, f32[64,512]{1,0:T(8,128)} %bitcast.16), custom_call_target="tpu_custom_call" | custom-call | flops 200000000 | bytes 5242880 | tf_op jit(solution)/shard_map/finish/pallas_call | solution.py:831

commit v4 on v3

--- a/solution.py
+++ b/solution.py
@@ -89,7 +89,7 @@
     x_h, r_h, d_h, v_h, e_h, c_h, li_h, lo_h, up_h,
     res_o, orth_o, proj_o, gram_o,
     x_v, r_v, d_v, v_v, e_v, c_v, m_v,
-    xp, xsb, hx, hy, hz, zsend, oh, gath, gath_in, gath_t,
+    xp, xsb, hx, hy, hz, zsend, z_ends, res_b, oh, gath, gath_in, gath_t,
     w0, wh, wl, vh, vl, eacc, pacc, vsh, vsl,
     sep_loc, sep_hop, sep_all, base_loc, base_in, base, state, stateb, tiles, fw_in, bw_in, ret,
     psend, pin1, psum1, pin2, pin3, pin4, pin5, pt_hl,
@@ -178,7 +178,8 @@
         copy.start()
         return copy
 
-    get_x = fetch(0, x_h, x_v)
+    x_order = (0, CX - 1) + tuple(range(1, CX - 1))
+    get_x = {cx: fetch((0, 16, 17, 18)[cx], x_h.at[:, cx], x_v.at[cx]) for cx in x_order}
     get_m = [fetch(1 + i, h, m_v.at[i]) for i, h in enumerate((li_h, lo_h, up_h))]
     get_c = fetch(4, c_h, c_v)
     get_d = fetch(5, d_h, d_v)
@@ -196,40 +197,41 @@
     def rows_at(start, n):
         return pl.ds(pl.multiple_of(start, n), n)
 
-    get_x.wait()
     pad = CY + 2
-
-    def spread_x(cx, carry):
+    q32, lane_all = iota((32, PAIRS * LANES), 0), iota((32, PAIRS * LANES), 1)
+    turn_all, l_all = lane_all // LANES, lax.rem(lane_all, LANES)
+    pick = ((q32 == turn_all) & (l_all == CZ - 1)) | ((q32 == 16 + turn_all) & (l_all == 0))
+    pick = pick.astype(bf16)
+
+    def spread_x(cx):
+        get_x[cx].wait()
+        rows = x_v.at[cx].reshape(RHS * CY, CZ)
         for cy in range(CY):
-            v = slab(x_v, cx * CY + cy)
+            v = rows[pl.ds(cy, RHS, stride=CY), :]
             xp[(cx + 1) * pad + cy + 1] = v
             xsb[cx, cy * RHS : (cy + 1) * RHS, :] = v.astype(bf16)
-        return carry
-
-    lax.fori_loop(0, CX, spread_x, 0)
-    pl.semaphore_wait(barrier, partners)
 
     def ring(axis, step):
         n = size[axis]
         return place(axis, lax.rem(pos_of[axis] + step + n, n))
 
+    spread_x(x_order[0])
+    spread_x(x_order[1])
+    pl.semaphore_wait(barrier, partners)
     halo = [
         send(xsb.at[CX - 1], hx.at[0], ring("gx", 1)),
         send(xsb.at[0], hx.at[1], ring("gx", -1)),
+    ]
+    for cx in x_order[2:]:
+        spread_x(cx)
+    halo += [
         send(xsb.at[:, pl.ds((CY - 1) * RHS, RHS)], hy.at[0], ring("gy", 1)),
         send(xsb.at[:, pl.ds(0, RHS)], hy.at[1], ring("gy", -1)),
     ]
-    q32, l32 = iota((32, LANES), 0), iota((32, LANES), 1)
-
-    def pick_edge(p, edge):
-        pick = ((q32 == p) & (l32 == CZ - 1)) | ((q32 == 16 + p) & (l32 == 0))
-        rows = xsb[p // 4, rows_at(lax.rem(p, 4) * 128, 128), :]
-        return edge + nt(pick.astype(bf16), rows)
-
-    zsend[...] = lax.fori_loop(
-        0, PAIRS, pick_edge, jnp.zeros((32, LANES), f32), unroll=4
-    ).astype(bf16)
-
+    rows = jnp.concatenate(
+        [xsb[p // 4, (p % 4) * LANES : (p % 4 + 1) * LANES, :] for p in range(PAIRS)], axis=1
+    )
+    zsend[...] = nt(pick, rows).astype(bf16)
     halo += [
         send(zsend.at[pl.ds(0, 16)], hz.at[0], ring("gz", 1)),
         send(zsend.at[pl.ds(16, 16)], hz.at[1], ring("gz", -1)),
@@ -387,22 +389,20 @@
     for k, mask in enumerate((flag(b > 0), flag(b < nb - 1))):
         for cx in range(CX):
             xp[(cx + 1) * pad + k * (CY + 1)] = hy[k, cx].astype(f32) * mask
-    q128, l128 = iota((LANES, LANES), 0), iota((LANES, LANES), 1)
+    q128, lane_all = iota((LANES, PAIRS * LANES), 0), iota((LANES, PAIRS * LANES), 1)
+    turn_all, l_all = lane_all // LANES, lax.rem(lane_all, LANES)
+    spread = ((q128 == turn_all) & (l_all == 0)) | ((q128 == 16 + turn_all) & (l_all == CZ - 1))
+    z_ends[...] = nn(ends, spread.astype(bf16))
     lane64 = iota((RHS, LANES), 1)
 
-    def residual_of(q, seps):
-        slabs = []
+    def residual_of(q, carry):
         for h in range(4):
             s = 4 * q + h
-            if h % 2 == 0:
-                p = 2 * q + h // 2
-                spread = ((q128 == p) & (l128 == 0)) | ((q128 == 16 + p) & (l128 == CZ - 1))
-                z_ends = nn(ends, spread.astype(bf16))
             i = (q // 2 + 1) * pad + lax.rem(q, 2) * 4 + h + 1
             x = xp[i]
             diag = 6.0 + d_v[pl.ds(s, 1), :]
             v0, v1, v2 = (v_v[pl.ds(k * SLABS + s, 1), :] for k in range(3))
-            end = z_ends[(h % 2) * RHS : (h % 2 + 1) * RHS, :]
+            end = z_ends[(h % 2) * RHS : (h % 2 + 1) * RHS, rows_at((2 * q + h // 2) * LANES, LANES)]
             before = jnp.where(lane64 == 0, end, pltpu.roll(x, 1, 1))
             after = jnp.where(lane64 == CZ - 1, end, pltpu.roll(x, CZ - 1, 1))
             res = slab(r_v, s) - diag * x
@@ -410,16 +410,20 @@
             res = res + (1.0 + v1) * xp[i - 1] + (1.0 - v1) * xp[i + 1]
             res = res + (1.0 + v2) * before + (1.0 - v2) * after
             r_v[pl.ds(s, RHS, stride=SLABS), :] = res
-            slabs.append(res.astype(bf16))
-            w = res / diag
+            at = slice(h * CZ, (h + 1) * CZ)
+            res_b[q, :, at] = res.astype(bf16)
+            w = res * (1.0 / diag)
             hi, lo = split(w)
-            at = slice(h * CZ, (h + 1) * CZ)
             w0[q, :, at] = w
             wh[q, :, at] = hi
             wl[q, :, at] = lo
-        return seps + nt(jnp.concatenate(slabs, axis=1), oh[q])
-
-    seps = lax.fori_loop(0, QUADS, residual_of, jnp.zeros((RHS, wide), f32))
+        return carry
+
+    lax.fori_loop(0, QUADS, residual_of, 0)
+    seps = nt(
+        jnp.concatenate([res_b[q] for q in range(QUADS)], axis=1),
+        jnp.concatenate([oh[q] for q in range(QUADS)], axis=1),
+    )
     put_res = pltpu.make_async_copy(r_v, res_o, loc_sem.at[9])
     put_res.start()
 
@@ -597,11 +601,13 @@
 
     sol_hl = jnp.concatenate([sol_h, sol_l], axis=1)
 
-    def add_sol(q, carry):
-        w0[q] = w0[q] + nn(sol_hl, jnp.concatenate([oh[q], oh[q]], axis=0))
-        return carry
-
-    lax.fori_loop(0, QUADS, add_sol, 0)
+    def add_sol(first):
+        twice = jnp.concatenate([oh[first], oh[first + 1]], axis=1)
+        change = nn(sol_hl, jnp.concatenate([twice, twice], axis=0))
+        w0[first] = w0[first] + change[:, : 4 * CZ]
+        w0[first + 1] = w0[first + 1] + change[:, 4 * CZ :]
+
+    add_sol(0)
 
     def total_of(ref, n):
         out = ref[0]
@@ -619,15 +625,20 @@
         psum1[i] = part[r * 8 : r * 8 + 8, c * width : (c + 1) * width]
     hop = share("gy", lambda to: psum1.at[to], pin2)
     pin2[b] = psum1[b]
+    add_sol(2)
     hop.wait()
     pin3[z] = total_of(pin2, nb)
     share("gz", lambda to: pin3.at[z], pin3).wait()
     pin4[b] = total_of(pin3, nz)
-    share("gy", lambda to: pin4.at[b], pin4).wait()
+    hop = share("gy", lambda to: pin4.at[b], pin4)
+    add_sol(4)
+    hop.wait()
     pin5[a] = jnp.concatenate(
         [jnp.concatenate([pin4[r * pw + c] for c in range(pw)], axis=1) for r in range(ph)], axis=0
     )
-    share("gx", lambda to: pin5.at[a], pin5).wait()
+    hop = share("gx", lambda to: pin5.at[a], pin5)
+    add_sol(6)
+    hop.wait()
     full = pin5[...].reshape(RHS, cols)
     pin5_put = pltpu.make_async_copy(pin5, proj_o, loc_sem.at[10])
     pin5_put.start()
@@ -635,15 +646,17 @@
     pt_hl[:RHS] = hi
     pt_hl[RHS:] = lo
 
-    def project(q, gram):
-        main = nn(pt_hl[...], vh[q])
-        o = w0[q] - (main[:RHS] + main[RHS:] + nn(pt_hl[:RHS], vl[q]))
-        hi, lo = split(o)
-        both = jnp.concatenate([hi, lo], axis=0)
-        orth[q] = both
-        return gram + nt(both, both)
-
-    gram = lax.fori_loop(0, QUADS, project, jnp.zeros((2 * RHS, 2 * RHS), f32))
+    def project(i, gram):
+        for q in (2 * i, 2 * i + 1):
+            main = nn(pt_hl[...], vh[q])
+            o = w0[q] - (main[:RHS] + main[RHS:] + nn(pt_hl[:RHS], vl[q]))
+            hi, lo = split(o)
+            both = jnp.concatenate([hi, lo], axis=0)
+            orth[q] = both
+            gram = gram + nt(both, both)
+        return gram
+
+    gram = lax.fori_loop(0, QUADS // 2, project, jnp.zeros((2 * RHS, 2 * RHS), f32))
     gram = gram[:RHS] + gram[RHS:]
     gram = gram + pltpu.roll(gram, RHS, 1)
     put_orth = pltpu.make_async_copy(orth, orth_o, loc_sem.at[11])
@@ -652,6 +665,32 @@
     g_loc[...] = gram.reshape(nz, piece, LANES)
     hop = share("gz", lambda to: g_loc.at[to], gin1)
     gin1[z] = g_loc[z]
+    for wait in sent[:-1]:
+        wait()
+    del sent[:-1]
+
+    @pl.when(use_low)
+    def _():
+        for stage in low_stages:
+            for copy in stage:
+                copy.wait_send()
+
+    @pl.when(use_up)
+    def _():
+        for stage in up_stages:
+            for copy in stage:
+                copy.wait_send()
+
+    @pl.when(z < nz - 1)
+    def _():
+        for copy in sweep_copies(fw_first, fw_in, 1):
+            copy.wait_send()
+
+    @pl.when(z > 0)
+    def _():
+        for copy in sweep_copies(bw_first, bw_in, -1):
+            copy.wait_send()
+
     hop.wait()
     gin2[b] = total_of(gin1, nz)
     share("gy", lambda to: gin2.at[b], gin2).wait()
@@ -664,29 +703,6 @@
     put_gram.start()
     for wait in sent:
         wait()
-
-    @pl.when(use_low)
-    def _():
-        for stage in low_stages:
-            for copy in stage:
-                copy.wait_send()
-
-    @pl.when(use_up)
-    def _():
-        for stage in up_stages:
-            for copy in stage:
-                copy.wait_send()
-
-    @pl.when(z < nz - 1)
-    def _():
-        for copy in sweep_copies(fw_first, fw_in, 1):
-            copy.wait_send()
-
-    @pl.when(z > 0)
-    def _():
-        for copy in sweep_copies(bw_first, bw_in, -1):
-            copy.wait_send()
-
     for put in (put_res, pin5_put, put_orth, put_gram):
         put.wait()
 
@@ -723,7 +739,7 @@
             new_v[pl.ds(4 * q + h, RHS, stride=SLABS), :] = out[:, h * CZ : (h + 1) * CZ]
         return carry
 
-    lax.fori_loop(0, QUADS, finish, 0)
+    lax.fori_loop(0, QUADS, finish, 0, unroll=4)
     put_new = pltpu.make_async_copy(new_v, new_o, sem.at[5])
     put_new.start()
     upper = jnp.concatenate([upper, jnp.zeros((LANES - RHS, LANES), f32)], axis=0)
@@ -747,7 +763,7 @@
     piece = RHS // nz
     vmem = pltpu.VMEM
     scratch = [
-        vmem((ROWS, CZ), f32),
+        vmem((CX, RHS, CY, CZ), f32),
         vmem((ROWS, CZ), f32),
         vmem((SLABS, CZ), f32),
         vmem((3 * SLABS, CZ), f32),
@@ -760,6 +776,8 @@
         vmem((2, CX, RHS, CZ), bf16),
         vmem((2, 16, LANES), bf16),
         vmem((32, LANES), bf16),
+        vmem((LANES, PAIRS * LANES), f32),
+        vmem((QUADS, RHS, 4 * CZ), bf16),
         vmem((QUADS, wide, 4 * CZ), bf16),
         vmem((2, na, members, SEP, depth), bf16),
         vmem((wide, depth), bf16),
@@ -799,7 +817,7 @@
         vmem((nb, piece, LANES), f32),
         vmem((na, piece, LANES), f32),
         vmem((nz, piece, LANES), f32),
-        pltpu.SemaphoreType.DMA((16,)),
+        pltpu.SemaphoreType.DMA((19,)),
         pltpu.SemaphoreType.DMA((144,)),
         pltpu.SemaphoreType.DMA((144,)),
     ]
@@ -825,7 +843,7 @@
         ),
         name="step",
     )(
-        flat(x_field), flat(right_side), flat(diag_shift), flat(velocity), flat(earlier_blocks),
+        x_field, flat(right_side), flat(diag_shift), flat(velocity), flat(earlier_blocks),
         sep_cells, low_inv[0], low_off[0], up_off[0],
     )
     res, new, projection, factor = pl.pallas_call(

time: 127 us -> 126 us (level)
  no operation moved by 1% of the time
where the time goes in v4:
time: 126 us; the launch traced here: 125 us
  Pallas kernels  125 us (99%)
    pallas_call x1, Pallas kernels, body(): pl.pallas_call(functools.partial(kernel, na, nb, nz), out_shape=(jax.Shap...  118 us
    pallas_call x1, Pallas kernels, body(): pl.pallas_call(functools.partial(finish_kernel, math.sqrt(na * nb * nz *...  6.88 us

profile of v4, /device:TPU:1, one launch (start us, length us, event | category | flops | bytes accessed | tf_op | source)
XLA Modules:
  0.0 125.2 jit_solution(624728585518558704)
XLA Ops:
  0.6 117.7 %step.1 = (f32[2048,128]{1,0:T(8,128)}, bf16[8,128,512]{2,1,0:T(8,128)(2,1)}, f32[4,16,512]{2,1,0:T(8,128)}, f32[8,8,128]{2,1,0:T(8,128)}) custom-call(f32[64,4,8,128]{3,2,1,0:T(8,128)} %x_h.1, f32[2048,128]{1,0:T(8,128)} %bitcast.13, f32[32,128]{1,0:T(8,128)} %bitcast.20, f32[96,128]{1,0:T(8,128)} %bitcast.18, f32[16384,128]{1,0:T(8,128)} %bitcast.12, ...), custom_call_target="tpu_custom_call" | custom-call | flops 2000000000 | bytes 13631488 | tf_op jit(solution)/shard_map/step/pallas_call | solution.py:827
  118.3 6.9 %finish.1 = (f32[2048,128]{1,0:T(8,128)}, f32[2048,128]{1,0:T(8,128)}, f32[64,512]{1,0:T(8,128)}, f32[64,64]{1,0:T(8,128)}) custom-call(f32[64,128]{1,0:T(8,128)} %bitcast.19, bf16[8,128,512]{2,1,0:T(8,128)(2,1)} %get-tuple-element.13.orth_h, f32[2048,128]{1,0:T(8,128)} %get-tuple-element.14.res_h, f32[64,512]{1,0:T(8,128)} %bitcast.14), custom_call_target="tpu_custom_call" | custom-call | flops 200000000 | bytes 5242880 | tf_op jit(solution)/shard_map/finish/pallas_call | solution.py:849

commit v5 on v4

--- a/solution.py
+++ b/solution.py
@@ -89,11 +89,11 @@
     x_h, r_h, d_h, v_h, e_h, c_h, li_h, lo_h, up_h,
     res_o, orth_o, proj_o, gram_o,
     x_v, r_v, d_v, v_v, e_v, c_v, m_v,
-    xp, xsb, hx, hy, hz, zsend, z_ends, res_b, oh, gath, gath_in, gath_t,
-    w0, wh, wl, vh, vl, eacc, pacc, vsh, vsl,
-    sep_loc, sep_hop, sep_all, base_loc, base_in, base, state, stateb, tiles, fw_in, bw_in, ret,
-    psend, pin1, psum1, pin2, pin3, pin4, pin5, pt_hl,
-    orth, g_loc, gin1, gin2, gin3, gin4,
+    xp, xsb, hx, hy, hz, zsend, z_ends, res_b, oh, gath, gath_t,
+    w0, wh, wl, vh, vl, eacc,
+    sep_loc, sep_in, base, state, stateb, tiles, fw_in, bw_in, ret,
+    psend, pin, fin, full_in, pt_v, pt_hl,
+    orth, g_loc, gin1, gin2, gin3,
     loc_sem, send_sem, recv_sem,
 ):
     a, b, z = lax.axis_index("gx"), lax.axis_index("gy"), lax.axis_index("gz")
@@ -134,15 +134,29 @@
         sent.append(copy.wait_send)
         return copy
 
-    def exchange(pairs, dst):
+    def exchange_later(pairs, dst):
         n = count[0]
         count[0] += 1
-        for src, there, where in pairs:
-            remote(n, src, there, where).start()
+        copies = [remote(n, *pair) for pair in pairs]
         whole = dst.at[pl.ds(0, len(pairs))]
         out = pltpu.make_async_copy(whole, whole, send_sem.at[n])
         sent.append(out.wait)
-        return pltpu.make_async_copy(whole, whole, recv_sem.at[n])
+        return copies, pltpu.make_async_copy(whole, whole, recv_sem.at[n])
+
+    def exchange(pairs, dst):
+        copies, came = exchange_later(pairs, dst)
+        for copy in copies:
+            copy.start()
+        return came
+
+    def plane_pairs(src_of, there):
+        pairs = []
+        for d in range(na):
+            for e in range(members):
+                if d or e:
+                    to, far = lax.rem(a + d, na), lax.rem(member + e, members)
+                    pairs.append((src_of(to, far), there, (to, far * 2 + core, z)))
+        return pairs
 
     def share(axis, src_of, dst):
         n = size[axis]
@@ -167,11 +181,9 @@
             greet(place(axis, lax.rem(pos[axis] + d, size[axis])))
             partners += 1
     for d in range(1, na):
-        for e in range(members):
-            greet((lax.rem(a + d, na), lax.rem(member + e, members) * 2 + core, z))
+        for e in range(nb):
+            greet((lax.rem(a + d, na), lax.rem(b + e, nb), z))
             partners += 1
-        greet((lax.rem(a + d, na), member * 2 + 1 - core, z))
-        partners += 1
 
     def fetch(n, src, dst):
         copy = pltpu.make_async_copy(src, dst, loc_sem.at[n])
@@ -257,10 +269,7 @@
                     piece = pltpu.roll(piece, shift, 1)
                 out = jnp.where(lane_group == g, piece, out)
             at = slice(t * LANES, (t + 1) * LANES)
-            if i == 0:
-                gath_in[mine, at] = out.astype(bf16)
-            else:
-                gath[i - 1, a, member, :, at] = out.astype(bf16)
+            gath[(3, 0, 1)[i], a, member, :, at] = out.astype(bf16)
 
     for i in range(3):
         reorder(i)
@@ -321,15 +330,14 @@
             got.wait_recv()
             copy.start()
 
-    low_stages, up_stages = gather_stages(0), gather_stages(1)
+    low_stages, up_stages, cell_stages, base_stages = (gather_stages(m) for m in range(4))
     use_low, use_up = z > 0, z < nz - 1
+    early = z >= nz // 2
+    late = jnp.logical_not(early)
     up_after = z < (nz * 5) // 8
     up_before = jnp.logical_and(use_up, jnp.logical_not(up_after))
+    launch(base_stages[0])
     pl.when(use_low)(lambda: launch(low_stages[0]))
-    gather_base = [
-        send(gath_in.at[mine], gath_in.at[mine], place("member", lax.rem(member + d, members)))
-        for d in range(1, members)
-    ]
 
     get_c.wait()
     cells = jnp.broadcast_to(c_v[...], (SEP, SEP)).astype(f32)
@@ -368,8 +376,11 @@
     get_d.wait()
     get_v.wait()
     get_r.wait()
+    relay(base_stages[0], base_stages[1])
     pl.when(use_low)(lambda: relay(low_stages[0], low_stages[1]))
     arrive(halo)
+    arrive(base_stages[1])
+    launch(base_stages[2])
 
     @pl.when(use_low)
     def _():
@@ -428,29 +439,33 @@
     put_res.start()
 
     sep_loc[...] = seps.astype(bf16).reshape(members, group, wide)
-    hop = share("member", lambda to: sep_loc.at[to], sep_hop)
-    sep_hop[member] = sep_loc[member]
-    pl.when(split_early)(lambda: relayout(1))
+    me = slot * members + member
+    pairs = []
+    for d in range(na):
+        for e in range(nb):
+            if d or e:
+                to, far = lax.rem(a + d, na), lax.rem(b + e, nb)
+                pairs.append((sep_loc.at[far // 2], sep_in.at[me], (to, far, z)))
+    hop = exchange(pairs, sep_in)
+    sep_in[me] = sep_loc[member]
+    relay(base_stages[2], base_stages[3])
+    for c in (1, 2, 3):
+        pl.when(split_early)(functools.partial(relayout, c))
+    pl.when(use_low)(lambda: relay(low_stages[2], low_stages[3]))
     hop.wait()
-    mixed = sep_hop[0].astype(f32)
-    for i in range(1, members):
-        mixed = mixed + sep_hop[i].astype(f32)
-    sep_all[slot] = mixed.astype(bf16)
-    hop = share("slot", lambda to: sep_all.at[slot], sep_all)
-    pl.when(split_early)(lambda: relayout(2))
-    pl.when(use_low)(lambda: relay(low_stages[2], low_stages[3]))
-    arrive(gather_base)
-    hop.wait()
+    arrive(base_stages[3])
 
     row8 = iota((8, LANES), 0)
-    base_loc[...] = nt(jnp.concatenate([sep_all[i] for i in range(slots)], axis=1), gath_in[...])
-    hop = share("gx", lambda to: base_loc, base_in)
-    base_in[a] = base_loc[...]
-    pl.when(split_early)(lambda: relayout(3))
-    hop.wait()
+    left = []
+    for i in range(slots):
+        v = sep_in[i * members].astype(f32)
+        for e in range(1, members):
+            v = v + sep_in[i * members + e].astype(f32)
+        left.append(v.astype(bf16))
+    wide_base = nt(jnp.concatenate(left, axis=1), gath[3].reshape(half, depth))
     gx_here = jnp.zeros((8, LANES), jnp.int32) + a
     for j in range(na):
-        both = base_in[j]
+        both = wide_base[:, j * wide : (j + 1) * wide]
         v = jnp.where(gx_here >= 2, both[8:], both[:8])
         v = jnp.where(lax.rem(gx_here, 2) == 1, pltpu.roll(v, 4, 0), v)
         base[:, j * wide : (j + 1) * wide] = jnp.where(row8 < 4, v, pltpu.roll(v, 4, 0))
@@ -463,14 +478,36 @@
         eacc[vecs:] += nt(vl[q], right)
         return carry
 
+    here = member * na + a
+    fold = vecs // 2
+    rowf = iota((8, fold), 0)
+    plane_sum, plane_came = exchange_later(
+        plane_pairs(lambda to, far: psend.at[far * na + to], pin.at[here]), pin
+    )
+
     def earlier_results():
         main = eacc[:vecs, :LANES] + eacc[vecs:, :LANES]
         main = main.T
-        pacc[...] = main[:RHS] + main[RHS:]
-        vsh[...] = eacc[:vecs, LANES:].T.astype(bf16)
-        vsl[...] = eacc[vecs:, LANES:].T.astype(bf16)
-
-    turns = (QUADS * z) // (2 * (nz - 1) - z)
+        main = main[:RHS] + main[RHS:]
+        for i in range(RHS // 8):
+            one = main[8 * i : 8 * i + 8, :fold]
+            two = main[8 * i : 8 * i + 8, fold:]
+            psend[2 * i] = jnp.where(rowf < 4, one, pltpu.roll(two, 4, 0))
+            psend[2 * i + 1] = jnp.where(rowf < 4, pltpu.roll(one, 4, 0), two)
+        launch(plane_sum)
+        for i in range(2):
+            values = eacc[i * vecs : (i + 1) * vecs, LANES:].T
+            v = values[:SEP]
+            for e in range(1, members):
+                v = v + values[e * SEP : (e + 1) * SEP]
+            gath[2, a, member, :, i * vecs : (i + 1) * vecs] = v.astype(bf16)
+
+    def gather_cells():
+        launch(cell_stages[0])
+        relay(cell_stages[0], cell_stages[1])
+        arrive(cell_stages[1])
+        launch(cell_stages[2])
+        relay(cell_stages[2], cell_stages[3])
 
     def sweep_copies(first, dst, step):
         return [
@@ -516,22 +553,30 @@
     bw_first = fw_first + 2
     count[0] = bw_first + 2
 
+    def products(first, last):
+        lax.fori_loop(first, last, earlier_product, 0)
+
+    pl.when(up_before)(lambda: launch(up_stages[0]))
+    pl.when(early)(lambda: products(0, QUADS // 2))
+
     @pl.when(up_before)
     def _():
-        launch(up_stages[0])
         relay(up_stages[0], up_stages[1])
         arrive(up_stages[1])
         launch(up_stages[2])
 
+    @pl.when(early)
+    def _():
+        products(QUADS // 2, QUADS)
+        earlier_results()
+
+    pl.when(up_before)(lambda: relay(up_stages[2], up_stages[3]))
+
     @pl.when(use_low)
     def _():
         arrive(low_stages[3])
         transpose_matrix(0)
 
-    lax.fori_loop(0, turns, earlier_product, 0)
-    pl.when(z == nz - 1)(earlier_results)
-    pl.when(up_before)(lambda: relay(up_stages[2], up_stages[3]))
-
     @pl.when(z == 0)
     def _():
         state[...] = base[...]
@@ -543,6 +588,10 @@
     @pl.when(z < nz - 1)
     def _():
         sweep_push(fw_first, fw_in, 1)
+
+    @pl.when(z == nz - 1)
+    def _():
+        sweep_push(bw_first, bw_in, -1)
 
     pl.when(up_after)(lambda: launch(up_stages[0]))
 
@@ -551,8 +600,7 @@
         for c in range(4):
             relayout(c)
 
-    half_way = (turns + QUADS) // 2
-    lax.fori_loop(turns, half_way, earlier_product, 0)
+    pl.when(late)(lambda: products(0, QUADS // 2))
 
     @pl.when(up_after)
     def _():
@@ -560,9 +608,13 @@
         arrive(up_stages[1])
         launch(up_stages[2])
 
-    lax.fori_loop(half_way, QUADS, earlier_product, 0)
-    pl.when(z < nz - 1)(earlier_results)
+    @pl.when(late)
+    def _():
+        products(QUADS // 2, QUADS)
+        earlier_results()
+
     pl.when(up_after)(lambda: relay(up_stages[2], up_stages[3]))
+    pl.when(late)(gather_cells)
 
     @pl.when(z < nz - 1)
     def _():
@@ -570,35 +622,45 @@
         transpose_matrix(1)
         state[...] = state[...] - product_of(bw_first, bw_in, -1)
 
-    @pl.when(z > 0)
+    @pl.when(jnp.logical_and(z > 0, z < nz - 1))
     def _():
         sweep_push(bw_first, bw_in, -1)
 
     for j in range(na):
         tiles[j] = state[:, j * wide : (j + 1) * wide]
-    here = member * na + a
+    ret_came = exchange(plane_pairs(lambda to, far: tiles.at[to], ret.at[here]), ret)
+    ret[here] = tiles[a]
+    pl.when(early)(gather_cells)
+
+    def total_of(ref, n):
+        out = ref[0]
+        for i in range(1, n):
+            out = out + ref[i]
+        return out
+
+    pin[here] = psend[here]
+    plane_came.wait()
+    arrive(cell_stages[3])
+    sol_h, sol_l = split(state[...])
+    part = nn(jnp.concatenate([sol_h, sol_l], axis=0), gath[2].reshape(half, 2 * vecs))
+    part = part[:8, :vecs] + part[8:, :vecs] + part[:8, vecs:]
+    part = jnp.where(rowf < 4, part[:, :fold], part[:, fold:]) + total_of(pin, na * members)
+    where_fin = z * 2 + core
+    fin[where_fin] = part
     pairs = []
-    for d in range(na):
-        for e in range(members):
+    for d in range(nz):
+        for e in range(2):
             if d or e:
-                to, far = lax.rem(a + d, na), lax.rem(member + e, members)
-                pairs.append((tiles.at[to], ret.at[here], (to, far * 2 + core, z)))
-    hop = exchange(pairs, ret)
-    ret[here] = tiles[a]
-    hop.wait()
+                to, kind = lax.rem(z + d, nz), lax.rem(core + e, 2)
+                mine_there = fin.at[where_fin]
+                pairs.append((mine_there, mine_there, (a, member * 2 + kind, to)))
+    hop = exchange(pairs, fin)
+
+    ret_came.wait()
     sol = jnp.concatenate(
         [jnp.where(row8 < 4, ret[2 * i], ret[2 * i + 1]) for i in range(na * members // 2)], axis=0
     )
     sol_h, sol_l = split(sol)
-    corr = nn(jnp.concatenate([sol_h, sol_l], axis=0), vsh[...])
-    corr = pacc[...] + corr[:RHS] + corr[RHS:] + nn(sol_h, vsl[...])
-    cols = vecs
-
-    part_rows = RHS // na
-    psend[...] = corr.reshape(na, part_rows, cols)
-    hop = share("gx", lambda to: psend.at[to], pin1)
-    pin1[a] = psend[a]
-
     sol_hl = jnp.concatenate([sol_h, sol_l], axis=1)
 
     def add_sol(first):
@@ -608,40 +670,20 @@
         w0[first + 1] = w0[first + 1] + change[:, 4 * CZ :]
 
     add_sol(0)
-
-    def total_of(ref, n):
-        out = ref[0]
-        for i in range(1, n):
-            out = out + ref[i]
-        return out
-
-    hop.wait()
-    part = total_of(pin1, na)
-    ph = part_rows // 8
-    pw = nb // ph
-    width = cols // pw
-    for i in range(nb):
-        r, c = divmod(i, pw)
-        psum1[i] = part[r * 8 : r * 8 + 8, c * width : (c + 1) * width]
-    hop = share("gy", lambda to: psum1.at[to], pin2)
-    pin2[b] = psum1[b]
     add_sol(2)
     hop.wait()
-    pin3[z] = total_of(pin2, nb)
-    share("gz", lambda to: pin3.at[z], pin3).wait()
-    pin4[b] = total_of(pin3, nz)
-    hop = share("gy", lambda to: pin4.at[b], pin4)
+    full_in[here] = total_of(fin, nz * 2)
+    hop = exchange(plane_pairs(lambda to, far: full_in.at[here], full_in.at[here]), full_in)
     add_sol(4)
-    hop.wait()
-    pin5[a] = jnp.concatenate(
-        [jnp.concatenate([pin4[r * pw + c] for c in range(pw)], axis=1) for r in range(ph)], axis=0
-    )
-    hop = share("gx", lambda to: pin5.at[a], pin5)
     add_sol(6)
     hop.wait()
-    full = pin5[...].reshape(RHS, cols)
-    pin5_put = pltpu.make_async_copy(pin5, proj_o, loc_sem.at[10])
+    for i in range(RHS // 8):
+        p, q = full_in[2 * i], full_in[2 * i + 1]
+        pt_v[8 * i : 8 * i + 8, :fold] = jnp.where(rowf < 4, p, pltpu.roll(q, 4, 0))
+        pt_v[8 * i : 8 * i + 8, fold:] = jnp.where(rowf < 4, pltpu.roll(p, 4, 0), q)
+    pin5_put = pltpu.make_async_copy(pt_v, proj_o, loc_sem.at[10])
     pin5_put.start()
+    full = pt_v[...]
     hi, lo = split(full)
     pt_hl[:RHS] = hi
     pt_hl[RHS:] = lo
@@ -669,6 +711,10 @@
         wait()
     del sent[:-1]
 
+    for stage in base_stages + cell_stages:
+        for copy in stage:
+            copy.wait_send()
+
     @pl.when(use_low)
     def _():
         for stage in low_stages:
@@ -692,14 +738,18 @@
             copy.wait_send()
 
     hop.wait()
-    gin2[b] = total_of(gin1, nz)
-    share("gy", lambda to: gin2.at[b], gin2).wait()
-    gin3[a] = total_of(gin2, nb)
-    share("gx", lambda to: gin3.at[a], gin3).wait()
-    gin4[z] = total_of(gin3, na)
-    share("gz", lambda to: gin4.at[z], gin4).wait()
-
-    put_gram = pltpu.make_async_copy(gin4, gram_o, loc_sem.at[12])
+    seat = a * nb + b
+    gin2[seat] = total_of(gin1, nz)
+    pairs = []
+    for d in range(na):
+        for e in range(nb):
+            if d or e:
+                to, far = lax.rem(a + d, na), lax.rem(b + e, nb)
+                pairs.append((gin2.at[seat], gin2.at[seat], (to, far, z)))
+    exchange(pairs, gin2).wait()
+    gin3[z] = total_of(gin2, na * nb)
+    share("gz", lambda to: gin3.at[z], gin3).wait()
+    put_gram = pltpu.make_async_copy(gin3, gram_o, loc_sem.at[12])
     put_gram.start()
     for wait in sent:
         wait()
@@ -756,10 +806,7 @@
     members, slots = nb // 2, na * 2
     group, wide = RHS // members, SEP * members
     depth, half = slots * wide, na * wide
-    part_rows = RHS // na
     vecs = earlier_blocks.shape[0] * earlier_blocks.shape[1]
-    pw = nb // (part_rows // 8)
-    width = vecs // pw
     piece = RHS // nz
     vmem = pltpu.VMEM
     scratch = [
@@ -779,8 +826,7 @@
         vmem((LANES, PAIRS * LANES), f32),
         vmem((QUADS, RHS, 4 * CZ), bf16),
         vmem((QUADS, wide, 4 * CZ), bf16),
-        vmem((2, na, members, SEP, depth), bf16),
-        vmem((wide, depth), bf16),
+        vmem((4, na, members, SEP, depth), bf16),
         vmem((depth, half), bf16),
         vmem((QUADS, RHS, 4 * CZ), f32),
         vmem((QUADS, RHS, 4 * CZ), bf16),
@@ -788,14 +834,8 @@
         vmem((QUADS, vecs, 4 * CZ), bf16),
         vmem((QUADS, vecs, 4 * CZ), bf16),
         vmem((2 * vecs, 2 * LANES), f32),
-        vmem((RHS, vecs), f32),
-        vmem((wide, vecs), bf16),
-        vmem((wide, vecs), bf16),
         vmem((members, group, wide), bf16),
-        vmem((members, group, wide), bf16),
-        vmem((slots, group, wide), bf16),
-        vmem((group, wide), f32),
-        vmem((na, group, wide), f32),
+        vmem((slots * members, group, wide), bf16),
         vmem((8, half), f32),
         vmem((8, half), f32),
         vmem((2, 16, wide), bf16),
@@ -803,19 +843,16 @@
         vmem((2, 16, wide), bf16),
         vmem((2, 16, wide), bf16),
         vmem((na * members, 8, wide), f32),
-        vmem((na, part_rows, vecs), f32),
-        vmem((na, part_rows, vecs), f32),
-        vmem((nb, 8, width), f32),
-        vmem((nb, 8, width), f32),
-        vmem((nz, 8, width), f32),
-        vmem((nb, 8, width), f32),
-        vmem((na, part_rows, vecs), f32),
+        vmem((na * members, 8, vecs // 2), f32),
+        vmem((na * members, 8, vecs // 2), f32),
+        vmem((2 * nz, 8, vecs // 2), f32),
+        vmem((na * members, 8, vecs // 2), f32),
+        vmem((RHS, vecs), f32),
         vmem((2 * RHS, vecs), bf16),
         vmem((QUADS, 2 * RHS, 4 * CZ), bf16),
         vmem((nz, piece, LANES), f32),
         vmem((nz, piece, LANES), f32),
-        vmem((nb, piece, LANES), f32),
-        vmem((na, piece, LANES), f32),
+        vmem((na * nb, piece, LANES), f32),
         vmem((nz, piece, LANES), f32),
         pltpu.SemaphoreType.DMA((19,)),
         pltpu.SemaphoreType.DMA((144,)),
@@ -829,7 +866,7 @@
         out_shape=(
             jax.ShapeDtypeStruct((ROWS, CZ), f32),
             jax.ShapeDtypeStruct((QUADS, 2 * RHS, 4 * CZ), bf16),
-            jax.ShapeDtypeStruct((na, part_rows, vecs), f32),
+            jax.ShapeDtypeStruct((RHS, vecs), f32),
             jax.ShapeDtypeStruct((nz, piece, LANES), f32),
         ),
         in_specs=[anywhere] * 9,
@@ -867,7 +904,7 @@
         compiler_params=pltpu.CompilerParams(vmem_limit_bytes=60 * 2**20),
         cost_estimate=pl.CostEstimate(flops=2 * 10**8, bytes_accessed=5 * 2**20, transcendentals=0),
         name="finish",
-    )(gram.reshape(RHS, LANES), orth, res, projection.reshape(RHS, vecs))
+    )(gram.reshape(RHS, LANES), orth, res, projection)
     shape = right_side.shape
     return (res.reshape(shape), new.reshape(shape), projection.T, factor)
 

time: 126 us -> 115 us (0.913)
  Pallas kernels: 125 us -> 114 us
    pallas_call x1, Pallas kernels: 118 us -> 107 us  [body(): pl.pallas_call(functools.partial(kernel, na, nb, nz), out_shape=(jax.Shap...]
where the time goes in v5:
time: 115 us
  Pallas kernels  114 us (99%)
    pallas_call x1, Pallas kernels, body(): pl.pallas_call(functools.partial(kernel, na, nb, nz), out_shape=(jax.Shap...  107 us
    pallas_call x1, Pallas kernels, body(): pl.pallas_call(functools.partial(finish_kernel, math.sqrt(na * nb * nz *...  6.88 us

profile of v5, /device:TPU:1, one launch (start us, length us, event | category | flops | bytes accessed | tf_op | source)
XLA Modules:
  0.0 115.0 jit_solution(264207911707607898)
XLA Ops:
  0.6 107.5 %step.1 = (f32[2048,128]{1,0:T(8,128)}, bf16[8,128,512]{2,1,0:T(8,128)(2,1)}, f32[64,512]{1,0:T(8,128)}, f32[8,8,128]{2,1,0:T(8,128)}) custom-call(f32[64,4,8,128]{3,2,1,0:T(8,128)} %x_h.1, f32[2048,128]{1,0:T(8,128)} %bitcast.12, f32[32,128]{1,0:T(8,128)} %bitcast.18, f32[96,128]{1,0:T(8,128)} %bitcast.16, f32[16384,128]{1,0:T(8,128)} %bitcast.11, ...), custom_call_target="tpu_custom_call" | custom-call | flops 2000000000 | bytes 13631488 | tf_op jit(solution)/shard_map/step/pallas_call | solution.py:864
  108.1 6.9 %finish.1 = (f32[2048,128]{1,0:T(8,128)}, f32[2048,128]{1,0:T(8,128)}, f32[64,512]{1,0:T(8,128)}, f32[64,64]{1,0:T(8,128)}) custom-call(f32[64,128]{1,0:T(8,128)} %bitcast.17, bf16[8,128,512]{2,1,0:T(8,128)(2,1)} %get-tuple-element.13.orth_h, f32[2048,128]{1,0:T(8,128)} %get-tuple-element.14.res_h, f32[64,512]{1,0:T(8,128)} %get-tuple-element.15.proj_h), custom_call_target="tpu_custom_call" | custom-call | flops 200000000 | bytes 5242880 | tf_op jit(solution)/shard_map/finish/pallas_call | solution.py:886

commit v6 on v5

--- a/solution.py
+++ b/solution.py
@@ -89,9 +89,9 @@
     x_h, r_h, d_h, v_h, e_h, c_h, li_h, lo_h, up_h,
     res_o, orth_o, proj_o, gram_o,
     x_v, r_v, d_v, v_v, e_v, c_v, m_v,
-    xp, xsb, hx, hy, hz, zsend, z_ends, res_b, oh, gath, gath_t,
+    xp, xsb, hx, hy, hz, zsend, z_ends, res_b, oh, gath, gath_sib, gath_t, gath_t2,
     w0, wh, wl, vh, vl, eacc,
-    sep_loc, sep_in, base, state, stateb, tiles, fw_in, bw_in, ret,
+    sep_loc, sep_in, base, state, stateb, tiles, fw_in, bw_in, ret, kept, other,
     psend, pin, fin, full_in, pt_v, pt_hl,
     orth, g_loc, gin1, gin2, gin3,
     loc_sem, send_sem, recv_sem,
@@ -330,14 +330,38 @@
             got.wait_recv()
             copy.start()
 
-    low_stages, up_stages, cell_stages, base_stages = (gather_stages(m) for m in range(4))
+    low_stages, up_stages, cell_stages, base_stages, pair_stages = (
+        gather_stages(m) for m in range(5)
+    )
     use_low, use_up = z > 0, z < nz - 1
-    early = z >= nz // 2
-    late = jnp.logical_not(early)
+    odd = lax.rem(z, 2) == 1
+    even = jnp.logical_not(odd)
+
+    def all_of(*conditions):
+        return functools.reduce(jnp.logical_and, conditions)
+
+    pair_low = all_of(even, z >= 4)
+    pair_up = all_of(odd, z <= nz - 3)
+    give_low = all_of(odd, z >= 3, z <= nz - 3)
+    give_up = all_of(even, z >= 2)
     up_after = z < (nz * 5) // 8
-    up_before = jnp.logical_and(use_up, jnp.logical_not(up_after))
+    up_before = all_of(use_up, jnp.logical_not(up_after))
+    first_before = z >= 3
+    second_before = all_of(odd, z >= 3)
+    cells_before = z <= nz // 2
+
+    def shift_copy(m, step):
+        n = count[0]
+        count[0] += 1
+        return remote(n, gath.at[m, a, member], gath.at[4, a, member], (a, b, z + step))
+
+    shift_low, shift_up = shift_copy(0, 1), shift_copy(1, -1)
+    sibling = remote(count[0], gath.at[4], gath_sib, (a, member * 2 + 1 - core, z))
+    count[0] += 1
     launch(base_stages[0])
     pl.when(use_low)(lambda: launch(low_stages[0]))
+    pl.when(give_low)(shift_low.start)
+    pl.when(give_up)(shift_up.start)
 
     get_c.wait()
     cells = jnp.broadcast_to(c_v[...], (SEP, SEP)).astype(f32)
@@ -381,6 +405,12 @@
     arrive(halo)
     arrive(base_stages[1])
     launch(base_stages[2])
+
+    @pl.when(pair_low)
+    def _():
+        shift_low.wait_recv()
+        launch(pair_stages[0])
+
 
     @pl.when(use_low)
     def _():
@@ -451,6 +481,7 @@
     relay(base_stages[2], base_stages[3])
     for c in (1, 2, 3):
         pl.when(split_early)(functools.partial(relayout, c))
+    pl.when(pair_low)(lambda: relay(pair_stages[0], pair_stages[1]))
     pl.when(use_low)(lambda: relay(low_stages[2], low_stages[3]))
     hop.wait()
     arrive(base_stages[3])
@@ -469,6 +500,22 @@
         v = jnp.where(gx_here >= 2, both[8:], both[:8])
         v = jnp.where(lax.rem(gx_here, 2) == 1, pltpu.roll(v, 4, 0), v)
         base[:, j * wide : (j + 1) * wide] = jnp.where(row8 < 4, v, pltpu.roll(v, 4, 0))
+
+    def plane_copies(first, src, dst, step):
+        return [
+            remote(first + d, src, dst, (a, member * 2 + lax.rem(core + d, 2), z + step))
+            for d in range(2)
+        ]
+
+    give_base = plane_copies(count[0], base, other.at[core], 1)
+    give_state = plane_copies(count[0] + 2, kept, other.at[core], -1)
+    count[0] += 4
+    pl.when(give_low)(lambda: launch(give_base))
+
+    @pl.when(pair_low)
+    def _():
+        arrive(pair_stages[1])
+        launch(pair_stages[2])
 
     eacc[...] = jnp.zeros(eacc.shape, f32)
 
@@ -509,128 +556,192 @@
         launch(cell_stages[2])
         relay(cell_stages[2], cell_stages[3])
 
-    def sweep_copies(first, dst, step):
-        return [
-            remote(
-                first + d, stateb.at[0 if step > 0 else 1], dst.at[core],
-                (a, member * 2 + lax.rem(core + d, 2), z + step),
-            )
-            for d in range(2)
-        ]
-
-    def sweep_push(first, dst, step):
-        v = state[...]
+    fw_1 = plane_copies(count[0], stateb.at[0], fw_in.at[core], 1)
+    fw_2 = plane_copies(count[0] + 2, stateb.at[0], fw_in.at[core], 2)
+    bw_1 = plane_copies(count[0] + 4, stateb.at[1], bw_in.at[core], -1)
+    bw_2 = plane_copies(count[0] + 6, stateb.at[1], bw_in.at[core], -2)
+    count[0] += 8
+    fw_near = all_of(z < nz - 1, jnp.logical_or(even, z == 1))
+    fw_far = all_of(even, z >= 2, z <= nz - 4)
+    bw_near, bw_far = odd, all_of(odd, z >= 3)
+    row_group = iota((16, LANES), 0) // 4
+
+    def pack(v):
         t = [v[:, j * wide : (j + 1) * wide] for j in range(na)]
-        packed = jnp.concatenate(
+        return jnp.concatenate(
             [jnp.where(row8 < 4, t[0], t[1]), jnp.where(row8 < 4, t[2], t[3])], axis=0
         )
-        stateb[0 if step > 0 else 1] = packed.astype(bf16)
-        for copy in sweep_copies(first, dst, step):
-            copy.start()
-
-    row_group = iota((16, LANES), 0) // 4
-
-    def product_of(first, dst, step):
-        arrive(sweep_copies(first, dst, step))
+
+    def product_of(packed, matrix):
         left = []
-        for i in range(2):
-            v = dst[i].astype(f32)
+        for v in packed:
+            v = v.astype(f32)
             left += [jnp.where(row_group == j, v, 0.0).astype(bf16) for j in range(na)]
-        out = nn(jnp.concatenate(left, axis=1), gath_t[...])
+        out = nn(jnp.concatenate(left, axis=1), matrix[...])
         out = out[:8] + out[8:]
         return out + pltpu.roll(out, 4, 0)
 
-    def transpose_matrix(m):
+    def two_steps(packed, start):
+        between = jnp.concatenate([other[0], other[1]], axis=1) - product_of(packed, gath_t2)
+        packed = [pack(between[:, k * half : (k + 1) * half]).astype(bf16) for k in range(2)]
+        return start - product_of(packed, gath_t)
+
+    def transpose_matrix(src, dst, column):
         def step(t, carry):
             at = rows_at(t * LANES, LANES)
-            block = gath[m, :, :, :, at].reshape(half, LANES)
-            gath_t[at, :] = block.astype(f32).T.astype(bf16)
+            block = src[:, :, :, at].reshape(half, LANES)
+            dst[at, pl.ds(column, half)] = block.astype(f32).T.astype(bf16)
             return carry
 
         lax.fori_loop(0, depth // LANES, step, 0)
 
-    fw_first = count[0]
-    bw_first = fw_first + 2
-    count[0] = bw_first + 2
+    def transpose_pair():
+        transpose_matrix(gath.at[4], gath_t2, pl.multiple_of(core * half, half))
+        sibling.wait_recv()
+        transpose_matrix(gath_sib, gath_t2, pl.multiple_of((1 - core) * half, half))
 
     def products(first, last):
         lax.fori_loop(first, last, earlier_product, 0)
 
-    pl.when(up_before)(lambda: launch(up_stages[0]))
-    pl.when(early)(lambda: products(0, QUADS // 2))
-
-    @pl.when(up_before)
-    def _():
+    not_first, not_second = jnp.logical_not(first_before), jnp.logical_not(second_before)
+    up_pair_before = all_of(pair_up, up_before)
+    up_pair_after = all_of(pair_up, up_after)
+
+    def up_launch(stage):
+        launch(up_stages[stage])
+
+    def up_middle():
         relay(up_stages[0], up_stages[1])
         arrive(up_stages[1])
         launch(up_stages[2])
 
-    @pl.when(early)
+    def pair_begin():
+        shift_up.wait_recv()
+        launch(pair_stages[0])
+
+    def pair_middle():
+        relay(pair_stages[0], pair_stages[1])
+        arrive(pair_stages[1])
+        launch(pair_stages[2])
+
+    def pair_end():
+        arrive(pair_stages[3])
+        sibling.start()
+
+    pl.when(up_before)(lambda: launch(up_stages[0]))
+    pl.when(up_pair_before)(pair_begin)
+    pl.when(first_before)(lambda: products(0, QUADS // 2))
+    pl.when(pair_low)(lambda: relay(pair_stages[2], pair_stages[3]))
+    pl.when(up_before)(up_middle)
+    pl.when(up_pair_before)(pair_middle)
+    pl.when(pair_low)(pair_end)
+
+    @pl.when(second_before)
     def _():
         products(QUADS // 2, QUADS)
         earlier_results()
 
     pl.when(up_before)(lambda: relay(up_stages[2], up_stages[3]))
+    pl.when(up_pair_before)(lambda: relay(pair_stages[2], pair_stages[3]))
 
     @pl.when(use_low)
     def _():
         arrive(low_stages[3])
-        transpose_matrix(0)
+        transpose_matrix(gath.at[0], gath_t, 0)
+
+    pl.when(pair_low)(transpose_pair)
 
     @pl.when(z == 0)
     def _():
         state[...] = base[...]
 
-    @pl.when(z > 0)
-    def _():
-        state[...] = base[...] - product_of(fw_first, fw_in, 1)
-
-    @pl.when(z < nz - 1)
-    def _():
-        sweep_push(fw_first, fw_in, 1)
+    @pl.when(all_of(z > 0, jnp.logical_not(pair_low)))
+    def _():
+        arrive(fw_1)
+        state[...] = base[...] - product_of([fw_in[0], fw_in[1]], gath_t)
+
+    @pl.when(pair_low)
+    def _():
+        arrive(give_base)
+        arrive(fw_2)
+        state[...] = two_steps([fw_in[0], fw_in[1]], base[...])
+
+    @pl.when(fw_near)
+    def _():
+        stateb[0] = pack(state[...]).astype(bf16)
+        launch(fw_1)
+
+    pl.when(fw_far)(lambda: launch(fw_2))
+
+    @pl.when(give_up)
+    def _():
+        kept[...] = state[...]
+        launch(give_state)
+
+    def push_back():
+        stateb[1] = pack(state[...]).astype(bf16)
+        launch(bw_1)
 
     @pl.when(z == nz - 1)
     def _():
-        sweep_push(bw_first, bw_in, -1)
+        push_back()
+        launch(bw_2)
 
     pl.when(up_after)(lambda: launch(up_stages[0]))
+    pl.when(up_pair_after)(pair_begin)
 
     @pl.when(jnp.logical_not(split_early))
     def _():
         for c in range(4):
             relayout(c)
 
-    pl.when(late)(lambda: products(0, QUADS // 2))
-
-    @pl.when(up_after)
-    def _():
-        relay(up_stages[0], up_stages[1])
-        arrive(up_stages[1])
-        launch(up_stages[2])
-
-    @pl.when(late)
+    pl.when(not_first)(lambda: products(0, QUADS // 2))
+    pl.when(up_after)(up_middle)
+    pl.when(up_pair_after)(pair_middle)
+
+    @pl.when(not_second)
     def _():
         products(QUADS // 2, QUADS)
         earlier_results()
 
     pl.when(up_after)(lambda: relay(up_stages[2], up_stages[3]))
-    pl.when(late)(gather_cells)
-
-    @pl.when(z < nz - 1)
+    pl.when(up_pair_after)(lambda: relay(pair_stages[2], pair_stages[3]))
+    pl.when(cells_before)(lambda: launch(cell_stages[0]))
+    pl.when(pair_up)(pair_end)
+
+    @pl.when(use_up)
     def _():
         arrive(up_stages[3])
-        transpose_matrix(1)
-        state[...] = state[...] - product_of(bw_first, bw_in, -1)
-
-    @pl.when(jnp.logical_and(z > 0, z < nz - 1))
-    def _():
-        sweep_push(bw_first, bw_in, -1)
+        transpose_matrix(gath.at[1], gath_t, 0)
+
+    @pl.when(cells_before)
+    def _():
+        relay(cell_stages[0], cell_stages[1])
+        arrive(cell_stages[1])
+        launch(cell_stages[2])
+
+    pl.when(pair_up)(transpose_pair)
+    pl.when(cells_before)(lambda: relay(cell_stages[2], cell_stages[3]))
+
+    @pl.when(all_of(use_up, jnp.logical_not(pair_up)))
+    def _():
+        arrive(bw_1)
+        state[...] = state[...] - product_of([bw_in[0], bw_in[1]], gath_t)
+
+    @pl.when(pair_up)
+    def _():
+        arrive(give_state)
+        arrive(bw_2)
+        state[...] = two_steps([bw_in[0], bw_in[1]], state[...])
+
+    pl.when(all_of(odd, use_up))(push_back)
+    pl.when(all_of(bw_far, use_up))(lambda: launch(bw_2))
 
     for j in range(na):
         tiles[j] = state[:, j * wide : (j + 1) * wide]
     ret_came = exchange(plane_pairs(lambda to, far: tiles.at[to], ret.at[here]), ret)
     ret[here] = tiles[a]
-    pl.when(early)(gather_cells)
+    pl.when(jnp.logical_not(cells_before))(gather_cells)
 
     def total_of(ref, n):
         out = ref[0]
@@ -727,15 +838,16 @@
             for copy in stage:
                 copy.wait_send()
 
-    @pl.when(z < nz - 1)
-    def _():
-        for copy in sweep_copies(fw_first, fw_in, 1):
-            copy.wait_send()
-
-    @pl.when(z > 0)
-    def _():
-        for copy in sweep_copies(bw_first, bw_in, -1):
-            copy.wait_send()
+    use_pair = jnp.logical_or(pair_low, pair_up)
+    for condition, copies in (
+        (use_pair, sum(pair_stages, [])), (use_pair, [sibling]),
+        (give_low, [shift_low] + give_base), (give_up, [shift_up] + give_state),
+        (fw_near, fw_1), (fw_far, fw_2), (bw_near, bw_1), (bw_far, bw_2),
+    ):
+        @pl.when(condition)
+        def _(copies=copies):
+            for copy in copies:
+                copy.wait_send()
 
     hop.wait()
     seat = a * nb + b
@@ -826,8 +938,10 @@
         vmem((LANES, PAIRS * LANES), f32),
         vmem((QUADS, RHS, 4 * CZ), bf16),
         vmem((QUADS, wide, 4 * CZ), bf16),
-        vmem((4, na, members, SEP, depth), bf16),
+        vmem((5, na, members, SEP, depth), bf16),
+        vmem((na, members, SEP, depth), bf16),
         vmem((depth, half), bf16),
+        vmem((depth, depth), bf16),
         vmem((QUADS, RHS, 4 * CZ), f32),
         vmem((QUADS, RHS, 4 * CZ), bf16),
         vmem((QUADS, RHS, 4 * CZ), bf16),
@@ -843,6 +957,8 @@
         vmem((2, 16, wide), bf16),
         vmem((2, 16, wide), bf16),
         vmem((na * members, 8, wide), f32),
+        vmem((8, half), f32),
+        vmem((2, 8, half), f32),
         vmem((na * members, 8, vecs // 2), f32),
         vmem((na * members, 8, vecs // 2), f32),
         vmem((2 * nz, 8, vecs // 2), f32),
@@ -855,8 +971,8 @@
         vmem((na * nb, piece, LANES), f32),
         vmem((nz, piece, LANES), f32),
         pltpu.SemaphoreType.DMA((19,)),
-        pltpu.SemaphoreType.DMA((144,)),
-        pltpu.SemaphoreType.DMA((144,)),
+        pltpu.SemaphoreType.DMA((160,)),
+        pltpu.SemaphoreType.DMA((160,)),
     ]
     flat = lambda v: v.reshape(-1, CZ)
     anywhere = pl.BlockSpec(memory_space=pl.ANY)

time: 115 us -> 116 us (level)
  Pallas kernels: 114 us -> 116 us
    pallas_call x1, Pallas kernels: 107 us -> 109 us  [body(): pl.pallas_call(functools.partial(kernel, na, nb, nz), out_shape=(jax.Shap...]
where the time goes in v6:
time: 116 us
  Pallas kernels  116 us (100%)
    pallas_call x1, Pallas kernels, body(): pl.pallas_call(functools.partial(kernel, na, nb, nz), out_shape=(jax.Shap...  109 us
    pallas_call x1, Pallas kernels, body(): pl.pallas_call(functools.partial(finish_kernel, math.sqrt(na * nb * nz *...  6.88 us

profile of v6, /device:TPU:1, one launch (start us, length us, event | category | flops | bytes accessed | tf_op | source)
XLA Modules:
  0.0 116.3 jit_solution(3766426586225204470)
XLA Ops:
  0.6 108.8 %step.1 = (f32[2048,128]{1,0:T(8,128)}, bf16[8,128,512]{2,1,0:T(8,128)(2,1)}, f32[64,512]{1,0:T(8,128)}, f32[8,8,128]{2,1,0:T(8,128)}) custom-call(f32[64,4,8,128]{3,2,1,0:T(8,128)} %x_h.1, f32[2048,128]{1,0:T(8,128)} %bitcast.12, f32[32,128]{1,0:T(8,128)} %bitcast.18, f32[96,128]{1,0:T(8,128)} %bitcast.16, f32[16384,128]{1,0:T(8,128)} %bitcast.11, ...), custom_call_target="tpu_custom_call" | custom-call | flops 2000000000 | bytes 13631488 | tf_op jit(solution)/shard_map/step/pallas_call | solution.py:980
  109.4 6.9 %finish.1 = (f32[2048,128]{1,0:T(8,128)}, f32[2048,128]{1,0:T(8,128)}, f32[64,512]{1,0:T(8,128)}, f32[64,64]{1,0:T(8,128)}) custom-call(f32[64,128]{1,0:T(8,128)} %bitcast.17, bf16[8,128,512]{2,1,0:T(8,128)(2,1)} %get-tuple-element.13.orth_h, f32[2048,128]{1,0:T(8,128)} %get-tuple-element.14.res_h, f32[64,512]{1,0:T(8,128)} %get-tuple-element.15.proj_h), custom_call_target="tpu_custom_call" | custom-call | flops 200000000 | bytes 5242880 | tf_op jit(solution)/shard_map/finish/pallas_call | solution.py:1002

commit v7 on v6

--- a/solution.py
+++ b/solution.py
@@ -89,7 +89,7 @@
     x_h, r_h, d_h, v_h, e_h, c_h, li_h, lo_h, up_h,
     res_o, orth_o, proj_o, gram_o,
     x_v, r_v, d_v, v_v, e_v, c_v, m_v,
-    xp, xsb, hx, hy, hz, zsend, z_ends, res_b, oh, gath, gath_sib, gath_t, gath_t2,
+    xp, xsb, hx, hy, hz, zsend, z_ends, res_b, oh, gath, gath_sib,
     w0, wh, wl, vh, vl, eacc,
     sep_loc, sep_in, base, state, stateb, tiles, fw_in, bw_in, ret, kept, other,
     psend, pin, fin, full_in, pt_v, pt_hl,
@@ -572,33 +572,27 @@
             [jnp.where(row8 < 4, t[0], t[1]), jnp.where(row8 < 4, t[2], t[3])], axis=0
         )
 
-    def product_of(packed, matrix):
+    def left_of(packed):
         left = []
         for v in packed:
             v = v.astype(f32)
             left += [jnp.where(row_group == j, v, 0.0).astype(bf16) for j in range(na)]
-        out = nn(jnp.concatenate(left, axis=1), matrix[...])
+        return jnp.concatenate(left, axis=1)
+
+    def product_of(left, rows):
+        out = nt(left, rows.reshape(half, depth)[...])
         out = out[:8] + out[8:]
         return out + pltpu.roll(out, 4, 0)
 
-    def two_steps(packed, start):
-        between = jnp.concatenate([other[0], other[1]], axis=1) - product_of(packed, gath_t2)
-        packed = [pack(between[:, k * half : (k + 1) * half]).astype(bf16) for k in range(2)]
-        return start - product_of(packed, gath_t)
-
-    def transpose_matrix(src, dst, column):
-        def step(t, carry):
-            at = rows_at(t * LANES, LANES)
-            block = src[:, :, :, at].reshape(half, LANES)
-            dst[at, pl.ds(column, half)] = block.astype(f32).T.astype(bf16)
-            return carry
-
-        lax.fori_loop(0, depth // LANES, step, 0)
-
-    def transpose_pair():
-        transpose_matrix(gath.at[4], gath_t2, pl.multiple_of(core * half, half))
-        sibling.wait_recv()
-        transpose_matrix(gath_sib, gath_t2, pl.multiple_of((1 - core) * half, half))
+    first_core = jnp.zeros((8, half), jnp.int32) + core == 0
+
+    def two_steps(left, start, m):
+        own, far = product_of(left, gath.at[4]), product_of(left, gath_sib)
+        between = (
+            other[0] - jnp.where(first_core, own, far),
+            other[1] - jnp.where(first_core, far, own),
+        )
+        return start - product_of(left_of([pack(v).astype(bf16) for v in between]), gath.at[m])
 
     def products(first, last):
         lax.fori_loop(first, last, earlier_product, 0)
@@ -644,12 +638,8 @@
     pl.when(up_before)(lambda: relay(up_stages[2], up_stages[3]))
     pl.when(up_pair_before)(lambda: relay(pair_stages[2], pair_stages[3]))
 
-    @pl.when(use_low)
-    def _():
-        arrive(low_stages[3])
-        transpose_matrix(gath.at[0], gath_t, 0)
-
-    pl.when(pair_low)(transpose_pair)
+    pl.when(use_low)(lambda: arrive(low_stages[3]))
+    pl.when(pair_low)(sibling.wait_recv)
 
     @pl.when(z == 0)
     def _():
@@ -658,13 +648,13 @@
     @pl.when(all_of(z > 0, jnp.logical_not(pair_low)))
     def _():
         arrive(fw_1)
-        state[...] = base[...] - product_of([fw_in[0], fw_in[1]], gath_t)
+        state[...] = base[...] - product_of(left_of([fw_in[0], fw_in[1]]), gath.at[0])
 
     @pl.when(pair_low)
     def _():
         arrive(give_base)
         arrive(fw_2)
-        state[...] = two_steps([fw_in[0], fw_in[1]], base[...])
+        state[...] = two_steps(left_of([fw_in[0], fw_in[1]]), base[...], 0)
 
     @pl.when(fw_near)
     def _():
@@ -709,10 +699,7 @@
     pl.when(cells_before)(lambda: launch(cell_stages[0]))
     pl.when(pair_up)(pair_end)
 
-    @pl.when(use_up)
-    def _():
-        arrive(up_stages[3])
-        transpose_matrix(gath.at[1], gath_t, 0)
+    pl.when(use_up)(lambda: arrive(up_stages[3]))
 
     @pl.when(cells_before)
     def _():
@@ -720,19 +707,19 @@
         arrive(cell_stages[1])
         launch(cell_stages[2])
 
-    pl.when(pair_up)(transpose_pair)
+    pl.when(pair_up)(sibling.wait_recv)
     pl.when(cells_before)(lambda: relay(cell_stages[2], cell_stages[3]))
 
     @pl.when(all_of(use_up, jnp.logical_not(pair_up)))
     def _():
         arrive(bw_1)
-        state[...] = state[...] - product_of([bw_in[0], bw_in[1]], gath_t)
+        state[...] = state[...] - product_of(left_of([bw_in[0], bw_in[1]]), gath.at[1])
 
     @pl.when(pair_up)
     def _():
         arrive(give_state)
         arrive(bw_2)
-        state[...] = two_steps([bw_in[0], bw_in[1]], state[...])
+        state[...] = two_steps(left_of([bw_in[0], bw_in[1]]), state[...], 1)
 
     pl.when(all_of(odd, use_up))(push_back)
     pl.when(all_of(bw_far, use_up))(lambda: launch(bw_2))
@@ -940,8 +927,6 @@
         vmem((QUADS, wide, 4 * CZ), bf16),
         vmem((5, na, members, SEP, depth), bf16),
         vmem((na, members, SEP, depth), bf16),
-        vmem((depth, half), bf16),
-        vmem((depth, depth), bf16),
         vmem((QUADS, RHS, 4 * CZ), f32),
         vmem((QUADS, RHS, 4 * CZ), bf16),
         vmem((QUADS, RHS, 4 * CZ), bf16),

time: 116 us -> 116 us (level)
  no operation moved by 1% of the time
where the time goes in v7:
time: 116 us
  Pallas kernels  115 us (99%)
    pallas_call x1, Pallas kernels, body(): pl.pallas_call(functools.partial(kernel, na, nb, nz), out_shape=(jax.Shap...  108 us
    pallas_call x1, Pallas kernels, body(): pl.pallas_call(functools.partial(finish_kernel, math.sqrt(na * nb * nz *...  6.88 us

profile of v7, /device:TPU:1, one launch (start us, length us, event | category | flops | bytes accessed | tf_op | source)
XLA Modules:
  0.0 116.0 jit_solution(3118943191546283208)
XLA Ops:
  0.6 108.5 %step.1 = (f32[2048,128]{1,0:T(8,128)}, bf16[8,128,512]{2,1,0:T(8,128)(2,1)}, f32[64,512]{1,0:T(8,128)}, f32[8,8,128]{2,1,0:T(8,128)}) custom-call(f32[64,4,8,128]{3,2,1,0:T(8,128)} %x_h.1, f32[2048,128]{1,0:T(8,128)} %bitcast.12, f32[32,128]{1,0:T(8,128)} %bitcast.18, f32[96,128]{1,0:T(8,128)} %bitcast.16, f32[16384,128]{1,0:T(8,128)} %bitcast.11, ...), custom_call_target="tpu_custom_call" | custom-call | flops 2000000000 | bytes 13631488 | tf_op jit(solution)/shard_map/step/pallas_call | solution.py:965
  109.1 6.9 %finish.1 = (f32[2048,128]{1,0:T(8,128)}, f32[2048,128]{1,0:T(8,128)}, f32[64,512]{1,0:T(8,128)}, f32[64,64]{1,0:T(8,128)}) custom-call(f32[64,128]{1,0:T(8,128)} %bitcast.17, bf16[8,128,512]{2,1,0:T(8,128)(2,1)} %get-tuple-element.13.orth_h, f32[2048,128]{1,0:T(8,128)} %get-tuple-element.14.res_h, f32[64,512]{1,0:T(8,128)} %get-tuple-element.15.proj_h), custom_call_target="tpu_custom_call" | custom-call | flops 200000000 | bytes 5242880 | tf_op jit(solution)/shard_map/finish/pallas_call | solution.py:987

commit v8 on v7

--- a/solution.py
+++ b/solution.py
@@ -90,7 +90,7 @@
     res_o, orth_o, proj_o, gram_o,
     x_v, r_v, d_v, v_v, e_v, c_v, m_v,
     xp, xsb, hx, hy, hz, zsend, z_ends, res_b, oh, gath, gath_sib,
-    w0, wh, wl, vh, vl, eacc,
+    w0, wh, wl, vh, vl, eacc, cell_v, sol_v,
     sep_loc, sep_in, base, state, stateb, tiles, fw_in, bw_in, ret, kept, other,
     psend, pin, fin, full_in, pt_v, pt_hl,
     orth, g_loc, gin1, gin2, gin3,
@@ -348,7 +348,8 @@
     up_before = all_of(use_up, jnp.logical_not(up_after))
     first_before = z >= 3
     second_before = all_of(odd, z >= 3)
-    cells_before = z <= nz // 2
+    cells_here = z <= 2
+    owners_add = jnp.logical_not(cells_here)
 
     def shift_copy(m, step):
         n = count[0]
@@ -532,29 +533,34 @@
         plane_pairs(lambda to, far: psend.at[far * na + to], pin.at[here]), pin
     )
 
-    def earlier_results():
-        main = eacc[:vecs, :LANES] + eacc[vecs:, :LANES]
-        main = main.T
-        main = main[:RHS] + main[RHS:]
+    def send_sums(main):
         for i in range(RHS // 8):
             one = main[8 * i : 8 * i + 8, :fold]
             two = main[8 * i : 8 * i + 8, fold:]
             psend[2 * i] = jnp.where(rowf < 4, one, pltpu.roll(two, 4, 0))
             psend[2 * i + 1] = jnp.where(rowf < 4, pltpu.roll(one, 4, 0), two)
         launch(plane_sum)
-        for i in range(2):
-            values = eacc[i * vecs : (i + 1) * vecs, LANES:].T
-            v = values[:SEP]
-            for e in range(1, members):
-                v = v + values[e * SEP : (e + 1) * SEP]
-            gath[2, a, member, :, i * vecs : (i + 1) * vecs] = v.astype(bf16)
-
-    def gather_cells():
-        launch(cell_stages[0])
-        relay(cell_stages[0], cell_stages[1])
-        arrive(cell_stages[1])
-        launch(cell_stages[2])
-        relay(cell_stages[2], cell_stages[3])
+
+    def earlier_results():
+        main = eacc[:vecs, :LANES] + eacc[vecs:, :LANES]
+        main = main.T
+        main = main[:RHS] + main[RHS:]
+
+        @pl.when(cells_here)
+        def _():
+            send_sums(main)
+            for i in range(2):
+                values = eacc[i * vecs : (i + 1) * vecs, LANES:].T
+                v = values[:SEP]
+                for e in range(1, members):
+                    v = v + values[e * SEP : (e + 1) * SEP]
+                gath[2, a, member, :, i * vecs : (i + 1) * vecs] = v.astype(bf16)
+
+        @pl.when(owners_add)
+        def _():
+            pt_v[...] = main
+            for i in range(2):
+                cell_v[i] = eacc[i * vecs : (i + 1) * vecs, LANES:].T.astype(bf16)
 
     fw_1 = plane_copies(count[0], stateb.at[0], fw_in.at[core], 1)
     fw_2 = plane_copies(count[0] + 2, stateb.at[0], fw_in.at[core], 2)
@@ -696,19 +702,19 @@
 
     pl.when(up_after)(lambda: relay(up_stages[2], up_stages[3]))
     pl.when(up_pair_after)(lambda: relay(pair_stages[2], pair_stages[3]))
-    pl.when(cells_before)(lambda: launch(cell_stages[0]))
+    pl.when(cells_here)(lambda: launch(cell_stages[0]))
     pl.when(pair_up)(pair_end)
 
     pl.when(use_up)(lambda: arrive(up_stages[3]))
 
-    @pl.when(cells_before)
+    @pl.when(cells_here)
     def _():
         relay(cell_stages[0], cell_stages[1])
         arrive(cell_stages[1])
         launch(cell_stages[2])
 
     pl.when(pair_up)(sibling.wait_recv)
-    pl.when(cells_before)(lambda: relay(cell_stages[2], cell_stages[3]))
+    pl.when(cells_here)(lambda: relay(cell_stages[2], cell_stages[3]))
 
     @pl.when(all_of(use_up, jnp.logical_not(pair_up)))
     def _():
@@ -728,7 +734,6 @@
         tiles[j] = state[:, j * wide : (j + 1) * wide]
     ret_came = exchange(plane_pairs(lambda to, far: tiles.at[to], ret.at[here]), ret)
     ret[here] = tiles[a]
-    pl.when(jnp.logical_not(cells_before))(gather_cells)
 
     def total_of(ref, n):
         out = ref[0]
@@ -736,15 +741,33 @@
             out = out + ref[i]
         return out
 
+    def take_sol():
+        ret_came.wait()
+        sol = jnp.concatenate(
+            [jnp.where(row8 < 4, ret[2 * i], ret[2 * i + 1]) for i in range(na * members // 2)],
+            axis=0,
+        )
+        sol_v[...] = jnp.concatenate(split(sol), axis=1)
+
+    @pl.when(owners_add)
+    def _():
+        take_sol()
+        sol_h, sol_l = sol_v[:, :wide], sol_v[:, wide:]
+        part = nn(jnp.concatenate([sol_h, sol_l], axis=0), cell_v[0])
+        send_sums(pt_v[...] + part[:RHS] + part[RHS:] + nn(sol_h, cell_v[1]))
+
     pin[here] = psend[here]
     plane_came.wait()
-    arrive(cell_stages[3])
-    sol_h, sol_l = split(state[...])
-    part = nn(jnp.concatenate([sol_h, sol_l], axis=0), gath[2].reshape(half, 2 * vecs))
-    part = part[:8, :vecs] + part[8:, :vecs] + part[:8, vecs:]
-    part = jnp.where(rowf < 4, part[:, :fold], part[:, fold:]) + total_of(pin, na * members)
     where_fin = z * 2 + core
-    fin[where_fin] = part
+    fin[where_fin] = total_of(pin, na * members)
+
+    @pl.when(cells_here)
+    def _():
+        arrive(cell_stages[3])
+        part = nn(jnp.concatenate(split(state[...]), axis=0), gath[2].reshape(half, 2 * vecs))
+        part = part[:8, :vecs] + part[8:, :vecs] + part[:8, vecs:]
+        fin[where_fin] = fin[where_fin] + jnp.where(rowf < 4, part[:, :fold], part[:, fold:])
+
     pairs = []
     for d in range(nz):
         for e in range(2):
@@ -754,12 +777,8 @@
                 pairs.append((mine_there, mine_there, (a, member * 2 + kind, to)))
     hop = exchange(pairs, fin)
 
-    ret_came.wait()
-    sol = jnp.concatenate(
-        [jnp.where(row8 < 4, ret[2 * i], ret[2 * i + 1]) for i in range(na * members // 2)], axis=0
-    )
-    sol_h, sol_l = split(sol)
-    sol_hl = jnp.concatenate([sol_h, sol_l], axis=1)
+    pl.when(cells_here)(take_sol)
+    sol_hl = sol_v[...]
 
     def add_sol(first):
         twice = jnp.concatenate([oh[first], oh[first + 1]], axis=1)
@@ -809,7 +828,7 @@
         wait()
     del sent[:-1]
 
-    for stage in base_stages + cell_stages:
+    for stage in base_stages:
         for copy in stage:
             copy.wait_send()
 
@@ -827,7 +846,7 @@
 
     use_pair = jnp.logical_or(pair_low, pair_up)
     for condition, copies in (
-        (use_pair, sum(pair_stages, [])), (use_pair, [sibling]),
+        (cells_here, sum(cell_stages, [])), (use_pair, sum(pair_stages, [])), (use_pair, [sibling]),
         (give_low, [shift_low] + give_base), (give_up, [shift_up] + give_state),
         (fw_near, fw_1), (fw_far, fw_2), (bw_near, bw_1), (bw_far, bw_2),
     ):
@@ -933,6 +952,8 @@
         vmem((QUADS, vecs, 4 * CZ), bf16),
         vmem((QUADS, vecs, 4 * CZ), bf16),
         vmem((2 * vecs, 2 * LANES), f32),
+        vmem((2, wide, vecs), bf16),
+        vmem((RHS, 2 * wide), bf16),
         vmem((members, group, wide), bf16),
         vmem((slots * members, group, wide), bf16),
         vmem((8, half), f32),

time: 116 us -> 114 us (0.983)
  Pallas kernels: 115 us -> 113 us
    pallas_call x1, Pallas kernels: 108 us -> 106 us  [body(): pl.pallas_call(functools.partial(kernel, na, nb, nz), out_shape=(jax.Shap...]
where the time goes in v8:
time: 114 us
  Pallas kernels  113 us (99%)
    pallas_call x1, Pallas kernels, body(): pl.pallas_call(functools.partial(kernel, na, nb, nz), out_shape=(jax.Shap...  106 us
    pallas_call x1, Pallas kernels, body(): pl.pallas_call(functools.partial(finish_kernel, math.sqrt(na * nb * nz *...  6.88 us

profile of v8, /device:TPU:1, one launch (start us, length us, event | category | flops | bytes accessed | tf_op | source)
XLA Modules:
  0.0 113.8 jit_solution(10416632461568910291)
XLA Ops:
  0.6 106.2 %step.1 = (f32[2048,128]{1,0:T(8,128)}, bf16[8,128,512]{2,1,0:T(8,128)(2,1)}, f32[64,512]{1,0:T(8,128)}, f32[8,8,128]{2,1,0:T(8,128)}) custom-call(f32[64,4,8,128]{3,2,1,0:T(8,128)} %x_h.1, f32[2048,128]{1,0:T(8,128)} %bitcast.12, f32[32,128]{1,0:T(8,128)} %bitcast.18, f32[96,128]{1,0:T(8,128)} %bitcast.16, f32[16384,128]{1,0:T(8,128)} %bitcast.11, ...), custom_call_target="tpu_custom_call" | custom-call | flops 2000000000 | bytes 13631488 | tf_op jit(solution)/shard_map/step/pallas_call | solution.py:986
  106.8 6.9 %finish.1 = (f32[2048,128]{1,0:T(8,128)}, f32[2048,128]{1,0:T(8,128)}, f32[64,512]{1,0:T(8,128)}, f32[64,64]{1,0:T(8,128)}) custom-call(f32[64,128]{1,0:T(8,128)} %bitcast.17, bf16[8,128,512]{2,1,0:T(8,128)(2,1)} %get-tuple-element.13.orth_h, f32[2048,128]{1,0:T(8,128)} %get-tuple-element.14.res_h, f32[64,512]{1,0:T(8,128)} %get-tuple-element.15.proj_h), custom_call_target="tpu_custom_call" | custom-call | flops 200000000 | bytes 5242880 | tf_op jit(solution)/shard_map/finish/pallas_call | solution.py:1008

commit v9 on v8

--- a/solution.py
+++ b/solution.py
@@ -344,11 +344,9 @@
     pair_up = all_of(odd, z <= nz - 3)
     give_low = all_of(odd, z >= 3, z <= nz - 3)
     give_up = all_of(even, z >= 2)
-    up_after = z < (nz * 5) // 8
-    up_before = all_of(use_up, jnp.logical_not(up_after))
-    first_before = z >= 3
-    second_before = all_of(odd, z >= 3)
-    cells_here = z <= 2
+    before, after = z >= 3, z < 3
+    up_before = all_of(use_up, before)
+    cells_here = jnp.logical_or(z == 0, z == 2)
     owners_add = jnp.logical_not(cells_here)
 
     def shift_copy(m, step):
@@ -484,6 +482,12 @@
         pl.when(split_early)(functools.partial(relayout, c))
     pl.when(pair_low)(lambda: relay(pair_stages[0], pair_stages[1]))
     pl.when(use_low)(lambda: relay(low_stages[2], low_stages[3]))
+
+    @pl.when(pair_low)
+    def _():
+        arrive(pair_stages[1])
+        launch(pair_stages[2])
+
     hop.wait()
     arrive(base_stages[3])
 
@@ -513,11 +517,6 @@
     count[0] += 4
     pl.when(give_low)(lambda: launch(give_base))
 
-    @pl.when(pair_low)
-    def _():
-        arrive(pair_stages[1])
-        launch(pair_stages[2])
-
     eacc[...] = jnp.zeros(eacc.shape, f32)
 
     def earlier_product(q, carry):
@@ -603,47 +602,44 @@
     def products(first, last):
         lax.fori_loop(first, last, earlier_product, 0)
 
-    not_first, not_second = jnp.logical_not(first_before), jnp.logical_not(second_before)
-    up_pair_before = all_of(pair_up, up_before)
-    up_pair_after = all_of(pair_up, up_after)
-
-    def up_launch(stage):
-        launch(up_stages[stage])
-
-    def up_middle():
+    def begin():
+        launch(up_stages[0])
+
+        @pl.when(pair_up)
+        def _():
+            shift_up.wait_recv()
+            launch(pair_stages[0])
+
+    def first_relay():
         relay(up_stages[0], up_stages[1])
+        pl.when(pair_up)(lambda: relay(pair_stages[0], pair_stages[1]))
+
+    def second_launch():
         arrive(up_stages[1])
         launch(up_stages[2])
 
-    def pair_begin():
-        shift_up.wait_recv()
-        launch(pair_stages[0])
-
-    def pair_middle():
-        relay(pair_stages[0], pair_stages[1])
-        arrive(pair_stages[1])
-        launch(pair_stages[2])
+        @pl.when(pair_up)
+        def _():
+            arrive(pair_stages[1])
+            launch(pair_stages[2])
+
+    def second_relay():
+        relay(up_stages[2], up_stages[3])
+        pl.when(pair_up)(lambda: relay(pair_stages[2], pair_stages[3]))
 
     def pair_end():
         arrive(pair_stages[3])
         sibling.start()
 
-    pl.when(up_before)(lambda: launch(up_stages[0]))
-    pl.when(up_pair_before)(pair_begin)
-    pl.when(first_before)(lambda: products(0, QUADS // 2))
     pl.when(pair_low)(lambda: relay(pair_stages[2], pair_stages[3]))
-    pl.when(up_before)(up_middle)
-    pl.when(up_pair_before)(pair_middle)
+    pl.when(up_before)(begin)
+    pl.when(before)(lambda: products(0, 2))
+    pl.when(up_before)(first_relay)
+    pl.when(before)(lambda: products(2, 4))
     pl.when(pair_low)(pair_end)
-
-    @pl.when(second_before)
-    def _():
-        products(QUADS // 2, QUADS)
-        earlier_results()
-
-    pl.when(up_before)(lambda: relay(up_stages[2], up_stages[3]))
-    pl.when(up_pair_before)(lambda: relay(pair_stages[2], pair_stages[3]))
-
+    pl.when(up_before)(second_launch)
+    pl.when(z >= 5)(lambda: products(4, 6))
+    pl.when(all_of(pair_up, before))(second_relay)
     pl.when(use_low)(lambda: arrive(low_stages[3]))
     pl.when(pair_low)(sibling.wait_recv)
 
@@ -683,36 +679,42 @@
         push_back()
         launch(bw_2)
 
-    pl.when(up_after)(lambda: launch(up_stages[0]))
-    pl.when(up_pair_after)(pair_begin)
-
-    @pl.when(jnp.logical_not(split_early))
-    def _():
-        for c in range(4):
-            relayout(c)
-
-    pl.when(not_first)(lambda: products(0, QUADS // 2))
-    pl.when(up_after)(up_middle)
-    pl.when(up_pair_after)(pair_middle)
-
-    @pl.when(not_second)
-    def _():
-        products(QUADS // 2, QUADS)
-        earlier_results()
-
-    pl.when(up_after)(lambda: relay(up_stages[2], up_stages[3]))
-    pl.when(up_pair_after)(lambda: relay(pair_stages[2], pair_stages[3]))
-    pl.when(cells_here)(lambda: launch(cell_stages[0]))
+    @pl.when(after)
+    def _():
+        begin()
+
+        @pl.when(jnp.logical_not(split_early))
+        def _():
+            relayout(0)
+            relayout(1)
+
+        pl.when(split_early)(lambda: products(0, 2))
+        first_relay()
+
+        @pl.when(jnp.logical_not(split_early))
+        def _():
+            relayout(2)
+            relayout(3)
+
+        pl.when(split_early)(lambda: products(2, 4))
+        second_launch()
+        pl.when(jnp.logical_not(split_early))(lambda: products(0, 4))
+
+    pl.when(all_of(up_before, even))(second_relay)
+    pl.when(z < 5)(lambda: products(4, 6))
+    pl.when(after)(second_relay)
+    products(6, 8)
     pl.when(pair_up)(pair_end)
-
-    pl.when(use_up)(lambda: arrive(up_stages[3]))
+    earlier_results()
 
     @pl.when(cells_here)
     def _():
+        launch(cell_stages[0])
         relay(cell_stages[0], cell_stages[1])
         arrive(cell_stages[1])
         launch(cell_stages[2])
 
+    pl.when(use_up)(lambda: arrive(up_stages[3]))
     pl.when(pair_up)(sibling.wait_recv)
     pl.when(cells_here)(lambda: relay(cell_stages[2], cell_stages[3]))
 

time: 114 us -> 117 us (1.026)
  Pallas kernels: 113 us -> 116 us
    pallas_call x1, Pallas kernels: 106 us -> 109 us  [body(): pl.pallas_call(functools.partial(kernel, na, nb, nz), out_shape=(jax.Shap...]
where the time goes in v9:
time: 117 us
  Pallas kernels  116 us (99%)
    pallas_call x1, Pallas kernels, body(): pl.pallas_call(functools.partial(kernel, na, nb, nz), out_shape=(jax.Shap...  109 us
    pallas_call x1, Pallas kernels, body(): pl.pallas_call(functools.partial(finish_kernel, math.sqrt(na * nb * nz *...  6.88 us

profile of v9, /device:TPU:1, one launch (start us, length us, event | category | flops | bytes accessed | tf_op | source)
XLA Modules:
  0.0 116.6 jit_solution(5081790374195910171)
XLA Ops:
  0.6 108.9 %step.1 = (f32[2048,128]{1,0:T(8,128)}, bf16[8,128,512]{2,1,0:T(8,128)(2,1)}, f32[64,512]{1,0:T(8,128)}, f32[8,8,128]{2,1,0:T(8,128)}) custom-call(f32[64,4,8,128]{3,2,1,0:T(8,128)} %x_h.1, f32[2048,128]{1,0:T(8,128)} %bitcast.12, f32[32,128]{1,0:T(8,128)} %bitcast.18, f32[96,128]{1,0:T(8,128)} %bitcast.16, f32[16384,128]{1,0:T(8,128)} %bitcast.11, ...), custom_call_target="tpu_custom_call" | custom-call | flops 2000000000 | bytes 13631488 | tf_op jit(solution)/shard_map/step/pallas_call | solution.py:988
  109.5 6.9 %finish.1 = (f32[2048,128]{1,0:T(8,128)}, f32[2048,128]{1,0:T(8,128)}, f32[64,512]{1,0:T(8,128)}, f32[64,64]{1,0:T(8,128)}) custom-call(f32[64,128]{1,0:T(8,128)} %bitcast.17, bf16[8,128,512]{2,1,0:T(8,128)(2,1)} %get-tuple-element.13.orth_h, f32[2048,128]{1,0:T(8,128)} %get-tuple-element.14.res_h, f32[64,512]{1,0:T(8,128)} %get-tuple-element.15.proj_h), custom_call_target="tpu_custom_call" | custom-call | flops 200000000 | bytes 5242880 | tf_op jit(solution)/shard_map/finish/pallas_call | solution.py:1010

commit v10 on v9

--- a/solution.py
+++ b/solution.py
@@ -340,13 +340,10 @@
     def all_of(*conditions):
         return functools.reduce(jnp.logical_and, conditions)
 
-    pair_low = all_of(even, z >= 4)
     pair_up = all_of(odd, z <= nz - 3)
-    give_low = all_of(odd, z >= 3, z <= nz - 3)
     give_up = all_of(even, z >= 2)
-    before, after = z >= 3, z < 3
-    up_before = all_of(use_up, before)
-    cells_here = jnp.logical_or(z == 0, z == 2)
+    up_before = all_of(use_up, z >= 5)
+    cells_here = z <= 2
     owners_add = jnp.logical_not(cells_here)
 
     def shift_copy(m, step):
@@ -354,12 +351,11 @@
         count[0] += 1
         return remote(n, gath.at[m, a, member], gath.at[4, a, member], (a, b, z + step))
 
-    shift_low, shift_up = shift_copy(0, 1), shift_copy(1, -1)
+    shift_up = shift_copy(1, -1)
     sibling = remote(count[0], gath.at[4], gath_sib, (a, member * 2 + 1 - core, z))
     count[0] += 1
     launch(base_stages[0])
     pl.when(use_low)(lambda: launch(low_stages[0]))
-    pl.when(give_low)(shift_low.start)
     pl.when(give_up)(shift_up.start)
 
     get_c.wait()
@@ -404,11 +400,6 @@
     arrive(halo)
     arrive(base_stages[1])
     launch(base_stages[2])
-
-    @pl.when(pair_low)
-    def _():
-        shift_low.wait_recv()
-        launch(pair_stages[0])
 
 
     @pl.when(use_low)
@@ -480,14 +471,7 @@
     relay(base_stages[2], base_stages[3])
     for c in (1, 2, 3):
         pl.when(split_early)(functools.partial(relayout, c))
-    pl.when(pair_low)(lambda: relay(pair_stages[0], pair_stages[1]))
     pl.when(use_low)(lambda: relay(low_stages[2], low_stages[3]))
-
-    @pl.when(pair_low)
-    def _():
-        arrive(pair_stages[1])
-        launch(pair_stages[2])
-
     hop.wait()
     arrive(base_stages[3])
 
@@ -512,10 +496,8 @@
             for d in range(2)
         ]
 
-    give_base = plane_copies(count[0], base, other.at[core], 1)
-    give_state = plane_copies(count[0] + 2, kept, other.at[core], -1)
-    count[0] += 4
-    pl.when(give_low)(lambda: launch(give_base))
+    give_state = plane_copies(count[0], kept, other.at[core], -1)
+    count[0] += 2
 
     eacc[...] = jnp.zeros(eacc.shape, f32)
 
@@ -562,12 +544,10 @@
                 cell_v[i] = eacc[i * vecs : (i + 1) * vecs, LANES:].T.astype(bf16)
 
     fw_1 = plane_copies(count[0], stateb.at[0], fw_in.at[core], 1)
-    fw_2 = plane_copies(count[0] + 2, stateb.at[0], fw_in.at[core], 2)
-    bw_1 = plane_copies(count[0] + 4, stateb.at[1], bw_in.at[core], -1)
-    bw_2 = plane_copies(count[0] + 6, stateb.at[1], bw_in.at[core], -2)
-    count[0] += 8
-    fw_near = all_of(z < nz - 1, jnp.logical_or(even, z == 1))
-    fw_far = all_of(even, z >= 2, z <= nz - 4)
+    bw_1 = plane_copies(count[0] + 2, stateb.at[1], bw_in.at[core], -1)
+    bw_2 = plane_copies(count[0] + 4, stateb.at[1], bw_in.at[core], -2)
+    count[0] += 6
+    fw_near = z < nz - 1
     bw_near, bw_far = odd, all_of(odd, z >= 3)
     row_group = iota((16, LANES), 0) // 4
 
@@ -631,39 +611,28 @@
         arrive(pair_stages[3])
         sibling.start()
 
-    pl.when(pair_low)(lambda: relay(pair_stages[2], pair_stages[3]))
     pl.when(up_before)(begin)
-    pl.when(before)(lambda: products(0, 2))
+    pl.when(z >= 3)(lambda: products(0, 2))
     pl.when(up_before)(first_relay)
-    pl.when(before)(lambda: products(2, 4))
-    pl.when(pair_low)(pair_end)
+    pl.when(z >= 3)(lambda: products(2, 4))
     pl.when(up_before)(second_launch)
     pl.when(z >= 5)(lambda: products(4, 6))
-    pl.when(all_of(pair_up, before))(second_relay)
+    pl.when(up_before)(second_relay)
     pl.when(use_low)(lambda: arrive(low_stages[3]))
-    pl.when(pair_low)(sibling.wait_recv)
 
     @pl.when(z == 0)
     def _():
         state[...] = base[...]
 
-    @pl.when(all_of(z > 0, jnp.logical_not(pair_low)))
+    @pl.when(z > 0)
     def _():
         arrive(fw_1)
         state[...] = base[...] - product_of(left_of([fw_in[0], fw_in[1]]), gath.at[0])
 
-    @pl.when(pair_low)
-    def _():
-        arrive(give_base)
-        arrive(fw_2)
-        state[...] = two_steps(left_of([fw_in[0], fw_in[1]]), base[...], 0)
-
     @pl.when(fw_near)
     def _():
         stateb[0] = pack(state[...]).astype(bf16)
         launch(fw_1)
-
-    pl.when(fw_far)(lambda: launch(fw_2))
 
     @pl.when(give_up)
     def _():
@@ -679,30 +648,30 @@
         push_back()
         launch(bw_2)
 
-    @pl.when(after)
+    @pl.when(z < 5)
     def _():
         begin()
 
-        @pl.when(jnp.logical_not(split_early))
+        @pl.when(z < 2)
         def _():
             relayout(0)
             relayout(1)
 
-        pl.when(split_early)(lambda: products(0, 2))
+        pl.when(z == 2)(lambda: products(0, 2))
+        pl.when(z >= 3)(lambda: products(4, 6))
         first_relay()
 
-        @pl.when(jnp.logical_not(split_early))
+        @pl.when(z < 2)
         def _():
             relayout(2)
             relayout(3)
 
-        pl.when(split_early)(lambda: products(2, 4))
+        pl.when(z == 2)(lambda: products(2, 4))
         second_launch()
-        pl.when(jnp.logical_not(split_early))(lambda: products(0, 4))
-
-    pl.when(all_of(up_before, even))(second_relay)
-    pl.when(z < 5)(lambda: products(4, 6))
-    pl.when(after)(second_relay)
+        pl.when(z < 2)(lambda: products(0, 4))
+        pl.when(z < 3)(lambda: products(4, 6))
+        second_relay()
+
     products(6, 8)
     pl.when(pair_up)(pair_end)
     earlier_results()
@@ -846,11 +815,9 @@
             for copy in stage:
                 copy.wait_send()
 
-    use_pair = jnp.logical_or(pair_low, pair_up)
     for condition, copies in (
-        (cells_here, sum(cell_stages, [])), (use_pair, sum(pair_stages, [])), (use_pair, [sibling]),
-        (give_low, [shift_low] + give_base), (give_up, [shift_up] + give_state),
-        (fw_near, fw_1), (fw_far, fw_2), (bw_near, bw_1), (bw_far, bw_2),
+        (cells_here, sum(cell_stages, [])), (pair_up, sum(pair_stages, [])), (pair_up, [sibling]),
+        (give_up, [shift_up] + give_state), (fw_near, fw_1), (bw_near, bw_1), (bw_far, bw_2),
     ):
         @pl.when(condition)
         def _(copies=copies):

time: 117 us -> 110 us (0.940)
  Pallas kernels: 116 us -> 109 us
    pallas_call x1, Pallas kernels: 109 us -> 102 us  [body(): pl.pallas_call(functools.partial(kernel, na, nb, nz), out_shape=(jax.Shap...]
where the time goes in v10:
time: 110 us; the launch traced here: 109 us
  Pallas kernels  109 us (99%)
    pallas_call x1, Pallas kernels, body(): pl.pallas_call(functools.partial(kernel, na, nb, nz), out_shape=(jax.Shap...  102 us
    pallas_call x1, Pallas kernels, body(): pl.pallas_call(functools.partial(finish_kernel, math.sqrt(na * nb * nz *...  6.87 us

profile of v10, /device:TPU:1, one launch (start us, length us, event | category | flops | bytes accessed | tf_op | source)
XLA Modules:
  0.0 109.4 jit_solution(14670193286792840718)
XLA Ops:
  0.6 101.8 %step.1 = (f32[2048,128]{1,0:T(8,128)}, bf16[8,128,512]{2,1,0:T(8,128)(2,1)}, f32[64,512]{1,0:T(8,128)}, f32[8,8,128]{2,1,0:T(8,128)}) custom-call(f32[64,4,8,128]{3,2,1,0:T(8,128)} %x_h.1, f32[2048,128]{1,0:T(8,128)} %bitcast.12, f32[32,128]{1,0:T(8,128)} %bitcast.18, f32[96,128]{1,0:T(8,128)} %bitcast.16, f32[16384,128]{1,0:T(8,128)} %bitcast.11, ...), custom_call_target="tpu_custom_call" | custom-call | flops 2000000000 | bytes 13631488 | tf_op jit(solution)/shard_map/step/pallas_call | solution.py:955
  102.4 6.9 %finish.1 = (f32[2048,128]{1,0:T(8,128)}, f32[2048,128]{1,0:T(8,128)}, f32[64,512]{1,0:T(8,128)}, f32[64,64]{1,0:T(8,128)}) custom-call(f32[64,128]{1,0:T(8,128)} %bitcast.17, bf16[8,128,512]{2,1,0:T(8,128)(2,1)} %get-tuple-element.13.orth_h, f32[2048,128]{1,0:T(8,128)} %get-tuple-element.14.res_h, f32[64,512]{1,0:T(8,128)} %get-tuple-element.15.proj_h), custom_call_target="tpu_custom_call" | custom-call | flops 200000000 | bytes 5242880 | tf_op jit(solution)/shard_map/finish/pallas_call | solution.py:977

commit v11 on v10

--- a/solution.py
+++ b/solution.py
@@ -271,8 +271,7 @@
             at = slice(t * LANES, (t + 1) * LANES)
             gath[(3, 0, 1)[i], a, member, :, at] = out.astype(bf16)
 
-    for i in range(3):
-        reorder(i)
+    reorder(0)
 
     axes = ("member", "gx")
 
@@ -355,6 +354,8 @@
     sibling = remote(count[0], gath.at[4], gath_sib, (a, member * 2 + 1 - core, z))
     count[0] += 1
     launch(base_stages[0])
+    reorder(1)
+    reorder(2)
     pl.when(use_low)(lambda: launch(low_stages[0]))
     pl.when(give_up)(shift_up.start)
 
@@ -614,9 +615,9 @@
     pl.when(up_before)(begin)
     pl.when(z >= 3)(lambda: products(0, 2))
     pl.when(up_before)(first_relay)
-    pl.when(z >= 3)(lambda: products(2, 4))
+    pl.when(z >= 4)(lambda: products(2, 4))
     pl.when(up_before)(second_launch)
-    pl.when(z >= 5)(lambda: products(4, 6))
+    pl.when(z >= 6)(lambda: products(4, 6))
     pl.when(up_before)(second_relay)
     pl.when(use_low)(lambda: arrive(low_stages[3]))
 
@@ -647,6 +648,11 @@
     def _():
         push_back()
         launch(bw_2)
+
+    @pl.when(z == 5)
+    def _():
+        pair_end()
+        products(4, 6)
 
     @pl.when(z < 5)
     def _():
@@ -658,7 +664,8 @@
             relayout(1)
 
         pl.when(z == 2)(lambda: products(0, 2))
-        pl.when(z >= 3)(lambda: products(4, 6))
+        pl.when(z == 3)(lambda: products(2, 4))
+        pl.when(z == 4)(lambda: products(4, 6))
         first_relay()
 
         @pl.when(z < 2)
@@ -667,13 +674,14 @@
             relayout(3)
 
         pl.when(z == 2)(lambda: products(2, 4))
+        pl.when(z == 3)(lambda: products(4, 6))
         second_launch()
         pl.when(z < 2)(lambda: products(0, 4))
         pl.when(z < 3)(lambda: products(4, 6))
         second_relay()
 
     products(6, 8)
-    pl.when(pair_up)(pair_end)
+    pl.when(all_of(pair_up, z < 5))(pair_end)
     earlier_results()
 
     @pl.when(cells_here)

time: 110 us -> 110 us (level)
  no operation moved by 1% of the time
where the time goes in v11:
time: 110 us; the launch traced here: 109 us
  Pallas kernels  109 us (99%)
    pallas_call x1, Pallas kernels, body(): pl.pallas_call(functools.partial(kernel, na, nb, nz), out_shape=(jax.Shap...  102 us
    pallas_call x1, Pallas kernels, body(): pl.pallas_call(functools.partial(finish_kernel, math.sqrt(na * nb * nz *...  6.87 us

profile of v11, /device:TPU:1, one launch (start us, length us, event | category | flops | bytes accessed | tf_op | source)
XLA Modules:
  0.0 109.4 jit_solution(5385164872511939173)
XLA Ops:
  0.6 101.8 %step.1 = (f32[2048,128]{1,0:T(8,128)}, bf16[8,128,512]{2,1,0:T(8,128)(2,1)}, f32[64,512]{1,0:T(8,128)}, f32[8,8,128]{2,1,0:T(8,128)}) custom-call(f32[64,4,8,128]{3,2,1,0:T(8,128)} %x_h.1, f32[2048,128]{1,0:T(8,128)} %bitcast.12, f32[32,128]{1,0:T(8,128)} %bitcast.18, f32[96,128]{1,0:T(8,128)} %bitcast.16, f32[16384,128]{1,0:T(8,128)} %bitcast.11, ...), custom_call_target="tpu_custom_call" | custom-call | flops 2000000000 | bytes 13631488 | tf_op jit(solution)/shard_map/step/pallas_call | solution.py:963
  102.4 6.9 %finish.1 = (f32[2048,128]{1,0:T(8,128)}, f32[2048,128]{1,0:T(8,128)}, f32[64,512]{1,0:T(8,128)}, f32[64,64]{1,0:T(8,128)}) custom-call(f32[64,128]{1,0:T(8,128)} %bitcast.17, bf16[8,128,512]{2,1,0:T(8,128)(2,1)} %get-tuple-element.13.orth_h, f32[2048,128]{1,0:T(8,128)} %get-tuple-element.14.res_h, f32[64,512]{1,0:T(8,128)} %get-tuple-element.15.proj_h), custom_call_target="tpu_custom_call" | custom-call | flops 200000000 | bytes 5242880 | tf_op jit(solution)/shard_map/finish/pallas_call | solution.py:985
